TPU v7x, 256 devices: a whole 4x4x8 slice. The times are simulated.
256 devices in a mesh: tile: 64 (over z, y, core), freq: 4 (over x).
Axes of the slice: x: 4, y: 4, z: 8, core: 2. Of those that a mesh axis runs over, the one named last changes fastest.
Arguments:
- displacement: float32 [2, 3, 512, 48, 256], P(None, None, ('freq', 'tile')), parts along dimension 2, may hold values from -6 to 6
- cell_scale: float32 [128, 48, 256], P('tile'), may hold values from 0.5 to 2
- material_id: int32 [128, 48, 256], P('tile'), may hold values from 0 to 15
- stiff_table: float32 [2, 64], P(None, 'freq'), parts along dimension 1, may hold values from 0.2 to 1.5
- mass_table: float32 [2, 64], P(None, 'freq'), parts along dimension 1, may hold values from -1 to 0.5
- pile_block: bfloat16 [256, 2, 1152, 1152], P(('freq', 'tile')), parts along dimension 0, may hold values from -0.125 to 0.125
- pile_owner: int32 [256], P('freq'), parts along dimension 0, may hold values from 0 to 63, each once
- node_index: int32 [64, 3, 128], replicated, may hold values from 0 to 1572863, as said below
Outputs:
- result: float32 [2, 3, 512, 48, 256], P(None, None, ('freq', 'tile')), parts along dimension 2
There are 4 independent parts, one for each index of `freq`. A program takes and returns all parts, laid end to end along the dimension named above; an argument that names none is the same for every part. Nothing has to cross between parts.
Inputs may be any that keep to these rules, and one draw needn't show every extreme that they name: `node_index`: each pile stands at one position along the farm: its blocks of 128 nodes lie in the cells of one tile of 2 planes, its lower blocks on some piles in the next tile; no cell appears twice; a tile holds at most 8 blocks, and some tile exactly 8.
All inputs are finite; a program needn't handle non-finite values.
Results may differ from a plain program's by a relative error of at most 0.0003.
Values may be sent and summed in bfloat16 or wider, within the bound.
No kernel may reach another device: no remote copies, remote signals or barrier semaphores. Data moves between devices by JAX's collectives and lax.ppermute only.
A program may use at most 64 MiB of HBM per device.

v0:
```python
import jax
import jax.numpy as jnp
from jax import lax
from jax.sharding import PartitionSpec as P

MOST = 8


def with_halo(array, sides, width):
    for axis, dim in sides:
        size, length = (lax.axis_size(axis), array.shape[dim])
        up = [(i, (i + 1) % size) for i in range(size - 1)]
        down = [(j, i) for i, j in up]
        last = lax.slice_in_dim(array, length - width, length, axis=dim)
        first = lax.slice_in_dim(array, 0, width, axis=dim)
        before = lax.ppermute(last, axis, up)
        after = lax.ppermute(first, axis, down)
        array = jnp.concatenate([before, array, after], axis=dim)
    return array


def soil_apply(padded, inertia):
    centre = padded[:, 1:-1, 1:-1, 1:-1]
    extent = centre.shape[1:]
    displace = centre[:6].reshape((2, 3) + extent)
    stiffness = centre[6:]
    total_real = inertia[0] * displace[0] - inertia[1] * displace[1]
    total_imag = inertia[0] * displace[1] + inertia[1] * displace[0]
    for direction in range(3):
        for offset in (0, 2):
            window = [slice(None), slice(1, -1), slice(1, -1), slice(1, -1)]
            window[direction + 1] = slice(offset, offset + extent[direction])
            beside = padded[tuple(window)]
            face_real = 0.5 * (stiffness[0] + beside[6])
            face_imag = 0.5 * (stiffness[1] + beside[7])
            strain = displace - beside[:6].reshape(displace.shape)
            total_real = total_real + face_real * strain[0] - face_imag * strain[1]
            total_imag = total_imag + face_real * strain[1] + face_imag * strain[0]
    return jnp.stack([total_real, total_imag])


def table_lookup(table, material_id):
    kinds = table.shape[1]
    looked = jnp.zeros((2,) + material_id.shape, jnp.float32)
    for kind in range(kinds):
        chosen = (material_id == kind)[None]
        looked = jnp.where(chosen, table[:, kind].reshape((2,) + (1,) * material_id.ndim), looked)
    return looked


def slot_labels(flat_blocks, cell_total, tile_count):
    block_total = flat_blocks.shape[0]
    block_tile = flat_blocks[:, 0] // cell_total
    device_range = jnp.arange(tile_count, dtype=jnp.int32)
    onto = block_tile[None, :] == device_range[:, None]
    slot_rank = jnp.cumsum(onto.astype(jnp.int32), axis=1) - 1
    slot_range = jnp.arange(MOST, dtype=jnp.int32)
    slot_match = onto[:, None, :] & (slot_rank[:, None, :] == slot_range[None, :, None])
    block_range = jnp.arange(block_total, dtype=jnp.int32)
    labels = jnp.sum(jnp.where(slot_match, block_range[None, None, :], 0), axis=2)
    labels = jnp.where(jnp.any(slot_match, axis=2), labels, -1)
    return labels.reshape(-1)


def per_device(
    displacement,
    cell_scale,
    material_id,
    stiff_table,
    mass_table,
    pile_block,
    pile_owner,
    node_index,
):
    extent = cell_scale.shape
    cell_total = cell_scale.size
    tile_count = lax.axis_size("tile")
    tile_index = lax.axis_index("tile")
    stiffness = table_lookup(stiff_table, material_id) * cell_scale
    inertia = table_lookup(mass_table, material_id)
    stacked = jnp.concatenate([displacement.reshape((6,) + extent), stiffness], axis=0)
    extended = with_halo(stacked, (("tile", 1),), 1)
    padded = jnp.pad(extended, ((0, 0), (0, 0), (1, 1), (1, 1)))
    soil_term = soil_apply(padded, inertia)
    pile_count, block_count, row_count = node_index.shape
    flat_blocks = node_index.reshape(pile_count * block_count, row_count)
    all_labels = slot_labels(flat_blocks, cell_total, tile_count)
    slot_id = lax.dynamic_slice_in_dim(all_labels, tile_index * MOST, MOST)
    filled = slot_id >= 0
    safe_id = jnp.maximum(slot_id, 0)
    slot_nodes = jnp.clip(flat_blocks[safe_id] - tile_index * cell_total, 0, cell_total - 1)
    local_field = displacement.reshape(6, cell_total)
    picked = jnp.take(local_field, slot_nodes.reshape(-1), axis=1).reshape(6, MOST, row_count)
    outgoing = jnp.where(filled[None, :, None], picked, 0.0).transpose(1, 0, 2).astype(jnp.bfloat16)
    device_range = jnp.arange(tile_count, dtype=jnp.int32)
    pile_range = jnp.arange(pile_count, dtype=jnp.int32)
    block_range = jnp.arange(block_count, dtype=jnp.int32)
    pile_of_device = jnp.sum(
        jnp.where(pile_owner[None, :] == device_range[:, None], pile_range[None, :], 0), axis=1
    )
    my_pile = lax.dynamic_index_in_dim(pile_of_device, tile_index, 0, keepdims=False)
    my_ids = my_pile * block_count + block_range
    returned_labels = (pile_of_device[:, None] * block_count + block_range[None, :]).reshape(-1)
    labels = all_labels
    matched = (labels[:, None] == my_ids[None, :]).astype(jnp.bfloat16)
    incoming = jnp.einsum(
        "kb,kcr->bcr",
        matched,
        lax.all_gather(outgoing, "tile", axis=0, tiled=True),
        preferred_element_type=jnp.float32,
    )
    interface = (
        incoming.reshape(block_count, 2, 3, row_count)
        .transpose(1, 2, 0, 3)
        .reshape(2, -1)
        .astype(jnp.bfloat16)
    )
    pile_matrix = pile_block[0]
    real_part = jnp.dot(pile_matrix[0], interface[0], preferred_element_type=jnp.float32) - jnp.dot(
        pile_matrix[1], interface[1], preferred_element_type=jnp.float32
    )
    imag_part = jnp.dot(pile_matrix[0], interface[1], preferred_element_type=jnp.float32) + jnp.dot(
        pile_matrix[1], interface[0], preferred_element_type=jnp.float32
    )
    traction = jnp.stack([real_part, imag_part]).astype(jnp.bfloat16)
    returning = (
        traction.reshape(2, 3, block_count, row_count)
        .transpose(2, 0, 1, 3)
        .reshape(block_count, 6, row_count)
    )
    labels = returned_labels
    matched = (slot_id[:, None] == labels[None, :]).astype(jnp.bfloat16)
    arriving = jnp.einsum(
        "sk,kcr->scr",
        matched,
        lax.all_gather(returning, "tile", axis=0, tiled=True),
        preferred_element_type=jnp.float32,
    )
    spread = arriving.transpose(1, 0, 2).reshape(6, -1)
    result = soil_term.reshape(6, -1).at[:, slot_nodes.reshape(-1)].add(spread)
    return result.reshape((2, 3) + extent)


def solution(mesh):
    placed = (
        P(None, None, ("freq", "tile"), None, None),
        P("tile", None, None),
        P("tile", None, None),
        P(None, "freq"),
        P(None, "freq"),
        P(("freq", "tile"), None, None, None),
        P("freq"),
        P(),
    )
    return jax.shard_map(
        per_device,
        mesh=mesh,
        in_specs=placed,
        out_specs=P(None, None, ("freq", "tile"), None, None),
        check_vma=False,
    )
```

profile of v0, /device:TPU:1, one launch (start us, length us, event | category | flops | bytes accessed | tf_op | source)
XLA Modules:
  0.0 182.9 jit_solution(12308777013180802330)
XLA Ops:
  0.0 1.7 slice_reduce_fusion.16
  1.7 1.1 broadcast_compare_fusion.15
  2.8 1.3 select_multiply_fusion
  4.1 1.1 fusion.29
  5.2 4.6 %collective-permute-start = (f32[8,1,48,256]{3,2,1,0:T(8,128)S(1)}, f32[8,1,48,256]{3,2,1,0:T(8,128)S(1)}, u32[]{:S(2)}, u32[]{:S(2)}) collective-permute-start(f32[8,1,48,256]{3,2,1,0:T(8,128)S(1)} %get-tuple-element.61), channel_id=1, source_target_pairs={{0,4},{4,8},{8,12},{12,16},{16,20},{20,24},{24,28},{28,32},{32,36}... | collective-permute-start | bytes 1179656 | tf_op jit(solution)/shard_map/ppermute | solution.py:16
  9.8 1.9 %collective-permute-start.1 = (f32[8,1,48,256]{3,2,1,0:T(8,128)S(1)}, f32[8,1,48,256]{3,2,1,0:T(8,128)S(1)}, u32[]{:S(2)}, u32[]{:S(2)}) collective-permute-start(f32[8,1,48,256]{3,2,1,0:T(8,128)S(1)} %get-tuple-element.62), channel_id=1, source_target_pairs={{4,0},{8,4},{12,8},{16,12},{20,16},{24,20},{28,24},{32,28},{36,32}... | collective-permute-start | bytes 1179656 | tf_op jit(solution)/shard_map/ppermute | solution.py:17
  12.1 0.6 reduce-window.6
  13.0 1.2 fusion.28
  14.2 1.2 select_reduce_fusion
  15.4 0.3 reshape.266
  15.9 0.6 dynamic_slice.8
  17.3 0.6 gather_fusion
  17.9 5.0 %copy.56 = bf16[6,24576]{0,1:T(8,128)(2,1)} copy(bf16[6,24576]{1,0:T(8,128)(2,1)S(1)} %reshape.266) | data formatting | bytes 589824 | tf_op jit(solution)/shard_map/reshape | solution.py:92
  22.9 6.5 %gather_fusion.1 = bf16[1024,6]{1,0:T(8,128)(2,1)S(1)} fusion(bf16[6,24576]{0,1:T(8,128)(2,1)} %copy.56, s32[1024]{0:T(1024)S(1)} %broadcast_clamp_fusion), kind=kCustom, calls=%fused_computation.1 | custom fusion | bytes 28672 | tf_op jit(solution)/shard_map/jit(_take)/gather | solution.py:93
  29.6 55.9 %all_gather.6 = bf16[512,6,128]{2,0,1:T(8,128)(2,1)S(1)} all-gather(bf16[8,6,128]{2,0,1:T(8,128)(2,1)S(1)} %fusion.55), channel_id=1, replica_groups=mesh['tile'=64,'freq'=4] {'tile'}, dimensions={0}, use_global_device_ids=true | all-gather | bytes 798720 | tf_op jit(solution)/shard_map/all_gather | solution.py:109
  85.8 2.6 %fusion.18 = f32[1152]{0:T(1024)S(1)} fusion(bf16[1152,1]{0,1:T(2,128)(2,1)S(1)} %reshape.299, bf16[1,2,1152,1152]{3,2,1,0:T(8,128)(2,1)} %param.13), kind=kOutput, calls=%fused_computation.30 | convolution fusion | flops 2654208 | bytes 2661120 | tf_op jit(solution)/shard_map/dot_general | solution.py:122
  88.3 2.6 %fusion.21 = f32[1152]{0:T(1024)S(1)} fusion(bf16[1152,1]{0,1:T(2,128)(2,1)S(1)} %reshape.299, bf16[1,2,1152,1152]{3,2,1,0:T(8,128)(2,1)} %param.13), kind=kOutput, calls=%fused_computation.31 | convolution fusion | flops 2654208 | bytes 2661120 | tf_op jit(solution)/shard_map/dot_general | solution.py:119
  90.9 2.6 %fusion.24 = f32[1152]{0:T(1024)S(1)} fusion(bf16[1152,1]{0,1:T(2,128)(2,1)S(1)} %reshape.297, bf16[1,2,1152,1152]{3,2,1,0:T(8,128)(2,1)} %param.13), kind=kOutput, calls=%fused_computation.32 | convolution fusion | flops 2654208 | bytes 2661120 | tf_op jit(solution)/shard_map/dot_general | solution.py:122
  93.5 2.6 %fusion.15 = f32[1152]{0:T(1024)S(1)} fusion(bf16[1152,1]{0,1:T(2,128)(2,1)S(1)} %reshape.297, bf16[1,2,1152,1152]{3,2,1,0:T(8,128)(2,1)} %param.13), kind=kOutput, calls=%fused_computation.29 | convolution fusion | flops 2654208 | bytes 2661120 | tf_op jit(solution)/shard_map/dot_general | solution.py:119
  96.1 0.5 slice_reduce_fusion.32
  96.9 48.1 %all_gather.7 = bf16[192,6,128]{2,1,0:T(8,128)(2,1)S(1)} all-gather(bf16[3,6,128]{2,1,0:T(8,128)(2,1)S(1)} %copy.58), channel_id=1, replica_groups=mesh['tile'=64,'freq'=4] {'tile'}, dimensions={0}, use_global_device_ids=true | all-gather | bytes 299520 | tf_op jit(solution)/shard_map/all_gather | solution.py:136
  145.4 0.3 select_select_fusion
  145.7 1.8 select_maximum_fusion
  147.8 0.6 fusion.64
  148.3 0.3 maximum_maximum_fusion
  148.7 0.5 fusion.65
  149.2 0.6 multiply_subtract_fusion
  149.8 0.6 multiply_add_fusion
  150.6 7.3 %copy.61 = f32[6,24576]{0,1:T(8,128)} copy(f32[6,24576]{1,0:T(8,128)S(1)} %reshape.262) | data formatting | bytes 1179648 | tf_op jit(solution)/shard_map/reshape | solution.py:140
  157.9 15.9 %scatter_fusion = f32[6,24576]{0,1:T(8,128)} fusion(f32[6,24576]{0,1:T(8,128)} %copy.61, s32[1024]{0:T(1024)S(1)} %bitcast.117, f32[1024,6]{1,0:T(8,128)S(1)} %bitcast.113), kind=kCustom, calls=%fused_computation.2 | custom fusion | flops 6144 | bytes 77824 | tf_op jit(solution)/shard_map/scatter-add | solution.py:140
  173.8 8.0 %copy.62 = f32[6,24576]{1,0:T(8,128)S(1)} copy(f32[6,24576]{0,1:T(8,128)} %scatter_fusion) | data formatting | bytes 1179648 | tf_op jit(solution)/shard_map/scatter-add | solution.py:140
  181.9 1.0 copy.68
  (57 shorter events, 2.8 us)
Async XLA Ops:
  0.0 15.4 %copy-start = (f32[2,3,2,48,256]{4,3,2,1,0:T(8,128)S(1)}, f32[2,3,2,48,256]{4,3,2,1,0:T(8,128)}, u32[]{:S(2)}) copy-start(f32[2,3,2,48,256]{4,3,2,1,0:T(8,128)} %param.8) | copy-start | bytes 1769476
  0.0 11.8 %copy-start.2 = (s32[64,3,128]{2,0,1:T(8,128)S(1)}, s32[64,3,128]{2,0,1:T(8,128)}, u32[]{:S(2)}) copy-start(s32[64,3,128]{2,0,1:T(8,128)} %param.15) | copy-start | bytes 294916
  0.0 15.7 %copy-start.3 = (s32[64]{0:T(128)S(1)}, s32[64]{0:T(128)}, u32[]{:S(2)}) copy-start(s32[64]{0:T(128)} %param.14) | copy-start | bytes 772
  5.2 140.5 %collective-permute-start = (f32[8,1,48,256]{3,2,1,0:T(8,128)S(1)}, f32[8,1,48,256]{3,2,1,0:T(8,128)S(1)}, u32[]{:S(2)}, u32[]{:S(2)}) collective-permute-start(f32[8,1,48,256]{3,2,1,0:T(8,128)S(1)} %get-tuple-element.61), channel_id=1, source_target_pairs={{0,4},{4,8},{8,12},{12,16},{16,20},{20,24},{24,28},{28,32},{32,36}... | collective-permute-start | bytes 1179656 | tf_op jit(solution)/shard_map/ppermute | solution.py:16
  9.8 135.9 %collective-permute-start.1 = (f32[8,1,48,256]{3,2,1,0:T(8,128)S(1)}, f32[8,1,48,256]{3,2,1,0:T(8,128)S(1)}, u32[]{:S(2)}, u32[]{:S(2)}) collective-permute-start(f32[8,1,48,256]{3,2,1,0:T(8,128)S(1)} %get-tuple-element.62), channel_id=1, source_target_pairs={{4,0},{8,4},{12,8},{16,12},{20,16},{24,20},{28,24},{32,28},{36,32}... | collective-permute-start | bytes 1179656 | tf_op jit(solution)/shard_map/ppermute | solution.py:17
  90.9 5.2 %copy-start.1 = (f32[2,16]{1,0:T(2,128)S(1)}, f32[2,16]{1,0:T(2,128)}, u32[]{:S(2)}) copy-start(f32[2,16]{1,0:T(2,128)} %param.12) | copy-start | bytes 388
where the time goes:
time: 184 us; the launch traced here: 183 us
  blocking collectives  104 us (57%)
  local copies, waits for them, and re-layouts  33.4 us (18%)
  other arithmetic  27.3 us (15%)
  matrix products  10.7 us (6%)
  starting transfers between devices  6.52 us (4%)
    all_gather x1, blocking collectives, per_device(): lax.all_gather(outgoing, 'tile', axis=0, tiled=True)  55.9 us
    all_gather x1, blocking collectives, per_device(): lax.all_gather(returning, 'tile', axis=0, tiled=True)  48.1 us
    scatter-add x1, other arithmetic, per_device(): result = soil_term.reshape(6, -1).at[:, slot_nodes.reshape(-1)].add(spread)  15.9 us
    scatter-add x1, local copies, waits for them, and re-layouts, per_device(): result = soil_term.reshape(6, -1).at[:, slot_nodes.reshape(-1)].add(spread)  8.02 us
    reshape x2, local copies, waits for them, and re-layouts, per_device(): result = soil_term.reshape(6, -1).at[:, slot_nodes.reshape(-1)].add(spread)  7.5 us
    gather x2, local copies, waits for them, and re-layouts, per_device(): jnp.take(local_field, slot_nodes.reshape(-1), axis=1)  6.61 us
    reshape x2, local copies, waits for them, and re-layouts, per_device(): local_field = displacement.reshape(6, cell_total)  5.32 us
    ppermute x1, starting transfers between devices, with_halo(): before = lax.ppermute(last, axis, up)  4.59 us
  transfers between devices with their start and end apart: 2, of which 0 were waited for; matrix products, arithmetic and copies ran while one was open for 16% of the time, Pallas kernels for 0%

commit v1 on v0

v1 whole, which is shorter than its diff:
```python
import functools

import jax
import jax.numpy as jnp
from jax import lax
from jax.experimental import pallas as pl
from jax.experimental.pallas import tpu as pltpu
from jax.sharding import PartitionSpec as P

MOST = 8
F32 = jnp.float32
BF16 = jnp.bfloat16
I32 = jnp.int32
NT = (((1,), (1,)), ((), ()))


def iota(shape, axis):
    return lax.broadcasted_iota(I32, shape, axis)


def onehot(mask):
    return jnp.where(mask, 1.0, 0.0).astype(BF16)


def dot(left, right):
    return jnp.dot(left, right, preferred_element_type=F32)


def dot_nt(left, right):
    return lax.dot_general(left, right, NT, preferred_element_type=F32)


def slots_of(nodes, me, cells, columns):
    blocks, width = nodes.shape
    local = nodes - me * cells
    inside = (local >= 0) & (local < cells)
    shift = columns.bit_length() - 1
    row1 = jnp.where(inside, (local >> shift) + 1, 0).astype(F32).astype(BF16)
    column = jnp.where(inside, local & (columns - 1), 0).astype(F32).astype(BF16)
    first = onehot(iota((MOST, width), 1) == 0)
    onto = dot_nt(first, onehot(inside))
    upper = onehot(iota((blocks, blocks), 0) < iota((blocks, blocks), 1))
    rank = dot(onto.astype(BF16), upper)
    slot = onehot((onto > 0.5) & (rank == iota((MOST, blocks), 0).astype(F32)))
    slot_row = dot(slot, row1).astype(I32) - 1
    slot_column = dot(slot, column).astype(I32)
    return slot, slot_row, slot_column


def target_row(owner_ref, tiles):
    owner = owner_ref[...]
    return jnp.concatenate([owner + (b * tiles + 1) for b in range(3)], axis=1)


def gather_kernel(tiles, displacement_ref, nodes_ref, owner_ref, payload_ref, row_ref, column_ref, info_ref, picked):
    me = lax.axis_index("tile")
    components, rows, columns = displacement_ref.shape
    blocks, width = nodes_ref.shape
    block_count = blocks // tiles
    nodes = nodes_ref[...]
    cells = rows * columns
    slot, slot_row, slot_column = slots_of(nodes, me, cells, columns)
    row_ref[...] = slot_row
    column_ref[...] = slot_column
    target = jnp.broadcast_to(target_row(owner_ref, tiles), (MOST, blocks))
    slot_target = dot_nt(target.astype(F32).astype(BF16), slot).astype(I32) - 1
    place = onehot(iota((blocks, MOST), 0) == slot_target[0:1, :])
    field = displacement_ref[...].reshape(components * rows, columns).astype(BF16)
    for s in range(MOST):
        at_column = onehot(iota((columns, width), 0) == slot_column[s : s + 1, :])
        taken = dot(field, at_column)
        at_row = iota((rows, width), 0) == slot_row[s : s + 1, :]
        for c in range(components):
            one = jnp.where(at_row, taken[c * rows : (c + 1) * rows], 0.0)
            picked[s : s + 1, c * width : (c + 1) * width] = jnp.sum(one, axis=0, keepdims=True)
    sent = dot(place, picked[...].astype(BF16)).astype(BF16)
    for b in range(block_count):
        for c in range(components):
            start = (c * block_count + b) * width
            payload_ref[:, start : start + width] = sent[b * tiles : (b + 1) * tiles, c * width : (c + 1) * width]
    owner = owner_ref[...]
    mine = jnp.where(owner == me, 1.0, 0.0)
    first = onehot(iota((MOST, width), 1) == 0)
    tile_of = jnp.floor(((nodes >> 13).astype(F32) + 0.5) * (1.0 / (cells >> 13)))
    tile_row = dot_nt(first, tile_of.astype(BF16))[0:1, :]
    for b in range(block_count):
        info_ref[b : b + 1, :] = jnp.broadcast_to(
            jnp.sum(tile_row[:, b * tiles : (b + 1) * tiles] * mine, axis=1, keepdims=True).astype(I32),
            (1, info_ref.shape[1]),
        )
    target_column = jnp.sum(
        jnp.where(iota((MOST, MOST), 0) == iota((MOST, MOST), 1), slot_target, 0), axis=1, keepdims=True
    )
    info_ref[MOST : 2 * MOST, :] = jnp.broadcast_to(target_column, (MOST, info_ref.shape[1]))


def pile_kernel(arrived_ref, block_ref, info_ref, payload_ref):
    tiles = payload_ref.shape[0]
    order = block_ref.shape[1]
    width = info_ref.shape[1]
    vector = jnp.sum(arrived_ref[...].astype(F32), axis=0).astype(BF16)
    by_real = dot_nt(vector, block_ref[0])
    by_imag = dot_nt(vector, block_ref[1])
    real = by_real[0:1] - by_imag[1:2]
    imag = by_real[1:2] + by_imag[0:1]
    device = iota((tiles, width), 0)
    for i, part in enumerate((real, imag)):
        for k in range(order // width):
            b = k % 3
            piece = jnp.where(device == info_ref[b : b + 1, :], part[:, k * width : (k + 1) * width], 0.0)
            start = i * order + k * width
            payload_ref[:, start : start + width] = piece.astype(BF16)


def scatter_kernel(tiles, soil_ref, arrived_ref, row_ref, column_ref, info_ref, result_ref, spread):
    components, rows, columns = soil_ref.shape
    width = row_ref.shape[1]
    for s in range(MOST):
        target = info_ref[MOST + s, 0]
        target = jnp.maximum(target, 0)
        b = target // tiles
        source = target - b * tiles
        at_row = iota((rows, width), 0) == row_ref[s : s + 1, :]
        for c in range(components // 2):
            piece = arrived_ref[source, :, pl.ds(pl.multiple_of((c * 3 + b) * width, width), width)].astype(F32)
            for i in range(2):
                k = i * (components // 2) + c
                spread[k * rows : (k + 1) * rows, s * width : (s + 1) * width] = jnp.where(
                    at_row, piece[i : i + 1, :], 0.0
                ).astype(BF16)
    at_column = jnp.concatenate(
        [onehot(iota((columns, width), 0) == column_ref[s : s + 1, :]) for s in range(MOST)], axis=1
    )
    added = dot_nt(spread[...], at_column)
    result_ref[...] = soil_ref[...] + added.reshape(components, rows, columns)


def lookup(table_ref, row, kind):
    bits = [(kind & (1 << k)) != 0 for k in range(4)]
    level = [table_ref[row, k] for k in range(16)]
    for bit in bits:
        level = [jnp.where(bit, level[2 * k + 1], level[2 * k]) for k in range(len(level) // 2)]
    return level[0]


def soil_kernel(displacement_ref, scale_ref, kind_ref, before_ref, after_ref, stiff_ref, mass_ref, soil_ref):
    _, planes, ny, nz = displacement_ref.shape
    shape = (ny, nz)
    at_y, at_z = iota(shape, 0), iota(shape, 1)
    y_last, z_last = at_y == ny - 1, at_z == nz - 1
    edges = (
        jnp.where(at_y == 0, 0.5, 0.0)
        + jnp.where(y_last, 0.5, 0.0)
        + jnp.where(at_z == 0, 0.5, 0.0)
        + jnp.where(z_last, 0.5, 0.0)
    )

    def half_stiffness(kind, scale):
        return [0.5 * (lookup(stiff_ref, i, kind) * scale) for i in range(2)]

    def field(x):
        if x < 0:
            return [before_ref[k] for k in range(6)]
        if x >= planes:
            return [after_ref[k] for k in range(6)]
        return [displacement_ref[k, x] for k in range(6)]

    half = [half_stiffness(before_ref[7].astype(I32), before_ref[6])]
    half += [half_stiffness(kind_ref[x], scale_ref[x]) for x in range(planes)]
    half += [half_stiffness(after_ref[7].astype(I32), after_ref[6])]

    def flux(face, near, far):
        strain = [near[k] - far[k] for k in range(6)]
        real = [face[0] * strain[c] - face[1] * strain[3 + c] for c in range(3)]
        imag = [face[0] * strain[3 + c] + face[1] * strain[c] for c in range(3)]
        return real + imag

    def x_flux(x):
        face = [half[x + 1][i] + half[x + 2][i] for i in range(2)]
        return flux(face, field(x), field(x + 1))

    flux_before = x_flux(-1)
    for x in range(planes):
        u = field(x)
        own = half[x + 1]
        diagonal = [lookup(mass_ref, i, kind_ref[x]) + 2.0 * edges * own[i] for i in range(2)]
        total = [diagonal[0] * u[c] - diagonal[1] * u[3 + c] for c in range(3)]
        total += [diagonal[0] * u[3 + c] + diagonal[1] * u[c] for c in range(3)]
        flux_after = x_flux(x)
        total = [total[k] + flux_after[k] - flux_before[k] for k in range(6)]
        flux_before = flux_after
        for axis, last in ((0, y_last), (1, z_last)):
            size = shape[axis]
            face = [jnp.where(last, 0.0, own[i] + pltpu.roll(own[i], size - 1, axis)) for i in range(2)]
            beside = [pltpu.roll(u[k], size - 1, axis) for k in range(6)]
            along = flux(face, u, beside)
            total = [total[k] + along[k] - pltpu.roll(along[k], 1, axis) for k in range(6)]
        for k in range(6):
            soil_ref[k, x] = total[k]


def halos(displacement, cell_scale, kind):
    size = lax.axis_size("tile")
    up = [(i, i + 1) for i in range(size - 1)]
    down = [(j, i) for i, j in up]

    def plane(x):
        return jnp.concatenate([displacement[:, x], cell_scale[x][None], kind[x][None].astype(F32)], axis=0)

    before = lax.ppermute(plane(displacement.shape[1] - 1), "tile", up)
    after = lax.ppermute(plane(0), "tile", down)
    return before, after


def per_device(
    displacement,
    cell_scale,
    material_id,
    stiff_table,
    mass_table,
    pile_block,
    pile_owner,
    node_index,
):
    planes, ny, nz = cell_scale.shape
    rows = planes * ny
    tiles = lax.axis_size("tile")
    _, block_count, width = node_index.shape
    order = pile_block.shape[-1]
    blocks = tiles * block_count
    vmem = pl.BlockSpec(memory_space=pltpu.VMEM)
    smem = pl.BlockSpec(memory_space=pltpu.SMEM)
    big = pltpu.CompilerParams(vmem_limit_bytes=32 * 1024 * 1024)
    field = displacement.reshape(6, planes, ny, nz)
    nodes = node_index.transpose(1, 0, 2).reshape(blocks, width)
    owner = pile_owner.reshape(1, tiles)
    payload, slot_row, slot_column, info = pl.pallas_call(
        functools.partial(gather_kernel, tiles),
        out_shape=(
            jax.ShapeDtypeStruct((tiles, 2 * order), BF16),
            jax.ShapeDtypeStruct((MOST, width), I32),
            jax.ShapeDtypeStruct((MOST, width), I32),
            jax.ShapeDtypeStruct((2 * MOST, width), I32),
        ),
        in_specs=[vmem] * 3,
        out_specs=(vmem,) * 4,
        scratch_shapes=[pltpu.VMEM((MOST, 6 * width), F32)],
        compiler_params=big,
        cost_estimate=pl.CostEstimate(flops=10**9, bytes_accessed=10**6, transcendentals=0),
        name="gather",
    )(displacement.reshape(6, rows, nz), nodes, owner)
    arrived = lax.all_to_all(payload.reshape(tiles, 2, order), "tile", 0, 0, tiled=True)
    before, after = halos(field, cell_scale, material_id)
    soil = pl.pallas_call(
        soil_kernel,
        out_shape=jax.ShapeDtypeStruct(field.shape, F32),
        in_specs=[vmem] * 5 + [smem] * 2,
        out_specs=vmem,
        compiler_params=big,
        cost_estimate=pl.CostEstimate(flops=10**7, bytes_accessed=10**7, transcendentals=0),
        name="soil",
    )(field, cell_scale, material_id, before, after, stiff_table, mass_table)
    returning = pl.pallas_call(
        pile_kernel,
        out_shape=jax.ShapeDtypeStruct((tiles, 2 * order), BF16),
        in_specs=[vmem] * 3,
        out_specs=vmem,
        compiler_params=big,
        cost_estimate=pl.CostEstimate(flops=10**8, bytes_accessed=6 * 10**6, transcendentals=0),
        name="pile",
    )(arrived, pile_block[0], info)
    landed = lax.all_to_all(returning.reshape(tiles, 2, order), "tile", 0, 0, tiled=True)
    result = pl.pallas_call(
        functools.partial(scatter_kernel, tiles),
        out_shape=jax.ShapeDtypeStruct((6, rows, nz), F32),
        in_specs=[vmem] * 4 + [smem],
        out_specs=vmem,
        scratch_shapes=[pltpu.VMEM((6 * rows, MOST * width), BF16)],
        compiler_params=big,
        cost_estimate=pl.CostEstimate(flops=10**9, bytes_accessed=2 * 10**6, transcendentals=0),
        name="scatter",
    )(soil.reshape(6, rows, nz), landed, slot_row, slot_column, info)
    return result.reshape(displacement.shape)


def solution(mesh):
    placed = (
        P(None, None, ("freq", "tile"), None, None),
        P("tile", None, None),
        P("tile", None, None),
        P(None, "freq"),
        P(None, "freq"),
        P(("freq", "tile"), None, None, None),
        P("freq"),
        P(),
    )
    return jax.shard_map(
        per_device,
        mesh=mesh,
        in_specs=placed,
        out_specs=P(None, None, ("freq", "tile"), None, None),
        check_vma=False,
    )
```

time: 184 us -> 60.7 us (0.33)
  the two profiles are of different devices: /device:TPU:1 before, /device:TPU:121 now
where the time goes in v1:
time: 60.7 us; the launch traced here: 60.2 us
  starting transfers between devices  26.2 us (43%)
  waiting for transfers between devices  19.3 us (32%)
  Pallas kernels  6.94 us (11%)
  local copies, waits for them, and re-layouts  6.81 us (11%)
  other arithmetic  0.89 us (1%)
    all_to_all x1, starting transfers between devices, per_device(): lax.all_to_all(payload.reshape(tiles, 2, order), 'tile', 0, 0, tiled=True)  10.9 us
    all_to_all x1, waiting for transfers between devices, per_device(): lax.all_to_all(payload.reshape(tiles, 2, order), 'tile', 0, 0, tiled=True)  8.8 us
    all_to_all x1, starting transfers between devices, per_device(): lax.all_to_all(returning.reshape(tiles, 2, order), 'tile', 0, 0, tiled=True)  8.76 us
    ppermute x1, waiting for transfers between devices, halos(): after = lax.ppermute(plane(0), 'tile', down)  6.17 us
    unnamed x19, local copies, waits for them, and re-layouts  5.18 us
    ppermute x1, starting transfers between devices, halos(): before = lax.ppermute(plane(displacement.shape[1] - 1), 'tile', up)  4.56 us
    ppermute x1, waiting for transfers between devices, halos(): before = lax.ppermute(plane(displacement.shape[1] - 1), 'tile', up)  4.32 us
    pallas_call x1, Pallas kernels, per_device(): pl.pallas_call(functools.partial(scatter_kernel, tiles), out_shape=jax.Sh...  2.1 us
  transfers between devices with their start and end apart: 4, of which 3 were waited for; matrix products, arithmetic and copies ran while one was open for 2% of the time, Pallas kernels for 3%

profile of v1, /device:TPU:121, one launch (start us, length us, event | category | flops | bytes accessed | tf_op | source)
XLA Modules:
  0.0 60.2 jit_solution(15976563674782963241)
XLA Ops:
  0.0 0.0 copy-start.1
  0.0 1.1 %copy-done.1 = f32[2,3,2,48,256]{4,3,2,1,0:T(8,128)S(1)} copy-done((f32[2,3,2,48,256]{4,3,2,1,0:T(8,128)S(1)}, f32[2,3,2,48,256]{4,3,2,1,0:T(8,128)}, u32[]{:S(2)}) %copy-start.1) | copy-done | bytes 589848
  1.1 0.0 copy-start.7
  1.1 0.9 %copy-done.7 = s32[64,3,128]{2,0,1:T(8,128)S(1)} copy-done((s32[64,3,128]{2,0,1:T(8,128)S(1)}, s32[64,3,128]{2,0,1:T(8,128)}, u32[]{:S(2)}) %copy-start.7) | copy-done | bytes 98328
  2.0 0.0 copy-start.8
  2.0 0.7 %copy-done.8 = s32[64]{0:T(128)S(1)} copy-done((s32[64]{0:T(128)S(1)}, s32[64]{0:T(128)}, u32[]{:S(2)}) %copy-start.8) | copy-done | bytes 280
  2.6 0.0 copy-start.3
  2.6 1.5 %gather.1 = (bf16[64,2304]{1,0:T(8,128)(2,1)S(1)}, s32[8,128]{1,0:T(8,128)S(1)}, s32[8,128]{1,0:T(8,128)S(1)}, s32[16,128]{1,0:T(8,128)S(1)}) custom-call(f32[6,96,256]{2,1,0:T(8,128)S(1)} %bitcast.15, s32[192,128]{1,0:T(8,128)S(1)} %bitcast.18, s32[1,64]{1,0:T(1,128)S(1)} %bitcast.19), custom_call_target="tpu_custom_call" | custom-call | flops 1000000000 | bytes 1000000 | tf_op jit(solution)/shard_map/gather/pallas_call | solution.py:237
  4.1 0.8 %reshape.29 = bf16[64,2,1152]{2,1,0:T(2,128)(2,1)} reshape(bf16[64,2304]{1,0:T(8,128)(2,1)S(1)} %get-tuple-element.9) | data formatting | bytes 589824 | tf_op jit(solution)/shard_map/reshape | solution.py:252
  4.9 10.9 %all-to-all-start = ((bf16[64,2,1152]{2,1,0:T(2,128)(2,1)}), bf16[64,2,1152]{2,1,0:T(2,128)(2,1)S(1)}, u32[]{:S(2)}, u32[]{:S(2)}) async-start(bf16[64,2,1152]{2,1,0:T(2,128)(2,1)} %reshape.29), calls=%async_computation | async-start | bytes 589824 | tf_op jit(solution)/shard_map/all_to_all | solution.py:252
  15.8 0.8 %slice_convert_fusion = (f32[1,48,256]{2,1,0:T(8,128)S(1)}, f32[1,48,256]{2,1,0:T(8,128)S(1)}) fusion(s32[2,48,256]{2,1,0:T(8,128)} %kind_ref.1), kind=kLoop, calls=%fused_computation.4 | loop fusion | flops 24576 | bytes 196608 | tf_op jit(solution)/shard_map/convert_element_type | solution.py:208
  16.7 0.0 copy-done.2
  16.7 0.0 copy-done.3
  16.7 0.0 copy-start.4
  16.7 0.0 copy-start.5
  16.7 0.0 copy-start.6
  16.8 8.8 %all-to-all-done.arrived_ref = bf16[64,2,1152]{2,1,0:T(2,128)(2,1)S(1)} async-done(((bf16[64,2,1152]{2,1,0:T(2,128)(2,1)}), bf16[64,2,1152]{2,1,0:T(2,128)(2,1)S(1)}, u32[]{:S(2)}, u32[]{:S(2)}) %all-to-all-start) | async-done | bytes 294944 | tf_op jit(solution)/shard_map/all_to_all | solution.py:252
  25.6 0.0 copy-start
  25.6 2.5 %copy-done = bf16[1,2,1152,1152]{3,2,1,0:T(8,128)(2,1)S(1)} copy-done((bf16[1,2,1152,1152]{3,2,1,0:T(8,128)(2,1)S(1)}, bf16[1,2,1152,1152]{3,2,1,0:T(8,128)(2,1)}, u32[]{:S(2)}) %copy-start) | copy-done | bytes 5308440
  28.1 1.6 %pile.1 = bf16[64,2304]{1,0:T(8,128)(2,1)S(1)} custom-call(bf16[64,2,1152]{2,1,0:T(2,128)(2,1)S(1)} %all-to-all-done.arrived_ref, bf16[2,1152,1152]{2,1,0:T(8,128)(2,1)S(1)} %bitcast.14, s32[16,128]{1,0:T(8,128)S(1)} %get-tuple-element.10.info_ref), custom_call_target="tpu_custom_call" | custom-call | flops 100000000 | bytes 6000000 | tf_op jit(solution)/shard_map/pile/pallas_call | solution.py:263
  29.8 0.8 %reshape.30 = bf16[64,2,1152]{2,1,0:T(2,128)(2,1)} reshape(bf16[64,2304]{1,0:T(8,128)(2,1)S(1)} %pile.1) | data formatting | bytes 589824 | tf_op jit(solution)/shard_map/reshape | solution.py:272
  30.6 8.8 %all-to-all-start.1 = ((bf16[64,2,1152]{2,1,0:T(2,128)(2,1)}), bf16[64,2,1152]{2,1,0:T(2,128)(2,1)S(1)}, u32[]{:S(2)}, u32[]{:S(2)}) async-start(bf16[64,2,1152]{2,1,0:T(2,128)(2,1)} %reshape.30), calls=%async_computation.1 | async-start | bytes 589824 | tf_op jit(solution)/shard_map/all_to_all | solution.py:272
  39.3 4.6 %collective-permute-start = (f32[8,48,256]{2,1,0:T(8,128)S(1)}, f32[8,48,256]{2,1,0:T(8,128)S(1)}, u32[]{:S(2)}, u32[]{:S(2)}) collective-permute-start(f32[8,48,256]{2,1,0:T(8,128)S(1)} %pad_maximum_fusion), channel_id=1, source_target_pairs={{0,4},{4,8},{8,12},{12,16},{16,20},{20,24},{24,28},{28,32},{32,36}... | collective-permute-start | bytes 1179656 | tf_op jit(solution)/shard_map/ppermute | solution.py:210
  44.0 1.9 %collective-permute-start.1 = (f32[8,48,256]{2,1,0:T(8,128)S(1)}, f32[8,48,256]{2,1,0:T(8,128)S(1)}, u32[]{:S(2)}, u32[]{:S(2)}) collective-permute-start(f32[8,48,256]{2,1,0:T(8,128)S(1)} %pad_maximum_fusion.1), channel_id=1, source_target_pairs={{4,0},{8,4},{12,8},{16,12},{20,16},{24,20},{28,24},{32,28},{36,32}... | collective-permute-start | bytes 1179656 | tf_op jit(solution)/shard_map/ppermute | solution.py:211
  45.9 4.3 %collective-permute-done.before_ref = f32[8,48,256]{2,1,0:T(8,128)S(1)} collective-permute-done((f32[8,48,256]{2,1,0:T(8,128)S(1)}, f32[8,48,256]{2,1,0:T(8,128)S(1)}, u32[]{:S(2)}, u32[]{:S(2)}) %collective-permute-start) | collective-permute-done | bytes 393248 | tf_op jit(solution)/shard_map/ppermute | solution.py:210
  50.2 6.2 %collective-permute-done.1.after_ref = f32[8,48,256]{2,1,0:T(8,128)S(1)} collective-permute-done((f32[8,48,256]{2,1,0:T(8,128)S(1)}, f32[8,48,256]{2,1,0:T(8,128)S(1)}, u32[]{:S(2)}, u32[]{:S(2)}) %collective-permute-start.1) | collective-permute-done | bytes 393248 | tf_op jit(solution)/shard_map/ppermute | solution.py:211
  56.4 0.0 copy-done.4
  56.4 0.0 copy-done.5
  56.4 0.0 copy-done.6
  56.4 1.7 %soil.1 = f32[6,2,48,256]{3,2,1,0:T(8,128)S(1)} custom-call(f32[6,2,48,256]{3,2,1,0:T(8,128)S(1)} %bitcast.16, f32[2,48,256]{2,1,0:T(8,128)S(1)} %copy-done.3, s32[2,48,256]{2,1,0:T(8,128)S(1)} %copy-done.4, f32[8,48,256]{2,1,0:T(8,128)S(1)} %collective-permute-done.before_ref, f32[8,48,256]{2,1,0:T(8,128)S(1)} %collective-permute-done.1.after_ref, ...), custom_call_target="tpu_custom_call" | custom-call | flops 10000000 | bytes 10000000 | tf_op jit(solution)/shard_map/soil/pallas_call | solution.py:254
  58.1 0.0 all-to-all-done.1.arrived_ref
  58.1 2.1 %scatter.1 = f32[6,96,256]{2,1,0:T(8,128)} custom-call(f32[6,96,256]{2,1,0:T(8,128)S(1)} %bitcast.17, bf16[64,2,1152]{2,1,0:T(2,128)(2,1)S(1)} %all-to-all-done.1.arrived_ref, s32[8,128]{1,0:T(8,128)S(1)} %get-tuple-element.11.row_ref, s32[8,128]{1,0:T(8,128)S(1)} %get-tuple-element.12.column_ref, s32[16,128]{1,0:T(8,128)S(1)} %get-tuple-element.10.info_ref), custom_call_target="tpu_custom_call" | custom-call | flops 1000000000 | bytes 2000000 | tf_op jit(solution)/shard_map/scatter/pallas_call | solution.py:273
  (6 shorter events, 0.1 us)
Async XLA Ops:
  0.0 1.1 %copy-start.1 = (f32[2,3,2,48,256]{4,3,2,1,0:T(8,128)S(1)}, f32[2,3,2,48,256]{4,3,2,1,0:T(8,128)}, u32[]{:S(2)}) copy-start(f32[2,3,2,48,256]{4,3,2,1,0:T(8,128)} %param.8) | copy-start | bytes 1769476
  1.1 0.9 %copy-start.7 = (s32[64,3,128]{2,0,1:T(8,128)S(1)}, s32[64,3,128]{2,0,1:T(8,128)}, u32[]{:S(2)}) copy-start(s32[64,3,128]{2,0,1:T(8,128)} %param.15) | copy-start | bytes 294916
  2.0 0.7 %copy-start.8 = (s32[64]{0:T(128)S(1)}, s32[64]{0:T(128)}, u32[]{:S(2)}) copy-start(s32[64]{0:T(128)} %param.14) | copy-start | bytes 772
  2.6 14.0 %copy-start.2 = (f32[2,3,2,48,256]{4,3,2,1,0:T(8,128)S(1)}, f32[2,3,2,48,256]{4,3,2,1,0:T(8,128)}, u32[]{:S(2)}) copy-start(f32[2,3,2,48,256]{4,3,2,1,0:T(8,128)} %param.8) | copy-start | bytes 1769476
  2.6 14.1 %copy-start.3 = (f32[2,48,256]{2,1,0:T(8,128)S(1)}, f32[2,48,256]{2,1,0:T(8,128)}, u32[]{:S(2)}) copy-start(f32[2,48,256]{2,1,0:T(8,128)} %scale_ref.1) | copy-start | bytes 294916
  4.9 20.7 %all-to-all-start = ((bf16[64,2,1152]{2,1,0:T(2,128)(2,1)}), bf16[64,2,1152]{2,1,0:T(2,128)(2,1)S(1)}, u32[]{:S(2)}, u32[]{:S(2)}) async-start(bf16[64,2,1152]{2,1,0:T(2,128)(2,1)} %reshape.29), calls=%async_computation | async-start | bytes 589824 | tf_op jit(solution)/shard_map/all_to_all | solution.py:252
  16.7 39.7 %copy-start.4 = (s32[2,48,256]{2,1,0:T(8,128)S(1)}, s32[2,48,256]{2,1,0:T(8,128)}, u32[]{:S(2)}) copy-start(s32[2,48,256]{2,1,0:T(8,128)} %kind_ref.1) | copy-start | bytes 294916
  16.7 39.6 %copy-start.5 = (f32[2,16]{1,0:T(2,128)S(1)}, f32[2,16]{1,0:T(2,128)}, u32[]{:S(2)}) copy-start(f32[2,16]{1,0:T(2,128)} %stiff_ref.1) | copy-start | bytes 388
  16.7 39.6 %copy-start.6 = (f32[2,16]{1,0:T(2,128)S(1)}, f32[2,16]{1,0:T(2,128)}, u32[]{:S(2)}) copy-start(f32[2,16]{1,0:T(2,128)} %mass_ref.1) | copy-start | bytes 388
  25.6 2.5 %copy-start = (bf16[1,2,1152,1152]{3,2,1,0:T(8,128)(2,1)S(1)}, bf16[1,2,1152,1152]{3,2,1,0:T(8,128)(2,1)}, u32[]{:S(2)}) copy-start(bf16[1,2,1152,1152]{3,2,1,0:T(8,128)(2,1)} %param.13) | copy-start | bytes 15925252
  30.6 27.6 %all-to-all-start.1 = ((bf16[64,2,1152]{2,1,0:T(2,128)(2,1)}), bf16[64,2,1152]{2,1,0:T(2,128)(2,1)S(1)}, u32[]{:S(2)}, u32[]{:S(2)}) async-start(bf16[64,2,1152]{2,1,0:T(2,128)(2,1)} %reshape.30), calls=%async_computation.1 | async-start | bytes 589824 | tf_op jit(solution)/shard_map/all_to_all | solution.py:272
  39.3 10.8 %collective-permute-start = (f32[8,48,256]{2,1,0:T(8,128)S(1)}, f32[8,48,256]{2,1,0:T(8,128)S(1)}, u32[]{:S(2)}, u32[]{:S(2)}) collective-permute-start(f32[8,48,256]{2,1,0:T(8,128)S(1)} %pad_maximum_fusion), channel_id=1, source_target_pairs={{0,4},{4,8},{8,12},{12,16},{16,20},{20,24},{24,28},{28,32},{32,36}... | collective-permute-start | bytes 1179656 | tf_op jit(solution)/shard_map/ppermute | solution.py:210
  44.0 12.4 %collective-permute-start.1 = (f32[8,48,256]{2,1,0:T(8,128)S(1)}, f32[8,48,256]{2,1,0:T(8,128)S(1)}, u32[]{:S(2)}, u32[]{:S(2)}) collective-permute-start(f32[8,48,256]{2,1,0:T(8,128)S(1)} %pad_maximum_fusion.1), channel_id=1, source_target_pairs={{4,0},{8,4},{12,8},{16,12},{20,16},{24,20},{28,24},{32,28},{36,32}... | collective-permute-start | bytes 1179656 | tf_op jit(solution)/shard_map/ppermute | solution.py:211

commit v2 on v1

v2 whole, which is shorter than its diff:
```python
import functools

import jax
import jax.numpy as jnp
from jax import lax
from jax.experimental import pallas as pl
from jax.experimental.pallas import tpu as pltpu
from jax.sharding import PartitionSpec as P

MOST = 8
F32 = jnp.float32
BF16 = jnp.bfloat16
I32 = jnp.int32
NT = (((1,), (1,)), ((), ()))


def iota(shape, axis):
    return lax.broadcasted_iota(I32, shape, axis)


def onehot(mask):
    return jnp.where(mask, 1.0, 0.0).astype(BF16)


def dot(left, right):
    return jnp.dot(left, right, preferred_element_type=F32)


def dot_nt(left, right):
    return lax.dot_general(left, right, NT, preferred_element_type=F32)


def slots_of(nodes, me, cells, columns):
    blocks, width = nodes.shape
    local = nodes - me * cells
    inside = (local >= 0) & (local < cells)
    shift = columns.bit_length() - 1
    row1 = jnp.where(inside, (local >> shift) + 1, 0).astype(F32).astype(BF16)
    column = jnp.where(inside, local & (columns - 1), 0).astype(F32).astype(BF16)
    first = onehot(iota((MOST, width), 1) == 0)
    onto = dot_nt(first, onehot(inside))
    upper = onehot(iota((blocks, blocks), 0) < iota((blocks, blocks), 1))
    rank = dot(onto.astype(BF16), upper)
    slot = (onto > 0.5) & (rank == iota((MOST, blocks), 0).astype(F32))
    chosen = onehot(slot)
    return slot, dot(chosen, row1).astype(I32) - 1, dot(chosen, column).astype(I32)


def gather_kernel(
    tiles,
    displacement_hbm,
    nodes_hbm,
    owner_hbm,
    picked_ref,
    info_ref,
    displacement,
    node_buffer,
    owner_buffer,
    semaphores,
):
    me = lax.axis_index("tile")
    copies = [
        pltpu.make_async_copy(source, target, semaphores.at[i])
        for i, (source, target) in enumerate(
            ((nodes_hbm, node_buffer), (owner_hbm, owner_buffer), (displacement_hbm, displacement))
        )
    ]
    for copy in copies:
        copy.start()
    copies[0].wait()
    copies[1].wait()
    components, rows, columns = displacement.shape
    blocks, width = node_buffer.shape
    block_count = blocks // tiles
    nodes = node_buffer[...]
    owner = owner_buffer[...]
    cells = rows * columns
    slot, slot_row, slot_column = slots_of(nodes, me, cells, columns)
    twin_slot, _, _ = slots_of(nodes, me ^ 1, cells, columns)
    target = jnp.concatenate([owner + (b * tiles + 1) for b in range(block_count)], axis=1)
    for i, chosen in enumerate((slot, twin_slot)):
        one = jnp.sum(jnp.where(chosen, target.astype(F32), 0.0), axis=1, keepdims=True).astype(I32) - 1
        info_ref[i * MOST : (i + 1) * MOST, :] = jnp.broadcast_to(one, (MOST, width))
    info_ref[2 * MOST :, :] = jnp.zeros((MOST, width), I32)
    first = onehot(iota((MOST, width), 1) == 0)
    tile_of = jnp.floor(((nodes >> 13).astype(F32) + 0.5) * (1.0 / (cells >> 13)))
    tile_row = dot_nt(first, tile_of.astype(BF16))[0:1, :]
    for b in range(block_count):
        own = jnp.where(owner == me, tile_row[:, b * tiles : (b + 1) * tiles], 0.0)
        info_ref[2 * MOST + b : 2 * MOST + b + 1, :] = jnp.broadcast_to(
            jnp.sum(own, axis=1, keepdims=True).astype(I32), (1, width)
        )
    copies[2].wait()
    field = displacement[...].reshape(components * rows, columns).astype(BF16)
    empty = jnp.zeros((8 - components, width), F32)
    for pair in range(MOST // 2):
        at_column = jnp.concatenate(
            [
                onehot(iota((columns, width), 0) == slot_column[s : s + 1, :])
                for s in (2 * pair, 2 * pair + 1)
            ],
            axis=1,
        )
        taken = dot(field, at_column)
        for i in range(2):
            s = 2 * pair + i
            at_row = iota((rows, width), 0) == slot_row[s : s + 1, :]
            found = []
            for c in range(components):
                one = taken[c * rows : (c + 1) * rows, i * width : (i + 1) * width]
                found.append(jnp.sum(jnp.where(at_row, one, 0.0), axis=0, keepdims=True))
            picked_ref[s] = jnp.concatenate(found + [empty], axis=0).astype(BF16)


def codes_in_lanes(targets, tiles, core, block_count, width):
    owner = targets & (tiles - 1)
    code = ((owner >> 1) * block_count + (targets >> (tiles.bit_length() - 1))) * 8
    code = jnp.where((targets >= 0) & ((owner & 1) == core), code, -width)
    count = targets.shape[0]
    lane = iota((count, width), 1)
    code = jnp.where((lane >> 3) == iota((count, width), 0), code + (lane & 7), 0)
    return jnp.sum(code, axis=0, keepdims=True)


def place_kernel(tiles, picked_ref, twin_ref, info_ref, payload_ref):
    core = lax.axis_index("tile") & 1
    chips, block_count, padded, width = payload_ref.shape
    code = codes_in_lanes(info_ref[0 : 2 * MOST, :], tiles, core, block_count, width)
    place = onehot(iota((chips * block_count * padded, width), 0) == code)
    picked = jnp.concatenate([picked_ref[...].reshape(MOST * 8, width), twin_ref[...].reshape(MOST * 8, width)], axis=0)
    payload_ref[...] = dot(place, picked).astype(BF16).reshape(payload_ref.shape)


def pile_kernel(arrived_ref, imag_ref, block_hbm, info_ref, order_ref, payload_ref, real_ref, semaphores):
    chips, block_count, padded, width = arrived_ref.shape
    components = 6
    half = components // 2
    part = real_ref.shape[0] // half
    copies = []
    for c in range(half):
        rows = slice(c * part, (c + 1) * part)
        copies.append(pltpu.make_async_copy(block_hbm.at[0, rows], real_ref.at[rows], semaphores.at[c]))
        copies[c].start()
    vector = jnp.sum(arrived_ref[...].astype(F32), axis=0)
    vector = jnp.concatenate(
        [
            jnp.concatenate(
                [vector[b, i * half + c : i * half + c + 1, :] for c in range(half) for b in range(block_count)], axis=1
            )
            for i in range(2)
        ],
        axis=0,
    ).astype(BF16)
    by_imag = dot_nt(vector, imag_ref[...])
    real, imag = [], []
    for c in range(half):
        rows = slice(c * part, (c + 1) * part)
        copies[c].wait()
        by_real = dot_nt(vector, real_ref[rows, :])
        real.append(by_real[0:1] - by_imag[1:2, rows])
        imag.append(by_real[1:2] + by_imag[0:1, rows])
    empty = jnp.zeros((padded - components, width), F32)
    for b in range(block_count):
        piece = [one[:, b * width : (b + 1) * width] for one in real + imag]
        piece = jnp.concatenate(piece + [empty], axis=0)
        chip = info_ref[2 * MOST + b : 2 * MOST + b + 1, :] >> 1
        for k in range(chips):
            payload_ref[k, b] = jnp.where(chip == k, piece, 0.0).astype(BF16)


def choose_kernel(tiles, landed_ref, info_ref, order_ref, own_ref, twin_ref):
    core = lax.axis_index("tile") & 1
    chips, block_count, padded, width = landed_ref.shape
    slab = chips * block_count * padded
    targets = info_ref[0 : 2 * MOST, :]
    owner = targets & (tiles - 1)
    code = ((owner >> 1) * block_count + (targets >> (tiles.bit_length() - 1))) * padded
    code = jnp.where((targets >= 0) & ((owner & 1) == core), code, -padded)
    shape = (2 * MOST, padded, slab)
    take = onehot(iota(shape, 2) == code[:, 0:1].reshape(2 * MOST, 1, 1) + iota(shape, 1))
    chosen = dot(take.reshape(2 * MOST * padded, slab), landed_ref[...].reshape(slab, width)).astype(BF16)
    chosen = chosen.reshape(2, MOST, padded, width)
    own_ref[...] = chosen[0]
    twin_ref[...] = chosen[1]


def scatter_kernel(soil_ref, own_ref, twin_ref, row_ref, at_column_ref, result_ref, spread):
    components, rows, columns = soil_ref.shape
    width = row_ref.shape[1]
    for s in range(MOST):
        piece = own_ref[s].astype(F32) + twin_ref[s].astype(F32)
        at_row = iota((rows, width), 0) == row_ref[s : s + 1, :]
        for k in range(components):
            spread[k * rows : (k + 1) * rows, s * width : (s + 1) * width] = jnp.where(
                at_row, piece[k : k + 1, :], 0.0
            ).astype(BF16)
    added = dot_nt(spread[...], at_column_ref[...])
    result_ref[...] = soil_ref[...] + added.reshape(components, rows, columns)


def fetch_kernel(after_ref, block_hbm, imag_ref, semaphore):
    copy = pltpu.make_async_copy(block_hbm.at[1], imag_ref, semaphore)
    copy.start()
    copy.wait()


def plane_kernel(last, order_ref, displacement_hbm, scale_hbm, kind_hbm, plane_ref, kind, semaphores):
    planes = scale_hbm.shape[0]
    x = jnp.where((lax.axis_index("tile") & 1) == last, planes - 1, 0)
    sources = (kind_hbm.at[x], scale_hbm.at[x], displacement_hbm.at[:, x])
    targets = (kind, plane_ref.at[6], plane_ref.at[0:6])
    copies = [pltpu.make_async_copy(*two, semaphores.at[i]) for i, two in enumerate(zip(sources, targets))]
    for copy in copies:
        copy.start()
    copies[0].wait()
    plane_ref[7] = kind[...].astype(F32)
    for copy in copies[1:]:
        copy.wait()


def lookup(table_ref, row, kind):
    bits = [(kind & (1 << k)) != 0 for k in range(4)]
    level = [table_ref[row, k] for k in range(16)]
    for bit in bits:
        level = [jnp.where(bit, level[2 * k + 1], level[2 * k]) for k in range(len(level) // 2)]
    return level[0]


def half_stiffness(table_ref, kind, scale):
    return [0.5 * (lookup(table_ref, i, kind) * scale) for i in range(2)]


def flux(face, near, far):
    strain = [near[k] - far[k] for k in range(6)]
    real = [face[0] * strain[c] - face[1] * strain[3 + c] for c in range(3)]
    imag = [face[0] * strain[3 + c] + face[1] * strain[c] for c in range(3)]
    return real + imag


def soil_kernel(
    order_ref,
    displacement_hbm,
    scale_hbm,
    kind_hbm,
    near_hbm,
    nodes_hbm,
    stiff_ref,
    mass_ref,
    soil_ref,
    edge_ref,
    row_ref,
    at_column_ref,
    displacement_ref,
    scale_ref,
    kind_ref,
    near_ref,
    node_buffer,
    semaphores,
):
    sources = (nodes_hbm, kind_hbm, scale_hbm, displacement_hbm, near_hbm)
    targets = (node_buffer, kind_ref, scale_ref, displacement_ref, near_ref)
    copies = [pltpu.make_async_copy(*two, semaphores.at[i]) for i, two in enumerate(zip(sources, targets))]
    for copy in copies:
        copy.start()
    _, planes, ny, nz = displacement_ref.shape
    shape = (ny, nz)
    tile = lax.axis_index("tile")
    odd = tile & 1
    even = odd == 0
    copies[0].wait()
    width = node_buffer.shape[1]
    _, row_ref[...], slot_column = slots_of(node_buffer[...], tile, planes * ny * nz, nz)
    for s in range(MOST):
        at_column = onehot(iota((nz, width), 0) == slot_column[s : s + 1, :])
        at_column_ref[:, s * width : (s + 1) * width] = at_column
    for copy in copies[1:]:
        copy.wait()
    at_y, at_z = iota(shape, 0), iota(shape, 1)
    y_last, z_last = at_y == ny - 1, at_z == nz - 1
    edges = (
        jnp.where(at_y == 0, 0.5, 0.0)
        + jnp.where(y_last, 0.5, 0.0)
        + jnp.where(at_z == 0, 0.5, 0.0)
        + jnp.where(z_last, 0.5, 0.0)
    )
    half = [half_stiffness(stiff_ref, kind_ref[x], scale_ref[x]) for x in range(planes)]
    near_half = half_stiffness(stiff_ref, near_ref[7].astype(I32), near_ref[6])
    near = [near_ref[k] for k in range(6)]
    fields = [[displacement_ref[k, x] for k in range(6)] for x in range(planes)]

    def chosen(first, last, flag):
        return [jnp.where(flag, b, a) for a, b in zip(first, last)]

    beside = chosen(fields[0], fields[-1], even)
    beside_half = chosen(half[0], half[-1], even)
    near_flux = flux([beside_half[i] + near_half[i] for i in range(2)], beside, near)
    outer = chosen(fields[0] + half[0], fields[-1] + half[-1], jnp.logical_not(even))
    for k in range(8):
        edge_ref[k] = outer[k]
    before = [0.0] * 6
    for x in range(planes):
        u, own = fields[x], half[x]
        diagonal = [lookup(mass_ref, i, kind_ref[x]) + 2.0 * edges * own[i] for i in range(2)]
        total = [diagonal[0] * u[c] - diagonal[1] * u[3 + c] for c in range(3)]
        total += [diagonal[0] * u[3 + c] + diagonal[1] * u[c] for c in range(3)]
        total = [total[k] - before[k] for k in range(6)]
        if x < planes - 1:
            before = flux([own[i] + half[x + 1][i] for i in range(2)], u, fields[x + 1])
            total = [total[k] + before[k] for k in range(6)]
        for axis, last in ((0, y_last), (1, z_last)):
            size = shape[axis]
            face = [jnp.where(last, 0.0, own[i] + pltpu.roll(own[i], size - 1, axis)) for i in range(2)]
            next_to = [pltpu.roll(u[k], size - 1, axis) for k in range(6)]
            along = flux(face, u, next_to)
            total = [total[k] + along[k] - pltpu.roll(along[k], 1, axis) for k in range(6)]
        if x in (0, planes - 1):
            total = [jnp.where(even == (x == planes - 1), total[k] + near_flux[k], total[k]) for k in range(6)]
        for k in range(6):
            soil_ref[k, x] = total[k]


def outer_kernel(soil_ref, edge_ref, far_ref, stiff_ref, result_ref):
    planes = result_ref.shape[1]
    far_half = half_stiffness(stiff_ref, far_ref[7].astype(I32), far_ref[6])
    face = [edge_ref[6 + i] + far_half[i] for i in range(2)]
    along = flux(face, [edge_ref[k] for k in range(6)], [far_ref[k] for k in range(6)])
    x = (lax.axis_index("tile") & 1) * (planes - 1)
    for k in range(6):
        result_ref[k, x] = soil_ref[k, x] + along[k]


def per_device(
    displacement,
    cell_scale,
    material_id,
    stiff_table,
    mass_table,
    pile_block,
    pile_owner,
    node_index,
):
    planes, ny, nz = cell_scale.shape
    rows = planes * ny
    tiles = lax.axis_size("tile")
    chips = tiles // 2
    _, block_count, width = node_index.shape
    blocks = tiles * block_count
    vmem = pl.BlockSpec(memory_space=pltpu.VMEM)
    smem = pl.BlockSpec(memory_space=pltpu.SMEM)
    hbm = pl.BlockSpec(memory_space=pltpu.HBM)
    anywhere = pl.BlockSpec(memory_space=pl.ANY)
    dma = pltpu.SemaphoreType.DMA

    def call(kernel, name, out_shape, in_specs, scratch=(), flops=10**8, moved=10**6):
        return pl.pallas_call(
            kernel,
            out_shape=out_shape,
            in_specs=in_specs,
            out_specs=jax.tree.map(lambda _: vmem, out_shape),
            scratch_shapes=list(scratch),
            compiler_params=pltpu.CompilerParams(vmem_limit_bytes=16 * 1024 * 1024),
            cost_estimate=pl.CostEstimate(flops=flops, bytes_accessed=moved, transcendentals=0),
            name=name,
        )

    def in_hbm(array):
        return pltpu.with_memory_space_constraint(array, pltpu.HBM)

    def shape(dims, kind):
        return jax.ShapeDtypeStruct(dims, kind)

    field = displacement.reshape(6, planes, ny, nz)
    nodes = node_index.transpose(1, 0, 2).reshape(blocks, width)
    owner = pile_owner.reshape(1, tiles)
    slab = (chips, block_count, 8, width)
    pair = [(i, i ^ 1) for i in range(tiles)]
    groups = [[2 * chip + core for chip in range(chips)] for core in range(2)]

    def exchange(payload):
        return lax.all_to_all(payload, "tile", 0, 0, axis_index_groups=groups, tiled=True)

    picked, info = call(
        functools.partial(gather_kernel, tiles),
        "gather",
        (
            shape((MOST, 8, width), BF16),
            shape((3 * MOST, width), I32),
        ),
        [hbm] * 3,
        [
            pltpu.VMEM((6, rows, nz), F32),
            pltpu.VMEM((blocks, width), I32),
            pltpu.VMEM((1, tiles), I32),
            dma((3,)),
        ],
    )(in_hbm(displacement.reshape(6, rows, nz)), in_hbm(nodes), in_hbm(owner))
    payload = call(functools.partial(place_kernel, tiles), "place", shape(slab, BF16), [vmem] * 3)(
        picked, lax.ppermute(picked, "tile", pair), info
    )
    arrived = exchange(payload)

    size = (8, ny, nz)

    def plane(last, order):
        return call(
            functools.partial(plane_kernel, last),
            "plane",
            shape(size, F32),
            [anywhere] + [hbm] * 3,
            [pltpu.VMEM((ny, nz), I32), dma((3,))],
        )(order, in_hbm(field), in_hbm(cell_scale), in_hbm(material_id))

    to_near = plane(0, payload)
    near = lax.ppermute(to_near, "tile", pair)
    order = pile_block.shape[-1]
    block = in_hbm(pile_block.reshape(2, order, order))
    square = (order, order)
    imag = call(fetch_kernel, "fetch", shape(square, BF16), [anywhere, hbm], [dma], flops=10**11, moved=10**8)(to_near, block)
    returning = call(
        pile_kernel,
        "pile",
        shape(slab, BF16),
        [vmem, vmem, hbm, vmem, anywhere],
        [pltpu.VMEM(square, BF16), dma((3,))],
    )(arrived, imag, block, info, near)
    landed = exchange(returning)
    next_chip = [(i, i + 1) for i in range(1, tiles - 1, 2)]
    far = lax.ppermute(plane(1, returning), "tile", next_chip + [(j, i) for i, j in next_chip])

    soil, edge, slot_row, at_column = call(
        soil_kernel,
        "soil",
        (shape(field.shape, F32), shape(size, F32), shape((MOST, width), I32), shape((nz, MOST * width), BF16)),
        [anywhere] + [hbm] * 5 + [smem] * 2,
        [
            pltpu.VMEM(field.shape, F32),
            pltpu.VMEM(cell_scale.shape, F32),
            pltpu.VMEM(cell_scale.shape, I32),
            pltpu.VMEM(size, F32),
            pltpu.VMEM((blocks, width), I32),
            dma((5,)),
        ],
        flops=10**11,
        moved=10**7,
    )(returning, *map(in_hbm, (field, cell_scale, material_id, near, nodes)), stiff_table, mass_table)
    slots = shape((MOST, 8, width), BF16)
    own, twin = call(functools.partial(choose_kernel, tiles), "choose", (slots, slots), [vmem] * 2 + [anywhere])(
        landed, info, soil
    )
    twin = lax.ppermute(twin, "tile", pair)
    soil = pl.pallas_call(
        outer_kernel,
        out_shape=shape(field.shape, F32),
        in_specs=[vmem] * 3 + [smem],
        out_specs=vmem,
        input_output_aliases={0: 0},
        compiler_params=pltpu.CompilerParams(vmem_limit_bytes=16 * 1024 * 1024),
        cost_estimate=pl.CostEstimate(flops=10**10, bytes_accessed=10**6, transcendentals=0),
        name="outer",
    )(soil, edge, far, stiff_table)
    result = call(
        scatter_kernel,
        "scatter",
        shape((6, rows, nz), F32),
        [vmem] * 5,
        [pltpu.VMEM((6 * rows, MOST * width), BF16)],
    )(soil.reshape(6, rows, nz), own, twin, slot_row, at_column)
    return result.reshape(displacement.shape)


def solution(mesh):
    placed = (
        P(None, None, ("freq", "tile"), None, None),
        P("tile", None, None),
        P("tile", None, None),
        P(None, "freq"),
        P(None, "freq"),
        P(("freq", "tile"), None, None, None),
        P("freq"),
        P(),
    )
    return jax.shard_map(
        per_device,
        mesh=mesh,
        in_specs=placed,
        out_specs=P(None, None, ("freq", "tile"), None, None),
        check_vma=False,
    )
```

time: 60.7 us -> 50.7 us (0.84)
  the two profiles are of different devices: /device:TPU:121 before, /device:TPU:1 now
where the time goes in v2:
time: 50.7 us; the launch traced here: 50.3 us
  starting transfers between devices  25.6 us (50%)
  Pallas kernels  16.8 us (33%)
  waiting for transfers between devices  7.74 us (15%)
    all_to_all x2, starting transfers between devices, exchange(): lax.all_to_all(payload, 'tile', 0, 0, axis_index_groups=groups, tiled=True)  13.6 us
    all_to_all x2, waiting for transfers between devices, exchange(): lax.all_to_all(payload, 'tile', 0, 0, axis_index_groups=groups, tiled=True)  6.82 us
    ppermute x1, starting transfers between devices, per_device(): lax.ppermute(plane(1, returning), 'tile', next_chip + [(j, i) for i, j in...  4.92 us
    pallas_call x1, Pallas kernels, per_device(): call(pile_kernel, 'pile', shape(slab, BF16), [vmem, vmem, hbm, vmem, anyw...  3.37 us
    ppermute x1, starting transfers between devices, per_device(): lax.ppermute(picked, 'tile', pair)  3.32 us
    pallas_call x1, Pallas kernels, per_device(): call(soil_kernel, 'soil', (shape(field.shape, F32), shape(size, F32), sha...  3.31 us
    ppermute x1, starting transfers between devices, per_device(): twin = lax.ppermute(twin, 'tile', pair)  3.04 us
    pallas_call x2, Pallas kernels, plane(): call(functools.partial(plane_kernel, last), 'plane', shape(size, F32), [a...  2.86 us
  transfers between devices with their start and end apart: 6, of which 4 were waited for; matrix products, arithmetic and copies ran while one was open for 0% of the time, Pallas kernels for 18%

profile of v2, /device:TPU:1, one launch (start us, length us, event | category | flops | bytes accessed | tf_op | source)
XLA Modules:
  0.0 50.3 jit_solution(11008134660279543235)
XLA Ops:
  0.0 2.2 %gather.1 = (bf16[8,8,128]{2,1,0:T(8,128)(2,1)S(1)}, s32[24,128]{1,0:T(8,128)S(1)}) custom-call(f32[6,96,256]{2,1,0:T(8,128)} %bitcast.12, s32[192,128]{1,0:T(8,128)} %bitcast.16, s32[1,64]{1,0:T(1,128)} %bitcast.18), custom_call_target="tpu_custom_call" | custom-call | flops 100000000 | bytes 1000000 | tf_op jit(solution)/shard_map/gather/pallas_call | solution.py:382
  2.2 3.3 %collective-permute-start = (bf16[8,8,128]{2,1,0:T(8,128)(2,1)S(1)}, bf16[8,8,128]{2,1,0:T(8,128)(2,1)S(1)}, u32[]{:S(2)}, u32[]{:S(2)}) collective-permute-start(bf16[8,8,128]{2,1,0:T(8,128)(2,1)S(1)} %get-tuple-element.13.picked_ref), channel_id=1, source_target_pairs={{0,4},{4,0},{8,12},{12,8},{16,20},{20,16},{24,28},{28,24},{32,36},... | collective-permute-start | bytes 49160 | tf_op jit(solution)/shard_map/ppermute | solution.py:398
  5.6 0.8 %collective-permute-done.twin_ref = bf16[8,8,128]{2,1,0:T(8,128)(2,1)S(1)} collective-permute-done((bf16[8,8,128]{2,1,0:T(8,128)(2,1)S(1)}, bf16[8,8,128]{2,1,0:T(8,128)(2,1)S(1)}, u32[]{:S(2)}, u32[]{:S(2)}) %collective-permute-start) | collective-permute-done | bytes 16416 | tf_op jit(solution)/shard_map/ppermute | solution.py:398
  6.4 0.9 %place.1.order_ref = bf16[32,3,8,128]{3,2,1,0:T(8,128)(2,1)} custom-call(bf16[8,8,128]{2,1,0:T(8,128)(2,1)S(1)} %get-tuple-element.13.picked_ref, bf16[8,8,128]{2,1,0:T(8,128)(2,1)S(1)} %collective-permute-done.twin_ref, s32[24,128]{1,0:T(8,128)S(1)} %get-tuple-element.14.info_ref), custom_call_target="tpu_custom_call" | custom-call | flops 100000000 | bytes 1000000 | tf_op jit(solution)/shard_map/place/pallas_call | solution.py:397
  7.3 9.5 %all-to-all-start = ((bf16[32,3,8,128]{3,2,1,0:T(8,128)(2,1)}), bf16[32,3,8,128]{3,2,1,0:T(8,128)(2,1)S(1)}, u32[]{:S(2)}, u32[]{:S(2)}) async-start(bf16[32,3,8,128]{3,2,1,0:T(8,128)(2,1)} %place.1.order_ref), calls=%async_computation | async-start | bytes 393216 | tf_op jit(solution)/shard_map/all_to_all | solution.py:380
  16.8 1.8 %plane.2.after_ref = f32[8,48,256]{2,1,0:T(8,128)} custom-call(bf16[32,3,8,128]{3,2,1,0:T(8,128)(2,1)} %place.1.order_ref, f32[6,2,48,256]{3,2,1,0:T(8,128)} %bitcast.13, f32[2,48,256]{2,1,0:T(8,128)} %scale_hbm.5, s32[2,48,256]{2,1,0:T(8,128)} %kind_hbm.5), custom_call_target="tpu_custom_call" | custom-call | flops 100000000 | bytes 1000000 | tf_op jit(solution)/shard_map/plane/pallas_call | solution.py:405
  18.6 0.7 %collective-permute-start.1 = (f32[8,48,256]{2,1,0:T(8,128)}, f32[8,48,256]{2,1,0:T(8,128)S(1)}, u32[]{:S(2)}, u32[]{:S(2)}) collective-permute-start(f32[8,48,256]{2,1,0:T(8,128)} %plane.2.after_ref), channel_id=1, source_target_pairs={{0,4},{4,0},{8,12},{12,8},{16,20},{20,16},{24,28},{28,24},{32,36},... | collective-permute-start | bytes 1179656 | tf_op jit(solution)/shard_map/ppermute | solution.py:414
  19.3 1.8 %fetch.1.imag_ref = bf16[1152,1152]{1,0:T(8,128)(2,1)S(1)} custom-call(f32[8,48,256]{2,1,0:T(8,128)} %plane.2.after_ref, bf16[2,1152,1152]{2,1,0:T(8,128)(2,1)} %bitcast.10), custom_call_target="tpu_custom_call" | custom-call | flops 99999997952 | bytes 100000000 | tf_op jit(solution)/shard_map/fetch/pallas_call | solution.py:418
  21.1 0.0 copy-start.1
  21.1 0.0 copy-start.2
  21.1 6.2 %all-to-all-done.arrived_ref = bf16[32,3,8,128]{3,2,1,0:T(8,128)(2,1)S(1)} async-done(((bf16[32,3,8,128]{3,2,1,0:T(8,128)(2,1)}), bf16[32,3,8,128]{3,2,1,0:T(8,128)(2,1)S(1)}, u32[]{:S(2)}, u32[]{:S(2)}) %all-to-all-start) | async-done | bytes 196640 | tf_op jit(solution)/shard_map/all_to_all | solution.py:380
  27.3 0.0 collective-permute-done.1.order_ref.near_hbm
  27.3 0.0 copy-start
  27.3 3.4 %pile.1.order_ref = bf16[32,3,8,128]{3,2,1,0:T(8,128)(2,1)} custom-call(bf16[32,3,8,128]{3,2,1,0:T(8,128)(2,1)S(1)} %all-to-all-done.arrived_ref, bf16[1152,1152]{1,0:T(8,128)(2,1)S(1)} %fetch.1.imag_ref, bf16[2,1152,1152]{2,1,0:T(8,128)(2,1)} %bitcast.11, s32[24,128]{1,0:T(8,128)S(1)} %get-tuple-element.14.info_ref, ...), custom_call_target="tpu_custom_call" | custom-call | flops 100000000 | bytes 1000000 | tf_op jit(solution)/shard_map/pile/pallas_call | solution.py:419
  30.7 4.2 %all-to-all-start.1 = ((bf16[32,3,8,128]{3,2,1,0:T(8,128)(2,1)}), bf16[32,3,8,128]{3,2,1,0:T(8,128)(2,1)S(1)}, u32[]{:S(2)}, u32[]{:S(2)}) async-start(bf16[32,3,8,128]{3,2,1,0:T(8,128)(2,1)} %pile.1.order_ref), calls=%async_computation.1 | async-start | bytes 393216 | tf_op jit(solution)/shard_map/all_to_all | solution.py:380
  34.9 1.1 %plane.3 = f32[8,48,256]{2,1,0:T(8,128)S(1)} custom-call(bf16[32,3,8,128]{3,2,1,0:T(8,128)(2,1)} %pile.1.order_ref, f32[6,2,48,256]{3,2,1,0:T(8,128)} %bitcast.14, f32[2,48,256]{2,1,0:T(8,128)} %scale_hbm.5, s32[2,48,256]{2,1,0:T(8,128)} %kind_hbm.5), custom_call_target="tpu_custom_call" | custom-call | flops 100000000 | bytes 1000000 | tf_op jit(solution)/shard_map/plane/pallas_call | solution.py:405
  36.0 4.9 %collective-permute-start.2 = (f32[8,48,256]{2,1,0:T(8,128)S(1)}, f32[8,48,256]{2,1,0:T(8,128)S(1)}, u32[]{:S(2)}, u32[]{:S(2)}) collective-permute-start(f32[8,48,256]{2,1,0:T(8,128)S(1)} %plane.3), channel_id=1, source_target_pairs={{4,8},{12,16},{20,24},{28,32},{36,40},{44,48},{52,56},{60,64},{68,... | collective-permute-start | bytes 1179656 | tf_op jit(solution)/shard_map/ppermute | solution.py:428
  40.9 0.0 copy-done
  40.9 0.0 copy-done.1
  40.9 0.0 copy-done.2
  40.9 3.3 %soil.1 = (f32[6,2,48,256]{3,2,1,0:T(8,128)S(1)}, f32[8,48,256]{2,1,0:T(8,128)S(1)}, s32[8,128]{1,0:T(8,128)S(1)}, bf16[256,1024]{1,0:T(8,128)(2,1)S(1)}) custom-call(bf16[32,3,8,128]{3,2,1,0:T(8,128)(2,1)} %pile.1.order_ref, f32[6,2,48,256]{3,2,1,0:T(8,128)} %bitcast.15, f32[2,48,256]{2,1,0:T(8,128)} %scale_hbm.5, s32[2,48,256]{2,1,0:T(8,128)} %kind_hbm.5, ...), custom_call_target="tpu_custom_call" | custom-call | flops 99999997952 | bytes 10000000 | tf_op jit(solution)/shard_map/soil/pallas_call | solution.py:430
  44.2 0.6 %all-to-all-done.1.landed_ref = bf16[32,3,8,128]{3,2,1,0:T(8,128)(2,1)S(1)} async-done(((bf16[32,3,8,128]{3,2,1,0:T(8,128)(2,1)}), bf16[32,3,8,128]{3,2,1,0:T(8,128)(2,1)S(1)}, u32[]{:S(2)}, u32[]{:S(2)}) %all-to-all-start.1) | async-done | bytes 196640 | tf_op jit(solution)/shard_map/all_to_all | solution.py:380
  44.8 0.3 choose.1
  45.1 3.0 %collective-permute-start.3 = (bf16[8,8,128]{2,1,0:T(8,128)(2,1)S(1)}, bf16[8,8,128]{2,1,0:T(8,128)(2,1)S(1)}, u32[]{:S(2)}, u32[]{:S(2)}) collective-permute-start(bf16[8,8,128]{2,1,0:T(8,128)(2,1)S(1)} %get-tuple-element.18), channel_id=1, source_target_pairs={{0,4},{4,0},{8,12},{12,8},{16,20},{20,16},{24,28},{28,24},{32,36},... | collective-permute-start | bytes 49160 | tf_op jit(solution)/shard_map/ppermute | solution.py:450
  48.1 0.0 collective-permute-done.2.far_ref
  48.1 0.8 %outer.1 = f32[6,2,48,256]{3,2,1,0:T(8,128)S(1)} custom-call(f32[6,2,48,256]{3,2,1,0:T(8,128)S(1)} %get-tuple-element.15.soil_ref.order_ref, f32[8,48,256]{2,1,0:T(8,128)S(1)} %get-tuple-element.16.edge_ref, f32[8,48,256]{2,1,0:T(8,128)S(1)} %collective-permute-done.2.far_ref, f32[2,16]{1,0:T(2,128)S(1)} %copy-done.2), custom_call_target="tpu_custom_call", output_to_operand_aliasing={{}: (0, {})} | custom-call | flops 10000000000 | bytes 1000000 | tf_op jit(solution)/shard_map/outer/pallas_call | solution.py:451
  48.9 0.1 collective-permute-done.3.twin_ref
  49.0 1.4 %scatter.1 = f32[6,96,256]{2,1,0:T(8,128)} custom-call(f32[6,96,256]{2,1,0:T(8,128)S(1)} %bitcast.9, bf16[8,8,128]{2,1,0:T(8,128)(2,1)S(1)} %get-tuple-element.17.own_ref, bf16[8,8,128]{2,1,0:T(8,128)(2,1)S(1)} %collective-permute-done.3.twin_ref, s32[8,128]{1,0:T(8,128)S(1)} %get-tuple-element.19.row_ref, bf16[256,1024]{1,0:T(8,128)(2,1)S(1)} %get-tuple-element.20.at_column_ref), custom_call_target="tpu_custom_call" | custom-call | flops 100000000 | bytes 1000000 | tf_op jit(solution)/shard_map/scatter/pallas_call | solution.py:461
Async XLA Ops:
  2.2 4.2 %collective-permute-start = (bf16[8,8,128]{2,1,0:T(8,128)(2,1)S(1)}, bf16[8,8,128]{2,1,0:T(8,128)(2,1)S(1)}, u32[]{:S(2)}, u32[]{:S(2)}) collective-permute-start(bf16[8,8,128]{2,1,0:T(8,128)(2,1)S(1)} %get-tuple-element.13.picked_ref), channel_id=1, source_target_pairs={{0,4},{4,0},{8,12},{12,8},{16,20},{20,16},{24,28},{28,24},{32,36},... | collective-permute-start | bytes 49160 | tf_op jit(solution)/shard_map/ppermute | solution.py:398
  7.3 20.0 %all-to-all-start = ((bf16[32,3,8,128]{3,2,1,0:T(8,128)(2,1)}), bf16[32,3,8,128]{3,2,1,0:T(8,128)(2,1)S(1)}, u32[]{:S(2)}, u32[]{:S(2)}) async-start(bf16[32,3,8,128]{3,2,1,0:T(8,128)(2,1)} %place.1.order_ref), calls=%async_computation | async-start | bytes 393216 | tf_op jit(solution)/shard_map/all_to_all | solution.py:380
  18.6 8.7 %collective-permute-start.1 = (f32[8,48,256]{2,1,0:T(8,128)}, f32[8,48,256]{2,1,0:T(8,128)S(1)}, u32[]{:S(2)}, u32[]{:S(2)}) collective-permute-start(f32[8,48,256]{2,1,0:T(8,128)} %plane.2.after_ref), channel_id=1, source_target_pairs={{0,4},{4,0},{8,12},{12,8},{16,20},{20,16},{24,28},{28,24},{32,36},... | collective-permute-start | bytes 1179656 | tf_op jit(solution)/shard_map/ppermute | solution.py:414
  21.1 19.8 %copy-start.1 = (f32[2,16]{1,0:T(2,128)S(1)}, f32[2,16]{1,0:T(2,128)}, u32[]{:S(2)}) copy-start(f32[2,16]{1,0:T(2,128)} %mass_ref.1) | copy-start | bytes 388
  21.1 19.8 %copy-start.2 = (f32[2,16]{1,0:T(2,128)S(1)}, f32[2,16]{1,0:T(2,128)}, u32[]{:S(2)}) copy-start(f32[2,16]{1,0:T(2,128)} %stiff_ref.3) | copy-start | bytes 388
  27.3 13.5 %copy-start = (f32[8,48,256]{2,1,0:T(8,128)}, f32[8,48,256]{2,1,0:T(8,128)S(1)}, u32[]{:S(2)}) copy-start(f32[8,48,256]{2,1,0:T(8,128)S(1)} %collective-permute-done.1.order_ref.near_hbm) | copy-start | bytes 1179652
  30.7 14.1 %all-to-all-start.1 = ((bf16[32,3,8,128]{3,2,1,0:T(8,128)(2,1)}), bf16[32,3,8,128]{3,2,1,0:T(8,128)(2,1)S(1)}, u32[]{:S(2)}, u32[]{:S(2)}) async-start(bf16[32,3,8,128]{3,2,1,0:T(8,128)(2,1)} %pile.1.order_ref), calls=%async_computation.1 | async-start | bytes 393216 | tf_op jit(solution)/shard_map/all_to_all | solution.py:380
  36.0 12.2 %collective-permute-start.2 = (f32[8,48,256]{2,1,0:T(8,128)S(1)}, f32[8,48,256]{2,1,0:T(8,128)S(1)}, u32[]{:S(2)}, u32[]{:S(2)}) collective-permute-start(f32[8,48,256]{2,1,0:T(8,128)S(1)} %plane.3), channel_id=1, source_target_pairs={{4,8},{12,16},{20,24},{28,32},{36,40},{44,48},{52,56},{60,64},{68,... | collective-permute-start | bytes 1179656 | tf_op jit(solution)/shard_map/ppermute | solution.py:428
  45.1 3.9 %collective-permute-start.3 = (bf16[8,8,128]{2,1,0:T(8,128)(2,1)S(1)}, bf16[8,8,128]{2,1,0:T(8,128)(2,1)S(1)}, u32[]{:S(2)}, u32[]{:S(2)}) collective-permute-start(bf16[8,8,128]{2,1,0:T(8,128)(2,1)S(1)} %get-tuple-element.18), channel_id=1, source_target_pairs={{0,4},{4,0},{8,12},{12,8},{16,20},{20,16},{24,28},{28,24},{32,36},... | collective-permute-start | bytes 49160 | tf_op jit(solution)/shard_map/ppermute | solution.py:450

commit v3 on v2

v3 whole, which is shorter than its diff:
```python
import functools

import jax
import jax.numpy as jnp
from jax import lax
from jax.experimental import pallas as pl
from jax.experimental.pallas import tpu as pltpu
from jax.sharding import PartitionSpec as P

MOST = 8
F32 = jnp.float32
BF16 = jnp.bfloat16
I32 = jnp.int32
NT = (((1,), (1,)), ((), ()))


def iota(shape, axis):
    return lax.broadcasted_iota(I32, shape, axis)


def onehot(mask):
    return jnp.where(mask, 1.0, 0.0).astype(BF16)


def dot(left, right):
    return jnp.dot(left, right, preferred_element_type=F32)


def dot_nt(left, right):
    return lax.dot_general(left, right, NT, preferred_element_type=F32)


def slots_of(nodes, me, cells, columns):
    blocks, width = nodes.shape
    local = nodes - me * cells
    inside = (local >= 0) & (local < cells)
    shift = columns.bit_length() - 1
    row1 = jnp.where(inside, (local >> shift) + 1, 0).astype(F32).astype(BF16)
    column = jnp.where(inside, local & (columns - 1), 0).astype(F32).astype(BF16)
    first = onehot(iota((MOST, width), 1) == 0)
    onto = dot_nt(first, onehot(inside))
    upper = onehot(iota((blocks, blocks), 0) < iota((blocks, blocks), 1))
    rank = dot(onto.astype(BF16), upper)
    slot = (onto > 0.5) & (rank == iota((MOST, blocks), 0).astype(F32))
    chosen = onehot(slot)
    return slot, dot(chosen, row1).astype(I32) - 1, dot(chosen, column).astype(I32)


def gather_kernel(
    tiles,
    displacement_hbm,
    nodes_hbm,
    owner_hbm,
    picked_ref,
    info_ref,
    displacement,
    node_buffer,
    owner_buffer,
    semaphores,
):
    me = lax.axis_index("tile")
    copies = [
        pltpu.make_async_copy(source, target, semaphores.at[i])
        for i, (source, target) in enumerate(
            ((nodes_hbm, node_buffer), (owner_hbm, owner_buffer), (displacement_hbm, displacement))
        )
    ]
    for copy in copies:
        copy.start()
    copies[0].wait()
    copies[1].wait()
    components, rows, columns = displacement.shape
    blocks, width = node_buffer.shape
    block_count = blocks // tiles
    nodes = node_buffer[...]
    owner = owner_buffer[...]
    cells = rows * columns
    slot, slot_row, slot_column = slots_of(nodes, me, cells, columns)
    twin_slot, _, _ = slots_of(nodes, me ^ 1, cells, columns)
    target = jnp.concatenate([owner + (b * tiles + 1) for b in range(block_count)], axis=1)
    for i, chosen in enumerate((slot, twin_slot)):
        one = jnp.sum(jnp.where(chosen, target.astype(F32), 0.0), axis=1, keepdims=True).astype(I32) - 1
        info_ref[i * MOST : (i + 1) * MOST, :] = jnp.broadcast_to(one, (MOST, width))
    info_ref[2 * MOST :, :] = jnp.zeros((MOST, width), I32)
    first = onehot(iota((MOST, width), 1) == 0)
    tile_of = jnp.floor(((nodes >> 13).astype(F32) + 0.5) * (1.0 / (cells >> 13)))
    tile_row = dot_nt(first, tile_of.astype(BF16))[0:1, :]
    for b in range(block_count):
        own = jnp.where(owner == me, tile_row[:, b * tiles : (b + 1) * tiles], 0.0)
        info_ref[2 * MOST + b : 2 * MOST + b + 1, :] = jnp.broadcast_to(
            jnp.sum(own, axis=1, keepdims=True).astype(I32), (1, width)
        )
    copies[2].wait()
    field = displacement[...].reshape(components * rows, columns).astype(BF16)
    empty = jnp.zeros((8 - components, width), F32)
    for pair in range(MOST // 2):
        at_column = jnp.concatenate(
            [
                onehot(iota((columns, width), 0) == slot_column[s : s + 1, :])
                for s in (2 * pair, 2 * pair + 1)
            ],
            axis=1,
        )
        taken = dot(field, at_column)
        for i in range(2):
            s = 2 * pair + i
            at_row = iota((rows, width), 0) == slot_row[s : s + 1, :]
            found = []
            for r in range(components):
                k = component(r)
                one = taken[k * rows : (k + 1) * rows, i * width : (i + 1) * width]
                found.append(jnp.sum(jnp.where(at_row, one, 0.0), axis=0, keepdims=True))
            picked_ref[s] = jnp.concatenate(found + [empty], axis=0).astype(BF16)


def component(row):
    return (row & 1) * 3 + (row >> 1)


def payload_rows(targets, row, tiles, core):
    owner = targets & (tiles - 1)
    block = targets >> (tiles.bit_length() - 1)
    code = (owner >> 1) * 18 + block * 2 + (row >> 1) * 6 + (row & 1)
    return jnp.where((targets >= 0) & ((owner & 1) == core) & (row < 6), code, -1)


def place_kernel(tiles, picked_ref, twin_ref, info_ref, payload_ref):
    core = lax.axis_index("tile") & 1
    rows, width = payload_ref.shape
    lane = iota((2 * MOST, width), 1)
    code = payload_rows(info_ref[0 : 2 * MOST, :], lane & 7, tiles, core)
    code = jnp.sum(jnp.where((lane >> 3) == iota((2 * MOST, width), 0), code, 0), axis=0, keepdims=True)
    place = onehot(iota((rows, width), 0) == code)
    picked = jnp.concatenate([picked_ref[...].reshape(MOST * 8, width), twin_ref[...].reshape(MOST * 8, width)], axis=0)
    payload_ref[...] = dot(place, picked).astype(BF16)


def pile_kernel(arrived_ref, imag_ref, more_ref, block_hbm, info_ref, order_ref, payload_ref, real_ref, semaphores):
    rows, width = payload_ref.shape
    _, pieces, _, _ = arrived_ref.shape
    order = imag_ref.shape[0]
    ahead = more_ref.shape[0]
    ends = (ahead, 640, order)
    copies = []
    for i, (start, stop) in enumerate(zip(ends, ends[1:])):
        copies.append(pltpu.make_async_copy(block_hbm.at[0, start:stop], real_ref.at[start:stop], semaphores.at[i]))
        copies[i].start()
    vector = jnp.sum(arrived_ref[...].astype(F32), axis=0)
    vector = jnp.concatenate([vector[k] for k in range(pieces)], axis=1).astype(BF16)
    by_imag = dot_nt(vector, imag_ref[...])
    by_real = [dot_nt(vector, more_ref[...])]
    for i, (start, stop) in enumerate(zip(ends, ends[1:])):
        copies[i].wait()
        by_real.append(dot_nt(vector, real_ref[start:stop, :]))
    by_real = jnp.concatenate(by_real, axis=1)
    real = by_real[0:1] - by_imag[1:2]
    imag = by_real[1:2] + by_imag[0:1]
    traction = [part[:, k * width : (k + 1) * width] for k in range(pieces) for part in (real, imag)]
    traction = jnp.concatenate(traction + [jnp.zeros((width - 2 * pieces, width), F32)], axis=0).astype(BF16)
    lane = iota((1, width), 1)
    block = (lane >> 1) % 3
    chip = info_ref[2 * MOST : 2 * MOST + 1, :] >> 1
    for b in (1, 2):
        chip = jnp.where(block == b, info_ref[2 * MOST + b : 2 * MOST + b + 1, :] >> 1, chip)
    code = jnp.where(lane < 2 * pieces, chip * (2 * pieces) + lane, -1)
    place = onehot(iota((rows, width), 0) == code)
    payload_ref[...] = dot(place, traction).astype(BF16)


def choose_kernel(tiles, landed_ref, info_ref, order_ref, own_ref, twin_ref):
    core = lax.axis_index("tile") & 1
    slab, width = landed_ref.shape
    count = 2 * MOST
    shape = (count, 8, slab)
    targets = info_ref[0:count, 0:1].reshape(count, 1, 1)
    code = payload_rows(targets, iota((count, 8, 1), 1), tiles, core)
    take = onehot(iota(shape, 2) == code).reshape(count * 8, slab)
    chosen = dot(take, landed_ref[...]).astype(BF16).reshape(2, MOST, 8, width)
    own_ref[...] = chosen[0]
    twin_ref[...] = chosen[1]


def scatter_kernel(soil_ref, own_ref, twin_ref, row_ref, at_column_ref, result_ref, spread):
    components, rows, columns = soil_ref.shape
    width = row_ref.shape[1]
    for s in range(MOST):
        piece = own_ref[s].astype(F32) + twin_ref[s].astype(F32)
        at_row = iota((rows, width), 0) == row_ref[s : s + 1, :]
        for r in range(components):
            k = component(r)
            spread[k * rows : (k + 1) * rows, s * width : (s + 1) * width] = jnp.where(
                at_row, piece[r : r + 1, :], 0.0
            ).astype(BF16)
    added = dot_nt(spread[...], at_column_ref[...])
    result_ref[...] = soil_ref[...] + added.reshape(components, rows, columns)


def ahead_kernel(
    order_ref,
    displacement_hbm,
    scale_hbm,
    kind_hbm,
    block_hbm,
    near_hbm,
    far_hbm,
    imag_ref,
    more_ref,
    near,
    far,
    kind,
    semaphores,
):
    planes = scale_hbm.shape[0]
    odd = lax.axis_index("tile") & 1
    sides = ((near, near_hbm, (1 - odd) * (planes - 1)), (far, far_hbm, odd * (planes - 1)))
    pairs = [(kind_hbm, kind)]
    for plane, _, x in sides:
        pairs += [(displacement_hbm.at[:, x], plane.at[0:6]), (scale_hbm.at[x], plane.at[6])]
    pairs += [(block_hbm.at[1], imag_ref), (block_hbm.at[0, 0 : more_ref.shape[0]], more_ref)]
    copies = [pltpu.make_async_copy(*pair, semaphores.at[i]) for i, pair in enumerate(pairs)]
    for copy in copies:
        copy.start()
    copies[0].wait()
    for plane, _, x in sides:
        plane[7] = kind[x].astype(F32)
    for i, (plane, target, _) in enumerate(sides):
        copies[2 * i + 1].wait()
        copies[2 * i + 2].wait()
        copies.append(pltpu.make_async_copy(plane, target, semaphores.at[7 + i]))
        copies[-1].start()
    for copy in copies[5:]:
        copy.wait()


def token_kernel(order_ref, token_ref):
    token_ref[...] = jnp.zeros(token_ref.shape, F32)


def lookup(table_ref, row, kind):
    bits = [(kind & (1 << k)) != 0 for k in range(4)]
    level = [table_ref[row, k] for k in range(16)]
    for bit in bits:
        level = [jnp.where(bit, level[2 * k + 1], level[2 * k]) for k in range(len(level) // 2)]
    return level[0]


def half_stiffness(table_ref, kind, scale):
    return [0.5 * (lookup(table_ref, i, kind) * scale) for i in range(2)]


def flux(face, near, far):
    strain = [near[k] - far[k] for k in range(6)]
    real = [face[0] * strain[c] - face[1] * strain[3 + c] for c in range(3)]
    imag = [face[0] * strain[3 + c] + face[1] * strain[c] for c in range(3)]
    return real + imag


def soil_kernel(
    tiles,
    order_ref,
    displacement_hbm,
    scale_hbm,
    kind_hbm,
    near_hbm,
    far_hbm,
    nodes_hbm,
    stiff_ref,
    mass_ref,
    soil_ref,
    row_ref,
    at_column_ref,
    displacement_ref,
    scale_ref,
    kind_ref,
    near_ref,
    far_ref,
    node_buffer,
    semaphores,
):
    sources = (nodes_hbm, kind_hbm, scale_hbm, displacement_hbm, near_hbm, far_hbm)
    targets = (node_buffer, kind_ref, scale_ref, displacement_ref, near_ref, far_ref)
    copies = [pltpu.make_async_copy(*two, semaphores.at[i]) for i, two in enumerate(zip(sources, targets))]
    for copy in copies:
        copy.start()
    _, planes, ny, nz = displacement_ref.shape
    shape = (ny, nz)
    tile = lax.axis_index("tile")
    odd = tile & 1
    even = odd == 0
    copies[0].wait()
    width = node_buffer.shape[1]
    _, row_ref[...], slot_column = slots_of(node_buffer[...], tile, planes * ny * nz, nz)
    for s in range(MOST):
        at_column = onehot(iota((nz, width), 0) == slot_column[s : s + 1, :])
        at_column_ref[:, s * width : (s + 1) * width] = at_column
    for copy in copies[1:]:
        copy.wait()

    @pl.when((tile == 0) | (tile == tiles - 1))
    def _():
        far_ref[...] = jnp.zeros(far_ref.shape, F32)

    at_y, at_z = iota(shape, 0), iota(shape, 1)
    y_last, z_last = at_y == ny - 1, at_z == nz - 1
    edges = (
        jnp.where(at_y == 0, 0.5, 0.0)
        + jnp.where(y_last, 0.5, 0.0)
        + jnp.where(at_z == 0, 0.5, 0.0)
        + jnp.where(z_last, 0.5, 0.0)
    )
    half = [half_stiffness(stiff_ref, kind_ref[x], scale_ref[x]) for x in range(planes)]
    fields = [[displacement_ref[k, x] for k in range(6)] for x in range(planes)]

    def outside(first, second, flag):
        return [jnp.where(flag, first[k], second[k]) for k in range(6)], [
            jnp.where(flag, a, b)
            for a, b in zip(*(half_stiffness(stiff_ref, ref[7].astype(I32), ref[6]) for ref in (first, second)))
        ]

    before, before_half = outside(far_ref, near_ref, even)
    after, after_half = outside(near_ref, far_ref, even)
    fields = [before] + fields + [after]
    half = [before_half] + half + [after_half]

    def x_flux(x):
        return flux([half[x][i] + half[x + 1][i] for i in range(2)], fields[x], fields[x + 1])

    before = x_flux(0)
    for x in range(planes):
        u, own = fields[x + 1], half[x + 1]
        diagonal = [lookup(mass_ref, i, kind_ref[x]) + 2.0 * edges * own[i] for i in range(2)]
        total = [diagonal[0] * u[c] - diagonal[1] * u[3 + c] for c in range(3)]
        total += [diagonal[0] * u[3 + c] + diagonal[1] * u[c] for c in range(3)]
        beyond = x_flux(x + 1)
        total = [total[k] + beyond[k] - before[k] for k in range(6)]
        before = beyond
        for axis, last in ((0, y_last), (1, z_last)):
            size = shape[axis]
            face = [jnp.where(last, 0.0, own[i] + pltpu.roll(own[i], size - 1, axis)) for i in range(2)]
            next_to = [pltpu.roll(u[k], size - 1, axis) for k in range(6)]
            along = flux(face, u, next_to)
            total = [total[k] + along[k] - pltpu.roll(along[k], 1, axis) for k in range(6)]
        for k in range(6):
            soil_ref[k, x] = total[k]


def per_device(
    displacement,
    cell_scale,
    material_id,
    stiff_table,
    mass_table,
    pile_block,
    pile_owner,
    node_index,
):
    planes, ny, nz = cell_scale.shape
    rows = planes * ny
    tiles = lax.axis_size("tile")
    chips = tiles // 2
    _, block_count, width = node_index.shape
    blocks = tiles * block_count
    vmem = pl.BlockSpec(memory_space=pltpu.VMEM)
    smem = pl.BlockSpec(memory_space=pltpu.SMEM)
    hbm = pl.BlockSpec(memory_space=pltpu.HBM)
    anywhere = pl.BlockSpec(memory_space=pl.ANY)
    dma = pltpu.SemaphoreType.DMA

    def call(kernel, name, out_shape, in_specs, scratch=(), flops=10**8, moved=10**6):
        return pl.pallas_call(
            kernel,
            out_shape=out_shape,
            in_specs=in_specs,
            out_specs=jax.tree.map(lambda _: vmem, out_shape),
            scratch_shapes=list(scratch),
            compiler_params=pltpu.CompilerParams(vmem_limit_bytes=16 * 1024 * 1024),
            cost_estimate=pl.CostEstimate(flops=flops, bytes_accessed=moved, transcendentals=0),
            name=name,
        )

    def in_hbm(array):
        return pltpu.with_memory_space_constraint(array, pltpu.HBM)

    def shape(dims, kind):
        return jax.ShapeDtypeStruct(dims, kind)

    field = displacement.reshape(6, planes, ny, nz)
    nodes = node_index.transpose(1, 0, 2).reshape(blocks, width)
    owner = pile_owner.reshape(1, tiles)
    slab = (chips * 18, width)
    cut = (chips, 9, 2, width)
    pair = [(i, i ^ 1) for i in range(tiles)]
    groups = [[2 * chip + core for chip in range(chips)] for core in range(2)]

    size = (8, ny, nz)

    def exchange(payload):
        return lax.all_to_all(payload.reshape(cut), "tile", 0, 0, axis_index_groups=groups, tiled=True)

    picked, info = call(
        functools.partial(gather_kernel, tiles),
        "gather",
        (
            shape((MOST, 8, width), BF16),
            shape((3 * MOST, width), I32),
        ),
        [hbm] * 3,
        [
            pltpu.VMEM((6, rows, nz), F32),
            pltpu.VMEM((blocks, width), I32),
            pltpu.VMEM((1, tiles), I32),
            dma((3,)),
        ],
    )(in_hbm(displacement.reshape(6, rows, nz)), in_hbm(nodes), in_hbm(owner))
    payload = call(functools.partial(place_kernel, tiles), "place", shape(slab, BF16), [vmem] * 3)(
        picked, lax.ppermute(picked, "tile", pair), info
    )
    arrived = exchange(payload)

    order = pile_block.shape[-1]
    block = in_hbm(pile_block.reshape(2, order, order))
    square = (order, order)
    some = (256, order)
    to_near, to_far, imag, more = pl.pallas_call(
        ahead_kernel,
        out_shape=(shape(size, F32), shape(size, F32), shape(square, BF16), shape(some, BF16)),
        in_specs=[anywhere] + [hbm] * 4,
        out_specs=(hbm, hbm, vmem, vmem),
        scratch_shapes=[pltpu.VMEM(size, F32), pltpu.VMEM(size, F32), pltpu.VMEM(material_id.shape, I32), dma((9,))],
        compiler_params=pltpu.CompilerParams(vmem_limit_bytes=16 * 1024 * 1024),
        cost_estimate=pl.CostEstimate(flops=10**8, bytes_accessed=10**6, transcendentals=0),
        name="ahead",
    )(payload, *map(in_hbm, (field, cell_scale, material_id)), block)
    near = lax.ppermute(to_near, "tile", pair)
    next_chip = [(i, (i + 1) % tiles) for i in range(1, tiles, 2)]
    far = lax.ppermute(to_far, "tile", next_chip + [(j, i) for i, j in next_chip])
    token = call(token_kernel, "token", shape((8, width), F32), [anywhere], flops=10**11)(to_far)
    returning = call(
        pile_kernel,
        "pile",
        shape(slab, BF16),
        [vmem, vmem, vmem, hbm, vmem, anywhere],
        [pltpu.VMEM(square, BF16), dma((2,))],
    )(arrived, imag, more, block, info, token)
    landed = exchange(returning)
    soil, slot_row, at_column = call(
        functools.partial(soil_kernel, tiles),
        "soil",
        (shape(field.shape, F32), shape((MOST, width), I32), shape((nz, MOST * width), BF16)),
        [anywhere] + [hbm] * 6 + [smem] * 2,
        [
            pltpu.VMEM(field.shape, F32),
            pltpu.VMEM(cell_scale.shape, F32),
            pltpu.VMEM(cell_scale.shape, I32),
            pltpu.VMEM(size, F32),
            pltpu.VMEM(size, F32),
            pltpu.VMEM((blocks, width), I32),
            dma((6,)),
        ],
        flops=10**11,
        moved=10**7,
    )(returning, *map(in_hbm, (field, cell_scale, material_id, near, far, nodes)), stiff_table, mass_table)
    slots = shape((MOST, 8, width), BF16)
    own, twin = call(functools.partial(choose_kernel, tiles), "choose", (slots, slots), [vmem] * 2 + [anywhere])(
        landed.reshape(slab), info, soil
    )
    twin = lax.ppermute(twin, "tile", pair)
    result = call(
        scatter_kernel,
        "scatter",
        shape((6, rows, nz), F32),
        [vmem] * 5,
        [pltpu.VMEM((6 * rows, MOST * width), BF16)],
    )(soil.reshape(6, rows, nz), own, twin, slot_row, at_column)
    return result.reshape(displacement.shape)


def solution(mesh):
    placed = (
        P(None, None, ("freq", "tile"), None, None),
        P("tile", None, None),
        P("tile", None, None),
        P(None, "freq"),
        P(None, "freq"),
        P(("freq", "tile"), None, None, None),
        P("freq"),
        P(),
    )
    return jax.shard_map(
        per_device,
        mesh=mesh,
        in_specs=placed,
        out_specs=P(None, None, ("freq", "tile"), None, None),
        check_vma=False,
    )
```

time: 50.7 us -> 49 us (0.966)
  waiting for transfers between devices: 7.74 us -> 12.6 us
  starting transfers between devices: 25.6 us -> 22.3 us
  Pallas kernels: 16.8 us -> 13.7 us
    all_to_all x2, waiting for transfers between devices: 6.82 us -> 10.9 us  [exchange(): lax.all_to_all(payload.reshape(cut), 'tile', 0, 0, axis_index_groups=grou...]
    ppermute x1, starting transfers between devices: 4.92 us -> 1.5 us  [per_device(): lax.ppermute(to_far, 'tile', next_chip + [(j, i) for i, j in next_chip])]
    pallas_call x6 -> x4, Pallas kernels: 12 us -> 9 us  [the longest x1 3.35 us: per_device(): call(functools.partial(soil_kernel, tiles), 'soil', (shape(field.shape, F...]
    ppermute x1, waiting for transfers between devices: 0.08 us -> 0.84 us  [per_device(): twin = lax.ppermute(twin, 'tile', pair)]
where the time goes in v3:
time: 49 us; the launch traced here: 48.7 us
  starting transfers between devices  22.3 us (46%)
  Pallas kernels  13.7 us (28%)
  waiting for transfers between devices  12.6 us (26%)
    all_to_all x2, starting transfers between devices, exchange(): lax.all_to_all(payload.reshape(cut), 'tile', 0, 0, axis_index_groups=grou...  13.5 us
    all_to_all x2, waiting for transfers between devices, exchange(): lax.all_to_all(payload.reshape(cut), 'tile', 0, 0, axis_index_groups=grou...  10.9 us
    pallas_call x1, Pallas kernels, per_device(): call(functools.partial(soil_kernel, tiles), 'soil', (shape(field.shape, F...  3.35 us
    ppermute x1, starting transfers between devices, per_device(): lax.ppermute(picked, 'tile', pair)  3.33 us
    ppermute x1, starting transfers between devices, per_device(): twin = lax.ppermute(twin, 'tile', pair)  3.25 us
    pallas_call x1, Pallas kernels, per_device(): call(pile_kernel, 'pile', shape(slab, BF16), [vmem, vmem, vmem, hbm, vmem...  3.14 us
    pallas_call x1, Pallas kernels, per_device(): pl.pallas_call(ahead_kernel, out_shape=(shape(size, F32), shape(size, F32...  2.51 us
    pallas_call x1, Pallas kernels, per_device(): call(functools.partial(gather_kernel, tiles), 'gather', (shape((MOST, 8,...  2.23 us
  transfers between devices with their start and end apart: 6, of which 4 were waited for; matrix products, arithmetic and copies ran while one was open for 0% of the time, Pallas kernels for 18%

profile of v3, /device:TPU:1, one launch (start us, length us, event | category | flops | bytes accessed | tf_op | source)
XLA Modules:
  0.0 48.7 jit_solution(5797889371385561158)
XLA Ops:
  0.0 2.2 %gather.1 = (bf16[8,8,128]{2,1,0:T(8,128)(2,1)S(1)}, s32[24,128]{1,0:T(8,128)S(1)}) custom-call(f32[6,96,256]{2,1,0:T(8,128)} %bitcast.16, s32[192,128]{1,0:T(8,128)} %bitcast.19, s32[1,64]{1,0:T(1,128)} %bitcast.21), custom_call_target="tpu_custom_call" | custom-call | flops 100000000 | bytes 1000000 | tf_op jit(solution)/shard_map/gather/pallas_call | solution.py:400
  2.2 3.3 %collective-permute-start = (bf16[8,8,128]{2,1,0:T(8,128)(2,1)S(1)}, bf16[8,8,128]{2,1,0:T(8,128)(2,1)S(1)}, u32[]{:S(2)}, u32[]{:S(2)}) collective-permute-start(bf16[8,8,128]{2,1,0:T(8,128)(2,1)S(1)} %get-tuple-element.16.picked_ref), channel_id=1, source_target_pairs={{0,4},{4,0},{8,12},{12,8},{16,20},{20,16},{24,28},{28,24},{32,36},... | collective-permute-start | bytes 49160 | tf_op jit(solution)/shard_map/ppermute | solution.py:416
  5.6 0.8 %collective-permute-done.twin_ref = bf16[8,8,128]{2,1,0:T(8,128)(2,1)S(1)} collective-permute-done((bf16[8,8,128]{2,1,0:T(8,128)(2,1)S(1)}, bf16[8,8,128]{2,1,0:T(8,128)(2,1)S(1)}, u32[]{:S(2)}, u32[]{:S(2)}) %collective-permute-start) | collective-permute-done | bytes 16416 | tf_op jit(solution)/shard_map/ppermute | solution.py:416
  6.4 0.9 %place.1.order_ref = bf16[576,128]{1,0:T(8,128)(2,1)} custom-call(bf16[8,8,128]{2,1,0:T(8,128)(2,1)S(1)} %get-tuple-element.16.picked_ref, bf16[8,8,128]{2,1,0:T(8,128)(2,1)S(1)} %collective-permute-done.twin_ref, s32[24,128]{1,0:T(8,128)S(1)} %get-tuple-element.17.info_ref), custom_call_target="tpu_custom_call" | custom-call | flops 100000000 | bytes 1000000 | tf_op jit(solution)/shard_map/place/pallas_call | solution.py:415
  7.3 9.5 %all-to-all-start = ((bf16[32,9,2,128]{3,2,1,0:T(2,128)(2,1)}), bf16[32,9,2,128]{3,2,1,0:T(2,128)(2,1)S(1)}, u32[]{:S(2)}, u32[]{:S(2)}) async-start(bf16[32,9,2,128]{3,2,1,0:T(2,128)(2,1)} %bitcast.4), calls=%async_computation | async-start | bytes 294912 | tf_op jit(solution)/shard_map/all_to_all | solution.py:398
  16.7 2.5 %ahead.1 = (f32[8,48,256]{2,1,0:T(8,128)}, f32[8,48,256]{2,1,0:T(8,128)}, bf16[1152,1152]{1,0:T(8,128)(2,1)S(1)}, bf16[256,1152]{1,0:T(8,128)(2,1)S(1)}) custom-call(bf16[576,128]{1,0:T(8,128)(2,1)} %place.1.order_ref, f32[6,2,48,256]{3,2,1,0:T(8,128)} %bitcast.17, f32[2,48,256]{2,1,0:T(8,128)} %scale_hbm.3, s32[2,48,256]{2,1,0:T(8,128)} %kind_hbm.3, ...), custom_call_target="tpu_custom_call" | custom-call | flops 100000000 | bytes 1000000 | tf_op jit(solution)/shard_map/ahead/pallas_call | solution.py:424
  19.2 0.7 %collective-permute-start.1 = (f32[8,48,256]{2,1,0:T(8,128)}, f32[8,48,256]{2,1,0:T(8,128)}, u32[]{:S(2)}, u32[]{:S(2)}) collective-permute-start(f32[8,48,256]{2,1,0:T(8,128)} %get-tuple-element.21), channel_id=1, source_target_pairs={{0,4},{4,0},{8,12},{12,8},{16,20},{20,16},{24,28},{28,24},{32,36},... | collective-permute-start | bytes 1179656 | tf_op jit(solution)/shard_map/ppermute | solution.py:434
  20.0 1.5 %collective-permute-start.2 = (f32[8,48,256]{2,1,0:T(8,128)}, f32[8,48,256]{2,1,0:T(8,128)}, u32[]{:S(2)}, u32[]{:S(2)}) collective-permute-start(f32[8,48,256]{2,1,0:T(8,128)} %get-tuple-element.20.order_ref), channel_id=1, source_target_pairs={{4,8},{12,16},{20,24},{28,32},{36,40},{44,48},{52,56},{60,64},{68,... | collective-permute-start | bytes 1179656 | tf_op jit(solution)/shard_map/ppermute | solution.py:436
  21.5 0.0 copy-start
  21.5 0.0 copy-start.1
  21.5 4.8 %all-to-all-done.arrived_ref = bf16[32,9,2,128]{3,2,1,0:T(2,128)(2,1)S(1)} async-done(((bf16[32,9,2,128]{3,2,1,0:T(2,128)(2,1)}), bf16[32,9,2,128]{3,2,1,0:T(2,128)(2,1)S(1)}, u32[]{:S(2)}, u32[]{:S(2)}) %all-to-all-start) | async-done | bytes 147488 | tf_op jit(solution)/shard_map/all_to_all | solution.py:398
  26.3 3.1 %pile.1.order_ref = bf16[576,128]{1,0:T(8,128)(2,1)} custom-call(bf16[32,9,2,128]{3,2,1,0:T(2,128)(2,1)S(1)} %all-to-all-done.arrived_ref, bf16[1152,1152]{1,0:T(8,128)(2,1)S(1)} %get-tuple-element.18.imag_ref, bf16[256,1152]{1,0:T(8,128)(2,1)S(1)} %get-tuple-element.19.more_ref, bf16[2,1152,1152]{2,1,0:T(8,128)(2,1)} %bitcast.15, ...), custom_call_target="tpu_custom_call" | custom-call | flops 100000000 | bytes 1000000 | tf_op jit(solution)/shard_map/pile/pallas_call | solution.py:438
  29.4 4.1 %all-to-all-start.1 = ((bf16[32,9,2,128]{3,2,1,0:T(2,128)(2,1)}), bf16[32,9,2,128]{3,2,1,0:T(2,128)(2,1)S(1)}, u32[]{:S(2)}, u32[]{:S(2)}) async-start(bf16[32,9,2,128]{3,2,1,0:T(2,128)(2,1)} %bitcast.8), calls=%async_computation.1 | async-start | bytes 294912 | tf_op jit(solution)/shard_map/all_to_all | solution.py:398
  33.5 0.0 collective-permute-done.1.near_hbm
  33.5 0.0 collective-permute-done.2.far_hbm
  33.6 0.0 copy-done
  33.6 0.0 copy-done.1
  33.6 3.4 %soil.1 = (f32[6,2,48,256]{3,2,1,0:T(8,128)S(1)}, s32[8,128]{1,0:T(8,128)S(1)}, bf16[256,1024]{1,0:T(8,128)(2,1)S(1)}) custom-call(bf16[576,128]{1,0:T(8,128)(2,1)} %pile.1.order_ref, f32[6,2,48,256]{3,2,1,0:T(8,128)} %bitcast.18, f32[2,48,256]{2,1,0:T(8,128)} %scale_hbm.3, s32[2,48,256]{2,1,0:T(8,128)} %kind_hbm.3, ...), custom_call_target="tpu_custom_call" | custom-call | flops 99999997952 | bytes 10000000 | tf_op jit(solution)/shard_map/soil/pallas_call | solution.py:446
  36.9 6.1 %all-to-all-done.1 = bf16[32,9,2,128]{3,2,1,0:T(2,128)(2,1)S(1)} async-done(((bf16[32,9,2,128]{3,2,1,0:T(2,128)(2,1)}), bf16[32,9,2,128]{3,2,1,0:T(2,128)(2,1)S(1)}, u32[]{:S(2)}, u32[]{:S(2)}) %all-to-all-start.1) | async-done | bytes 147488 | tf_op jit(solution)/shard_map/all_to_all | solution.py:398
  43.0 0.3 choose.1
  43.3 3.2 %collective-permute-start.3 = (bf16[8,8,128]{2,1,0:T(8,128)(2,1)S(1)}, bf16[8,8,128]{2,1,0:T(8,128)(2,1)S(1)}, u32[]{:S(2)}, u32[]{:S(2)}) collective-permute-start(bf16[8,8,128]{2,1,0:T(8,128)(2,1)S(1)} %get-tuple-element.24), channel_id=1, source_target_pairs={{0,4},{4,0},{8,12},{12,8},{16,20},{20,16},{24,28},{28,24},{32,36},... | collective-permute-start | bytes 49160 | tf_op jit(solution)/shard_map/ppermute | solution.py:467
  46.5 0.8 %collective-permute-done.3.twin_ref = bf16[8,8,128]{2,1,0:T(8,128)(2,1)S(1)} collective-permute-done((bf16[8,8,128]{2,1,0:T(8,128)(2,1)S(1)}, bf16[8,8,128]{2,1,0:T(8,128)(2,1)S(1)}, u32[]{:S(2)}, u32[]{:S(2)}) %collective-permute-start.3) | collective-permute-done | bytes 16416 | tf_op jit(solution)/shard_map/ppermute | solution.py:467
  47.4 1.4 %scatter.1 = f32[6,96,256]{2,1,0:T(8,128)} custom-call(f32[6,96,256]{2,1,0:T(8,128)S(1)} %bitcast.12, bf16[8,8,128]{2,1,0:T(8,128)(2,1)S(1)} %get-tuple-element.23.own_ref, bf16[8,8,128]{2,1,0:T(8,128)(2,1)S(1)} %collective-permute-done.3.twin_ref, s32[8,128]{1,0:T(8,128)S(1)} %get-tuple-element.25.row_ref, bf16[256,1024]{1,0:T(8,128)(2,1)S(1)} %get-tuple-element.26.at_column_ref), custom_call_target="tpu_custom_call" | custom-call | flops 100000000 | bytes 1000000 | tf_op jit(solution)/shard_map/scatter/pallas_call | solution.py:468
  (1 shorter events, 0.0 us)
Async XLA Ops:
  2.2 4.2 %collective-permute-start = (bf16[8,8,128]{2,1,0:T(8,128)(2,1)S(1)}, bf16[8,8,128]{2,1,0:T(8,128)(2,1)S(1)}, u32[]{:S(2)}, u32[]{:S(2)}) collective-permute-start(bf16[8,8,128]{2,1,0:T(8,128)(2,1)S(1)} %get-tuple-element.16.picked_ref), channel_id=1, source_target_pairs={{0,4},{4,0},{8,12},{12,8},{16,20},{20,16},{24,28},{28,24},{32,36},... | collective-permute-start | bytes 49160 | tf_op jit(solution)/shard_map/ppermute | solution.py:416
  7.3 19.0 %all-to-all-start = ((bf16[32,9,2,128]{3,2,1,0:T(2,128)(2,1)}), bf16[32,9,2,128]{3,2,1,0:T(2,128)(2,1)S(1)}, u32[]{:S(2)}, u32[]{:S(2)}) async-start(bf16[32,9,2,128]{3,2,1,0:T(2,128)(2,1)} %bitcast.4), calls=%async_computation | async-start | bytes 294912 | tf_op jit(solution)/shard_map/all_to_all | solution.py:398
  19.2 14.3 %collective-permute-start.1 = (f32[8,48,256]{2,1,0:T(8,128)}, f32[8,48,256]{2,1,0:T(8,128)}, u32[]{:S(2)}, u32[]{:S(2)}) collective-permute-start(f32[8,48,256]{2,1,0:T(8,128)} %get-tuple-element.21), channel_id=1, source_target_pairs={{0,4},{4,0},{8,12},{12,8},{16,20},{20,16},{24,28},{28,24},{32,36},... | collective-permute-start | bytes 1179656 | tf_op jit(solution)/shard_map/ppermute | solution.py:434
  20.0 13.6 %collective-permute-start.2 = (f32[8,48,256]{2,1,0:T(8,128)}, f32[8,48,256]{2,1,0:T(8,128)}, u32[]{:S(2)}, u32[]{:S(2)}) collective-permute-start(f32[8,48,256]{2,1,0:T(8,128)} %get-tuple-element.20.order_ref), channel_id=1, source_target_pairs={{4,8},{12,16},{20,24},{28,32},{36,40},{44,48},{52,56},{60,64},{68,... | collective-permute-start | bytes 1179656 | tf_op jit(solution)/shard_map/ppermute | solution.py:436
  21.5 12.1 %copy-start = (f32[2,16]{1,0:T(2,128)S(1)}, f32[2,16]{1,0:T(2,128)}, u32[]{:S(2)}) copy-start(f32[2,16]{1,0:T(2,128)} %stiff_ref.1) | copy-start | bytes 388
  21.5 12.1 %copy-start.1 = (f32[2,16]{1,0:T(2,128)S(1)}, f32[2,16]{1,0:T(2,128)}, u32[]{:S(2)}) copy-start(f32[2,16]{1,0:T(2,128)} %mass_ref.1) | copy-start | bytes 388
  29.4 13.6 %all-to-all-start.1 = ((bf16[32,9,2,128]{3,2,1,0:T(2,128)(2,1)}), bf16[32,9,2,128]{3,2,1,0:T(2,128)(2,1)S(1)}, u32[]{:S(2)}, u32[]{:S(2)}) async-start(bf16[32,9,2,128]{3,2,1,0:T(2,128)(2,1)} %bitcast.8), calls=%async_computation.1 | async-start | bytes 294912 | tf_op jit(solution)/shard_map/all_to_all | solution.py:398
  43.3 4.1 %collective-permute-start.3 = (bf16[8,8,128]{2,1,0:T(8,128)(2,1)S(1)}, bf16[8,8,128]{2,1,0:T(8,128)(2,1)S(1)}, u32[]{:S(2)}, u32[]{:S(2)}) collective-permute-start(bf16[8,8,128]{2,1,0:T(8,128)(2,1)S(1)} %get-tuple-element.24), channel_id=1, source_target_pairs={{0,4},{4,0},{8,12},{12,8},{16,20},{20,16},{24,28},{28,24},{32,36},... | collective-permute-start | bytes 49160 | tf_op jit(solution)/shard_map/ppermute | solution.py:467

commit v4 on v3

--- a/solution.py
+++ b/solution.py
@@ -52,7 +52,6 @@
     nodes_hbm,
     owner_hbm,
     picked_ref,
-    info_ref,
     displacement,
     node_buffer,
     owner_buffer,
@@ -76,23 +75,12 @@
     owner = owner_buffer[...]
     cells = rows * columns
     slot, slot_row, slot_column = slots_of(nodes, me, cells, columns)
-    twin_slot, _, _ = slots_of(nodes, me ^ 1, cells, columns)
     target = jnp.concatenate([owner + (b * tiles + 1) for b in range(block_count)], axis=1)
-    for i, chosen in enumerate((slot, twin_slot)):
-        one = jnp.sum(jnp.where(chosen, target.astype(F32), 0.0), axis=1, keepdims=True).astype(I32) - 1
-        info_ref[i * MOST : (i + 1) * MOST, :] = jnp.broadcast_to(one, (MOST, width))
-    info_ref[2 * MOST :, :] = jnp.zeros((MOST, width), I32)
-    first = onehot(iota((MOST, width), 1) == 0)
-    tile_of = jnp.floor(((nodes >> 13).astype(F32) + 0.5) * (1.0 / (cells >> 13)))
-    tile_row = dot_nt(first, tile_of.astype(BF16))[0:1, :]
-    for b in range(block_count):
-        own = jnp.where(owner == me, tile_row[:, b * tiles : (b + 1) * tiles], 0.0)
-        info_ref[2 * MOST + b : 2 * MOST + b + 1, :] = jnp.broadcast_to(
-            jnp.sum(own, axis=1, keepdims=True).astype(I32), (1, width)
-        )
+    target = jnp.sum(jnp.where(slot, target.astype(F32), 0.0), axis=1, keepdims=True)
+    target = jnp.broadcast_to(target, (MOST, width))
     copies[2].wait()
     field = displacement[...].reshape(components * rows, columns).astype(BF16)
-    empty = jnp.zeros((8 - components, width), F32)
+    empty = jnp.zeros((7 - components, width), F32)
     for pair in range(MOST // 2):
         at_column = jnp.concatenate(
             [
@@ -110,7 +98,7 @@
                 k = component(r)
                 one = taken[k * rows : (k + 1) * rows, i * width : (i + 1) * width]
                 found.append(jnp.sum(jnp.where(at_row, one, 0.0), axis=0, keepdims=True))
-            picked_ref[s] = jnp.concatenate(found + [empty], axis=0).astype(BF16)
+            picked_ref[s] = jnp.concatenate(found + [target[s : s + 1, :], empty], axis=0).astype(BF16)
 
 
 def component(row):
@@ -124,18 +112,21 @@
     return jnp.where((targets >= 0) & ((owner & 1) == core) & (row < 6), code, -1)
 
 
-def place_kernel(tiles, picked_ref, twin_ref, info_ref, payload_ref):
+def place_kernel(tiles, picked_ref, twin_ref, payload_ref, target_ref):
     core = lax.axis_index("tile") & 1
     rows, width = payload_ref.shape
+    picked = jnp.concatenate([picked_ref[...].reshape(MOST * 8, width), twin_ref[...].reshape(MOST * 8, width)], axis=0)
+    targets = jnp.concatenate([ref[s, 6:7, :].astype(F32) for ref in (picked_ref, twin_ref) for s in range(MOST)], axis=0)
+    targets = targets.astype(I32) - 1
+    target_ref[...] = targets
     lane = iota((2 * MOST, width), 1)
-    code = payload_rows(info_ref[0 : 2 * MOST, :], lane & 7, tiles, core)
+    code = payload_rows(targets, lane & 7, tiles, core)
     code = jnp.sum(jnp.where((lane >> 3) == iota((2 * MOST, width), 0), code, 0), axis=0, keepdims=True)
     place = onehot(iota((rows, width), 0) == code)
-    picked = jnp.concatenate([picked_ref[...].reshape(MOST * 8, width), twin_ref[...].reshape(MOST * 8, width)], axis=0)
     payload_ref[...] = dot(place, picked).astype(BF16)
 
 
-def pile_kernel(arrived_ref, imag_ref, more_ref, block_hbm, info_ref, order_ref, payload_ref, real_ref, semaphores):
+def pile_kernel(arrived_ref, imag_ref, more_ref, block_hbm, chip_ref, order_ref, payload_ref, real_ref, semaphores):
     rows, width = payload_ref.shape
     _, pieces, _, _ = arrived_ref.shape
     order = imag_ref.shape[0]
@@ -159,20 +150,20 @@
     traction = jnp.concatenate(traction + [jnp.zeros((width - 2 * pieces, width), F32)], axis=0).astype(BF16)
     lane = iota((1, width), 1)
     block = (lane >> 1) % 3
-    chip = info_ref[2 * MOST : 2 * MOST + 1, :] >> 1
+    chip = chip_ref[0:1, :]
     for b in (1, 2):
-        chip = jnp.where(block == b, info_ref[2 * MOST + b : 2 * MOST + b + 1, :] >> 1, chip)
+        chip = jnp.where(block == b, chip_ref[b : b + 1, :], chip)
     code = jnp.where(lane < 2 * pieces, chip * (2 * pieces) + lane, -1)
     place = onehot(iota((rows, width), 0) == code)
     payload_ref[...] = dot(place, traction).astype(BF16)
 
 
-def choose_kernel(tiles, landed_ref, info_ref, order_ref, own_ref, twin_ref):
+def choose_kernel(tiles, landed_ref, target_ref, order_ref, own_ref, twin_ref):
     core = lax.axis_index("tile") & 1
     slab, width = landed_ref.shape
     count = 2 * MOST
     shape = (count, 8, slab)
-    targets = info_ref[0:count, 0:1].reshape(count, 1, 1)
+    targets = target_ref[:, 0:1].reshape(count, 1, 1)
     code = payload_rows(targets, iota((count, 8, 1), 1), tiles, core)
     take = onehot(iota(shape, 2) == code).reshape(count * 8, slab)
     chosen = dot(take, landed_ref[...]).astype(BF16).reshape(2, MOST, 8, width)
@@ -180,19 +171,25 @@
     twin_ref[...] = chosen[1]
 
 
-def scatter_kernel(soil_ref, own_ref, twin_ref, row_ref, at_column_ref, result_ref, spread):
+def scatter_kernel(soil_ref, own_ref, twin_ref, at_row_ref, at_column_ref, result_hbm, result, semaphores):
     components, rows, columns = soil_ref.shape
-    width = row_ref.shape[1]
-    for s in range(MOST):
-        piece = own_ref[s].astype(F32) + twin_ref[s].astype(F32)
-        at_row = iota((rows, width), 0) == row_ref[s : s + 1, :]
-        for r in range(components):
-            k = component(r)
-            spread[k * rows : (k + 1) * rows, s * width : (s + 1) * width] = jnp.where(
-                at_row, piece[r : r + 1, :], 0.0
-            ).astype(BF16)
-    added = dot_nt(spread[...], at_column_ref[...])
-    result_ref[...] = soil_ref[...] + added.reshape(components, rows, columns)
+    pieces = [own_ref[s].astype(F32) + twin_ref[s].astype(F32) for s in range(MOST)]
+    pieces = jnp.concatenate(pieces, axis=1)
+    at_row = at_row_ref[...]
+    half = components // 2
+    copies = []
+    for i in range(2):
+        spread = []
+        for k in range(i * half, (i + 1) * half):
+            row = (k % half) * 2 + i
+            spread.append(jnp.broadcast_to(pieces[row : row + 1, :], at_row.shape).astype(BF16) * at_row)
+        added = dot_nt(jnp.concatenate(spread, axis=0), at_column_ref[...])
+        part = slice(i * half, (i + 1) * half)
+        result[part] = soil_ref[part] + added.reshape(half, rows, columns)
+        copies.append(pltpu.make_async_copy(result.at[part], result_hbm.at[part], semaphores.at[i]))
+        copies[i].start()
+    for copy in copies:
+        copy.wait()
 
 
 def ahead_kernel(
@@ -201,13 +198,18 @@
     scale_hbm,
     kind_hbm,
     block_hbm,
+    nodes_hbm,
+    owner_hbm,
     near_hbm,
     far_hbm,
     imag_ref,
     more_ref,
+    chip_ref,
     near,
     far,
     kind,
+    node_buffer,
+    owner_buffer,
     semaphores,
 ):
     planes = scale_hbm.shape[0]
@@ -217,18 +219,32 @@
     for plane, _, x in sides:
         pairs += [(displacement_hbm.at[:, x], plane.at[0:6]), (scale_hbm.at[x], plane.at[6])]
     pairs += [(block_hbm.at[1], imag_ref), (block_hbm.at[0, 0 : more_ref.shape[0]], more_ref)]
+    pairs += [(nodes_hbm, node_buffer), (owner_hbm, owner_buffer)]
     copies = [pltpu.make_async_copy(*pair, semaphores.at[i]) for i, pair in enumerate(pairs)]
     for copy in copies:
         copy.start()
     copies[0].wait()
     for plane, _, x in sides:
         plane[7] = kind[x].astype(F32)
+    sends = []
     for i, (plane, target, _) in enumerate(sides):
         copies[2 * i + 1].wait()
         copies[2 * i + 2].wait()
-        copies.append(pltpu.make_async_copy(plane, target, semaphores.at[7 + i]))
-        copies[-1].start()
-    for copy in copies[5:]:
+        sends.append(pltpu.make_async_copy(plane, target, semaphores.at[9 + i]))
+        sends[i].start()
+    copies[7].wait()
+    copies[8].wait()
+    blocks, width = node_buffer.shape
+    tiles = owner_buffer.shape[1]
+    cells = planes * displacement_hbm.shape[2] * displacement_hbm.shape[3]
+    first = onehot(iota((MOST, width), 1) == 0)
+    tile_of = jnp.floor(((node_buffer[...] >> 13).astype(F32) + 0.5) * (1.0 / (cells >> 13)))
+    tile_row = dot_nt(first, tile_of.astype(BF16))[0:1, :]
+    mine = owner_buffer[...] == lax.axis_index("tile")
+    for b in range(blocks // tiles):
+        own = jnp.sum(jnp.where(mine, tile_row[:, b * tiles : (b + 1) * tiles], 0.0), axis=1, keepdims=True)
+        chip_ref[b : b + 1, :] = jnp.broadcast_to(own.astype(I32) >> 1, (1, width))
+    for copy in copies[5:7] + sends:
         copy.wait()
 
 
@@ -267,7 +283,7 @@
     stiff_ref,
     mass_ref,
     soil_ref,
-    row_ref,
+    at_row_ref,
     at_column_ref,
     displacement_ref,
     scale_ref,
@@ -289,10 +305,11 @@
     even = odd == 0
     copies[0].wait()
     width = node_buffer.shape[1]
-    _, row_ref[...], slot_column = slots_of(node_buffer[...], tile, planes * ny * nz, nz)
+    _, slot_row, slot_column = slots_of(node_buffer[...], tile, planes * ny * nz, nz)
     for s in range(MOST):
-        at_column = onehot(iota((nz, width), 0) == slot_column[s : s + 1, :])
-        at_column_ref[:, s * width : (s + 1) * width] = at_column
+        lanes = slice(s * width, (s + 1) * width)
+        at_row_ref[:, lanes] = onehot(iota((planes * ny, width), 0) == slot_row[s : s + 1, :])
+        at_column_ref[:, lanes] = onehot(iota((nz, width), 0) == slot_column[s : s + 1, :])
     for copy in copies[1:]:
         copy.wait()
 
@@ -397,13 +414,10 @@
     def exchange(payload):
         return lax.all_to_all(payload.reshape(cut), "tile", 0, 0, axis_index_groups=groups, tiled=True)
 
-    picked, info = call(
+    picked = call(
         functools.partial(gather_kernel, tiles),
         "gather",
-        (
-            shape((MOST, 8, width), BF16),
-            shape((3 * MOST, width), I32),
-        ),
+        shape((MOST, 8, width), BF16),
         [hbm] * 3,
         [
             pltpu.VMEM((6, rows, nz), F32),
@@ -412,25 +426,35 @@
             dma((3,)),
         ],
     )(in_hbm(displacement.reshape(6, rows, nz)), in_hbm(nodes), in_hbm(owner))
-    payload = call(functools.partial(place_kernel, tiles), "place", shape(slab, BF16), [vmem] * 3)(
-        picked, lax.ppermute(picked, "tile", pair), info
-    )
+    payload, targets = call(
+        functools.partial(place_kernel, tiles),
+        "place",
+        (shape(slab, BF16), shape((2 * MOST, width), I32)),
+        [vmem] * 2,
+    )(picked, lax.ppermute(picked, "tile", pair))
     arrived = exchange(payload)
 
     order = pile_block.shape[-1]
     block = in_hbm(pile_block.reshape(2, order, order))
     square = (order, order)
     some = (256, order)
-    to_near, to_far, imag, more = pl.pallas_call(
+    to_near, to_far, imag, more, chip = pl.pallas_call(
         ahead_kernel,
-        out_shape=(shape(size, F32), shape(size, F32), shape(square, BF16), shape(some, BF16)),
-        in_specs=[anywhere] + [hbm] * 4,
-        out_specs=(hbm, hbm, vmem, vmem),
-        scratch_shapes=[pltpu.VMEM(size, F32), pltpu.VMEM(size, F32), pltpu.VMEM(material_id.shape, I32), dma((9,))],
+        out_shape=(shape(size, F32), shape(size, F32), shape(square, BF16), shape(some, BF16), shape((MOST, width), I32)),
+        in_specs=[anywhere] + [hbm] * 6,
+        out_specs=(hbm, hbm, vmem, vmem, vmem),
+        scratch_shapes=[
+            pltpu.VMEM(size, F32),
+            pltpu.VMEM(size, F32),
+            pltpu.VMEM(material_id.shape, I32),
+            pltpu.VMEM((blocks, width), I32),
+            pltpu.VMEM((1, tiles), I32),
+            dma((11,)),
+        ],
         compiler_params=pltpu.CompilerParams(vmem_limit_bytes=16 * 1024 * 1024),
         cost_estimate=pl.CostEstimate(flops=10**8, bytes_accessed=10**6, transcendentals=0),
         name="ahead",
-    )(payload, *map(in_hbm, (field, cell_scale, material_id)), block)
+    )(payload, *map(in_hbm, (field, cell_scale, material_id)), block, in_hbm(nodes), in_hbm(owner))
     near = lax.ppermute(to_near, "tile", pair)
     next_chip = [(i, (i + 1) % tiles) for i in range(1, tiles, 2)]
     far = lax.ppermute(to_far, "tile", next_chip + [(j, i) for i, j in next_chip])
@@ -441,12 +465,12 @@
         shape(slab, BF16),
         [vmem, vmem, vmem, hbm, vmem, anywhere],
         [pltpu.VMEM(square, BF16), dma((2,))],
-    )(arrived, imag, more, block, info, token)
+    )(arrived, imag, more, block, chip, token)
     landed = exchange(returning)
-    soil, slot_row, at_column = call(
+    soil, at_row, at_column = call(
         functools.partial(soil_kernel, tiles),
         "soil",
-        (shape(field.shape, F32), shape((MOST, width), I32), shape((nz, MOST * width), BF16)),
+        (shape(field.shape, F32), shape((rows, MOST * width), BF16), shape((nz, MOST * width), BF16)),
         [anywhere] + [hbm] * 6 + [smem] * 2,
         [
             pltpu.VMEM(field.shape, F32),
@@ -462,16 +486,20 @@
     )(returning, *map(in_hbm, (field, cell_scale, material_id, near, far, nodes)), stiff_table, mass_table)
     slots = shape((MOST, 8, width), BF16)
     own, twin = call(functools.partial(choose_kernel, tiles), "choose", (slots, slots), [vmem] * 2 + [anywhere])(
-        landed.reshape(slab), info, soil
+        landed.reshape(slab), targets, soil
     )
     twin = lax.ppermute(twin, "tile", pair)
-    result = call(
+    sums = (6, rows, nz)
+    result = pl.pallas_call(
         scatter_kernel,
-        "scatter",
-        shape((6, rows, nz), F32),
-        [vmem] * 5,
-        [pltpu.VMEM((6 * rows, MOST * width), BF16)],
-    )(soil.reshape(6, rows, nz), own, twin, slot_row, at_column)
+        out_shape=shape(sums, F32),
+        in_specs=[vmem] * 5,
+        out_specs=hbm,
+        scratch_shapes=[pltpu.VMEM(sums, F32), dma((2,))],
+        compiler_params=pltpu.CompilerParams(vmem_limit_bytes=16 * 1024 * 1024),
+        cost_estimate=pl.CostEstimate(flops=10**8, bytes_accessed=10**6, transcendentals=0),
+        name="scatter",
+    )(soil.reshape(sums), own, twin, at_row, at_column)
     return result.reshape(displacement.shape)
 
 

time: 49 us -> 48.5 us (0.990)
  transfers between devices with their start and end apart: 6 -> 6, of which waited for: 4 -> 4; matrix products, arithmetic and copies ran while one was open for 0% -> 0% of each run, Pallas kernels for 18% -> 19%
where the time goes in v4:
time: 48.5 us; the launch traced here: 48.3 us
  starting transfers between devices  22.2 us (46%)
  Pallas kernels  13.7 us (28%)
  waiting for transfers between devices  12.2 us (25%)
    all_to_all x2, starting transfers between devices, exchange(): lax.all_to_all(payload.reshape(cut), 'tile', 0, 0, axis_index_groups=grou...  13.9 us
    all_to_all x2, waiting for transfers between devices, exchange(): lax.all_to_all(payload.reshape(cut), 'tile', 0, 0, axis_index_groups=grou...  10.5 us
    pallas_call x1, Pallas kernels, per_device(): call(functools.partial(soil_kernel, tiles), 'soil', (shape(field.shape, F...  3.41 us
    ppermute x1, starting transfers between devices, per_device(): lax.ppermute(picked, 'tile', pair)  3.33 us
    pallas_call x1, Pallas kernels, per_device(): call(pile_kernel, 'pile', shape(slab, BF16), [vmem, vmem, vmem, hbm, vmem...  3.14 us
    pallas_call x1, Pallas kernels, per_device(): pl.pallas_call(ahead_kernel, out_shape=(shape(size, F32), shape(size, F32...  2.85 us
    ppermute x1, starting transfers between devices, per_device(): twin = lax.ppermute(twin, 'tile', pair)  2.83 us
    pallas_call x1, Pallas kernels, per_device(): call(functools.partial(gather_kernel, tiles), 'gather', shape((MOST, 8, w...  1.86 us
  transfers between devices with their start and end apart: 6, of which 4 were waited for; matrix products, arithmetic and copies ran while one was open for 0% of the time, Pallas kernels for 19%

profile of v4, /device:TPU:1, one launch (start us, length us, event | category | flops | bytes accessed | tf_op | source)
XLA Modules:
  0.0 48.3 jit_solution(532772518609558511)
XLA Ops:
  0.0 1.9 %gather.1.picked_ref = bf16[8,8,128]{2,1,0:T(8,128)(2,1)S(1)} custom-call(f32[6,96,256]{2,1,0:T(8,128)} %bitcast.16, s32[192,128]{1,0:T(8,128)} %bitcast.19, s32[1,64]{1,0:T(1,128)} %bitcast.22), custom_call_target="tpu_custom_call" | custom-call | flops 100000000 | bytes 1000000 | tf_op jit(solution)/shard_map/gather/pallas_call | solution.py:417
  1.9 3.3 %collective-permute-start = (bf16[8,8,128]{2,1,0:T(8,128)(2,1)S(1)}, bf16[8,8,128]{2,1,0:T(8,128)(2,1)S(1)}, u32[]{:S(2)}, u32[]{:S(2)}) collective-permute-start(bf16[8,8,128]{2,1,0:T(8,128)(2,1)S(1)} %gather.1.picked_ref), channel_id=1, source_target_pairs={{0,4},{4,0},{8,12},{12,8},{16,20},{20,16},{24,28},{28,24},{32,36},... | collective-permute-start | bytes 49160 | tf_op jit(solution)/shard_map/ppermute | solution.py:434
  5.2 0.8 %collective-permute-done.twin_ref = bf16[8,8,128]{2,1,0:T(8,128)(2,1)S(1)} collective-permute-done((bf16[8,8,128]{2,1,0:T(8,128)(2,1)S(1)}, bf16[8,8,128]{2,1,0:T(8,128)(2,1)S(1)}, u32[]{:S(2)}, u32[]{:S(2)}) %collective-permute-start) | collective-permute-done | bytes 16416 | tf_op jit(solution)/shard_map/ppermute | solution.py:434
  6.0 0.9 %place.1 = (bf16[576,128]{1,0:T(8,128)(2,1)}, s32[16,128]{1,0:T(8,128)S(1)}) custom-call(bf16[8,8,128]{2,1,0:T(8,128)(2,1)S(1)} %gather.1.picked_ref, bf16[8,8,128]{2,1,0:T(8,128)(2,1)S(1)} %collective-permute-done.twin_ref), custom_call_target="tpu_custom_call" | custom-call | flops 100000000 | bytes 1000000 | tf_op jit(solution)/shard_map/place/pallas_call | solution.py:429
  6.9 9.5 %all-to-all-start = ((bf16[32,9,2,128]{3,2,1,0:T(2,128)(2,1)}), bf16[32,9,2,128]{3,2,1,0:T(2,128)(2,1)S(1)}, u32[]{:S(2)}, u32[]{:S(2)}) async-start(bf16[32,9,2,128]{3,2,1,0:T(2,128)(2,1)} %bitcast.4), calls=%async_computation | async-start | bytes 294912 | tf_op jit(solution)/shard_map/all_to_all | solution.py:415
  16.4 2.9 %ahead.1 = (f32[8,48,256]{2,1,0:T(8,128)}, f32[8,48,256]{2,1,0:T(8,128)}, bf16[1152,1152]{1,0:T(8,128)(2,1)S(1)}, bf16[256,1152]{1,0:T(8,128)(2,1)S(1)}, s32[8,128]{1,0:T(8,128)S(1)}) custom-call(bf16[576,128]{1,0:T(8,128)(2,1)} %get-tuple-element.17.order_ref, f32[6,2,48,256]{3,2,1,0:T(8,128)} %bitcast.17, f32[2,48,256]{2,1,0:T(8,128)} %scale_hbm.3, ...), custom_call_target="tpu_custom_call" | custom-call | flops 100000000 | bytes 1000000 | tf_op jit(solution)/shard_map/ahead/pallas_call | solution.py:441
  19.2 0.7 %collective-permute-start.1 = (f32[8,48,256]{2,1,0:T(8,128)}, f32[8,48,256]{2,1,0:T(8,128)}, u32[]{:S(2)}, u32[]{:S(2)}) collective-permute-start(f32[8,48,256]{2,1,0:T(8,128)} %get-tuple-element.22), channel_id=1, source_target_pairs={{0,4},{4,0},{8,12},{12,8},{16,20},{20,16},{24,28},{28,24},{32,36},... | collective-permute-start | bytes 1179656 | tf_op jit(solution)/shard_map/ppermute | solution.py:458
  20.0 1.5 %collective-permute-start.2 = (f32[8,48,256]{2,1,0:T(8,128)}, f32[8,48,256]{2,1,0:T(8,128)}, u32[]{:S(2)}, u32[]{:S(2)}) collective-permute-start(f32[8,48,256]{2,1,0:T(8,128)} %get-tuple-element.21.order_ref), channel_id=1, source_target_pairs={{4,8},{12,16},{20,24},{28,32},{36,40},{44,48},{52,56},{60,64},{68,... | collective-permute-start | bytes 1179656 | tf_op jit(solution)/shard_map/ppermute | solution.py:460
  21.4 0.0 copy-start
  21.5 0.0 copy-start.1
  21.5 4.5 %all-to-all-done.arrived_ref = bf16[32,9,2,128]{3,2,1,0:T(2,128)(2,1)S(1)} async-done(((bf16[32,9,2,128]{3,2,1,0:T(2,128)(2,1)}), bf16[32,9,2,128]{3,2,1,0:T(2,128)(2,1)S(1)}, u32[]{:S(2)}, u32[]{:S(2)}) %all-to-all-start) | async-done | bytes 147488 | tf_op jit(solution)/shard_map/all_to_all | solution.py:415
  25.9 3.1 %pile.1.order_ref = bf16[576,128]{1,0:T(8,128)(2,1)} custom-call(bf16[32,9,2,128]{3,2,1,0:T(2,128)(2,1)S(1)} %all-to-all-done.arrived_ref, bf16[1152,1152]{1,0:T(8,128)(2,1)S(1)} %get-tuple-element.18.imag_ref, bf16[256,1152]{1,0:T(8,128)(2,1)S(1)} %get-tuple-element.19.more_ref, bf16[2,1152,1152]{2,1,0:T(8,128)(2,1)} %bitcast.15, ...), custom_call_target="tpu_custom_call" | custom-call | flops 100000000 | bytes 1000000 | tf_op jit(solution)/shard_map/pile/pallas_call | solution.py:462
  29.1 4.4 %all-to-all-start.1 = ((bf16[32,9,2,128]{3,2,1,0:T(2,128)(2,1)}), bf16[32,9,2,128]{3,2,1,0:T(2,128)(2,1)S(1)}, u32[]{:S(2)}, u32[]{:S(2)}) async-start(bf16[32,9,2,128]{3,2,1,0:T(2,128)(2,1)} %bitcast.9), calls=%async_computation.1 | async-start | bytes 294912 | tf_op jit(solution)/shard_map/all_to_all | solution.py:415
  33.5 0.0 collective-permute-done.1.near_hbm
  33.5 0.0 collective-permute-done.2.far_hbm
  33.5 0.0 copy-done
  33.5 0.0 copy-done.1
  33.5 3.4 %soil.1 = (f32[6,2,48,256]{3,2,1,0:T(8,128)S(1)}, bf16[96,1024]{1,0:T(8,128)(2,1)S(1)}, bf16[256,1024]{1,0:T(8,128)(2,1)S(1)}) custom-call(bf16[576,128]{1,0:T(8,128)(2,1)} %pile.1.order_ref, f32[6,2,48,256]{3,2,1,0:T(8,128)} %bitcast.18, f32[2,48,256]{2,1,0:T(8,128)} %scale_hbm.3, s32[2,48,256]{2,1,0:T(8,128)} %kind_hbm.3, ...), custom_call_target="tpu_custom_call" | custom-call | flops 99999997952 | bytes 10000000 | tf_op jit(solution)/shard_map/soil/pallas_call | solution.py:470
  37.0 6.0 %all-to-all-done.1 = bf16[32,9,2,128]{3,2,1,0:T(2,128)(2,1)S(1)} async-done(((bf16[32,9,2,128]{3,2,1,0:T(2,128)(2,1)}), bf16[32,9,2,128]{3,2,1,0:T(2,128)(2,1)S(1)}, u32[]{:S(2)}, u32[]{:S(2)}) %all-to-all-start.1) | async-done | bytes 147488 | tf_op jit(solution)/shard_map/all_to_all | solution.py:415
  43.0 0.3 choose.1
  43.2 2.8 %collective-permute-start.3 = (bf16[8,8,128]{2,1,0:T(8,128)(2,1)S(1)}, bf16[8,8,128]{2,1,0:T(8,128)(2,1)S(1)}, u32[]{:S(2)}, u32[]{:S(2)}) collective-permute-start(bf16[8,8,128]{2,1,0:T(8,128)(2,1)S(1)} %get-tuple-element.26), channel_id=1, source_target_pairs={{0,4},{4,0},{8,12},{12,8},{16,20},{20,16},{24,28},{28,24},{32,36},... | collective-permute-start | bytes 49160 | tf_op jit(solution)/shard_map/ppermute | solution.py:491
  46.1 0.8 %collective-permute-done.3.twin_ref = bf16[8,8,128]{2,1,0:T(8,128)(2,1)S(1)} collective-permute-done((bf16[8,8,128]{2,1,0:T(8,128)(2,1)S(1)}, bf16[8,8,128]{2,1,0:T(8,128)(2,1)S(1)}, u32[]{:S(2)}, u32[]{:S(2)}) %collective-permute-start.3) | collective-permute-done | bytes 16416 | tf_op jit(solution)/shard_map/ppermute | solution.py:491
  46.9 1.3 %scatter.1 = f32[6,96,256]{2,1,0:T(8,128)} custom-call(f32[6,96,256]{2,1,0:T(8,128)S(1)} %bitcast.12, bf16[8,8,128]{2,1,0:T(8,128)(2,1)S(1)} %get-tuple-element.25.own_ref, bf16[8,8,128]{2,1,0:T(8,128)(2,1)S(1)} %collective-permute-done.3.twin_ref, bf16[96,1024]{1,0:T(8,128)(2,1)S(1)} %get-tuple-element.27.at_row_ref, ...), custom_call_target="tpu_custom_call" | custom-call | flops 100000000 | bytes 1000000 | tf_op jit(solution)/shard_map/scatter/pallas_call | solution.py:493
  (1 shorter events, 0.0 us)
Async XLA Ops:
  1.9 4.2 %collective-permute-start = (bf16[8,8,128]{2,1,0:T(8,128)(2,1)S(1)}, bf16[8,8,128]{2,1,0:T(8,128)(2,1)S(1)}, u32[]{:S(2)}, u32[]{:S(2)}) collective-permute-start(bf16[8,8,128]{2,1,0:T(8,128)(2,1)S(1)} %gather.1.picked_ref), channel_id=1, source_target_pairs={{0,4},{4,0},{8,12},{12,8},{16,20},{20,16},{24,28},{28,24},{32,36},... | collective-permute-start | bytes 49160 | tf_op jit(solution)/shard_map/ppermute | solution.py:434
  6.9 19.1 %all-to-all-start = ((bf16[32,9,2,128]{3,2,1,0:T(2,128)(2,1)}), bf16[32,9,2,128]{3,2,1,0:T(2,128)(2,1)S(1)}, u32[]{:S(2)}, u32[]{:S(2)}) async-start(bf16[32,9,2,128]{3,2,1,0:T(2,128)(2,1)} %bitcast.4), calls=%async_computation | async-start | bytes 294912 | tf_op jit(solution)/shard_map/all_to_all | solution.py:415
  19.2 14.3 %collective-permute-start.1 = (f32[8,48,256]{2,1,0:T(8,128)}, f32[8,48,256]{2,1,0:T(8,128)}, u32[]{:S(2)}, u32[]{:S(2)}) collective-permute-start(f32[8,48,256]{2,1,0:T(8,128)} %get-tuple-element.22), channel_id=1, source_target_pairs={{0,4},{4,0},{8,12},{12,8},{16,20},{20,16},{24,28},{28,24},{32,36},... | collective-permute-start | bytes 1179656 | tf_op jit(solution)/shard_map/ppermute | solution.py:458
  20.0 13.6 %collective-permute-start.2 = (f32[8,48,256]{2,1,0:T(8,128)}, f32[8,48,256]{2,1,0:T(8,128)}, u32[]{:S(2)}, u32[]{:S(2)}) collective-permute-start(f32[8,48,256]{2,1,0:T(8,128)} %get-tuple-element.21.order_ref), channel_id=1, source_target_pairs={{4,8},{12,16},{20,24},{28,32},{36,40},{44,48},{52,56},{60,64},{68,... | collective-permute-start | bytes 1179656 | tf_op jit(solution)/shard_map/ppermute | solution.py:460
  21.4 12.1 %copy-start = (f32[2,16]{1,0:T(2,128)S(1)}, f32[2,16]{1,0:T(2,128)}, u32[]{:S(2)}) copy-start(f32[2,16]{1,0:T(2,128)} %stiff_ref.1) | copy-start | bytes 388
  21.5 12.1 %copy-start.1 = (f32[2,16]{1,0:T(2,128)S(1)}, f32[2,16]{1,0:T(2,128)}, u32[]{:S(2)}) copy-start(f32[2,16]{1,0:T(2,128)} %mass_ref.1) | copy-start | bytes 388
  29.1 13.9 %all-to-all-start.1 = ((bf16[32,9,2,128]{3,2,1,0:T(2,128)(2,1)}), bf16[32,9,2,128]{3,2,1,0:T(2,128)(2,1)S(1)}, u32[]{:S(2)}, u32[]{:S(2)}) async-start(bf16[32,9,2,128]{3,2,1,0:T(2,128)(2,1)} %bitcast.9), calls=%async_computation.1 | async-start | bytes 294912 | tf_op jit(solution)/shard_map/all_to_all | solution.py:415
  43.2 3.7 %collective-permute-start.3 = (bf16[8,8,128]{2,1,0:T(8,128)(2,1)S(1)}, bf16[8,8,128]{2,1,0:T(8,128)(2,1)S(1)}, u32[]{:S(2)}, u32[]{:S(2)}) collective-permute-start(bf16[8,8,128]{2,1,0:T(8,128)(2,1)S(1)} %get-tuple-element.26), channel_id=1, source_target_pairs={{0,4},{4,0},{8,12},{12,8},{16,20},{20,16},{24,28},{28,24},{32,36},... | collective-permute-start | bytes 49160 | tf_op jit(solution)/shard_map/ppermute | solution.py:491

commit v5 on v4

--- a/solution.py
+++ b/solution.py
@@ -42,8 +42,8 @@
     upper = onehot(iota((blocks, blocks), 0) < iota((blocks, blocks), 1))
     rank = dot(onto.astype(BF16), upper)
     slot = (onto > 0.5) & (rank == iota((MOST, blocks), 0).astype(F32))
-    chosen = onehot(slot)
-    return slot, dot(chosen, row1).astype(I32) - 1, dot(chosen, column).astype(I32)
+    places = dot(onehot(slot), jnp.concatenate([row1, column], axis=1)).astype(I32)
+    return slot, places[:, :width] - 1, places[:, width:]
 
 
 def gather_kernel(
@@ -98,7 +98,7 @@
                 k = component(r)
                 one = taken[k * rows : (k + 1) * rows, i * width : (i + 1) * width]
                 found.append(jnp.sum(jnp.where(at_row, one, 0.0), axis=0, keepdims=True))
-            picked_ref[s] = jnp.concatenate(found + [target[s : s + 1, :], empty], axis=0).astype(BF16)
+            picked_ref[s] = jnp.concatenate(found + [target[s : s + 1, :], empty], axis=0)
 
 
 def component(row):
@@ -116,14 +116,14 @@
     core = lax.axis_index("tile") & 1
     rows, width = payload_ref.shape
     picked = jnp.concatenate([picked_ref[...].reshape(MOST * 8, width), twin_ref[...].reshape(MOST * 8, width)], axis=0)
-    targets = jnp.concatenate([ref[s, 6:7, :].astype(F32) for ref in (picked_ref, twin_ref) for s in range(MOST)], axis=0)
+    targets = jnp.concatenate([ref[s, 6:7, :] for ref in (picked_ref, twin_ref) for s in range(MOST)], axis=0)
     targets = targets.astype(I32) - 1
     target_ref[...] = targets
     lane = iota((2 * MOST, width), 1)
     code = payload_rows(targets, lane & 7, tiles, core)
     code = jnp.sum(jnp.where((lane >> 3) == iota((2 * MOST, width), 0), code, 0), axis=0, keepdims=True)
     place = onehot(iota((rows, width), 0) == code)
-    payload_ref[...] = dot(place, picked).astype(BF16)
+    payload_ref[...] = dot(place, picked.astype(BF16)).astype(BF16)
 
 
 def pile_kernel(arrived_ref, imag_ref, more_ref, block_hbm, chip_ref, order_ref, payload_ref, real_ref, semaphores):
@@ -166,14 +166,14 @@
     targets = target_ref[:, 0:1].reshape(count, 1, 1)
     code = payload_rows(targets, iota((count, 8, 1), 1), tiles, core)
     take = onehot(iota(shape, 2) == code).reshape(count * 8, slab)
-    chosen = dot(take, landed_ref[...]).astype(BF16).reshape(2, MOST, 8, width)
+    chosen = dot(take, landed_ref[...]).reshape(2, MOST, 8, width)
     own_ref[...] = chosen[0]
     twin_ref[...] = chosen[1]
 
 
 def scatter_kernel(soil_ref, own_ref, twin_ref, at_row_ref, at_column_ref, result_hbm, result, semaphores):
     components, rows, columns = soil_ref.shape
-    pieces = [own_ref[s].astype(F32) + twin_ref[s].astype(F32) for s in range(MOST)]
+    pieces = [own_ref[s] + twin_ref[s] for s in range(MOST)]
     pieces = jnp.concatenate(pieces, axis=1)
     at_row = at_row_ref[...]
     half = components // 2
@@ -417,7 +417,7 @@
     picked = call(
         functools.partial(gather_kernel, tiles),
         "gather",
-        shape((MOST, 8, width), BF16),
+        shape((MOST, 8, width), F32),
         [hbm] * 3,
         [
             pltpu.VMEM((6, rows, nz), F32),
@@ -484,7 +484,7 @@
         flops=10**11,
         moved=10**7,
     )(returning, *map(in_hbm, (field, cell_scale, material_id, near, far, nodes)), stiff_table, mass_table)
-    slots = shape((MOST, 8, width), BF16)
+    slots = shape((MOST, 8, width), F32)
     own, twin = call(functools.partial(choose_kernel, tiles), "choose", (slots, slots), [vmem] * 2 + [anywhere])(
         landed.reshape(slab), targets, soil
     )

time: 48.5 us -> 48.6 us (level)
  no operation moved by 1% of the time
where the time goes in v5:
time: 48.6 us; the launch traced here: 48.3 us
  starting transfers between devices  22.3 us (46%)
  Pallas kernels  13.7 us (28%)
  waiting for transfers between devices  12.2 us (25%)
    all_to_all x2, starting transfers between devices, exchange(): lax.all_to_all(payload.reshape(cut), 'tile', 0, 0, axis_index_groups=grou...  13.9 us
    all_to_all x2, waiting for transfers between devices, exchange(): lax.all_to_all(payload.reshape(cut), 'tile', 0, 0, axis_index_groups=grou...  10.5 us
    pallas_call x1, Pallas kernels, per_device(): call(functools.partial(soil_kernel, tiles), 'soil', (shape(field.shape, F...  3.41 us
    ppermute x1, starting transfers between devices, per_device(): lax.ppermute(picked, 'tile', pair)  3.33 us
    pallas_call x1, Pallas kernels, per_device(): call(pile_kernel, 'pile', shape(slab, BF16), [vmem, vmem, vmem, hbm, vmem...  3.14 us
    pallas_call x1, Pallas kernels, per_device(): pl.pallas_call(ahead_kernel, out_shape=(shape(size, F32), shape(size, F32...  2.85 us
    ppermute x1, starting transfers between devices, per_device(): twin = lax.ppermute(twin, 'tile', pair)  2.83 us
    pallas_call x1, Pallas kernels, per_device(): call(functools.partial(gather_kernel, tiles), 'gather', shape((MOST, 8, w...  1.84 us
  transfers between devices with their start and end apart: 6, of which 4 were waited for; matrix products, arithmetic and copies ran while one was open for 0% of the time, Pallas kernels for 19%

profile of v5, /device:TPU:1, one launch (start us, length us, event | category | flops | bytes accessed | tf_op | source)
XLA Modules:
  0.0 48.3 jit_solution(15943482537290476941)
XLA Ops:
  0.0 1.8 %gather.1.picked_ref = f32[8,8,128]{2,1,0:T(8,128)S(1)} custom-call(f32[6,96,256]{2,1,0:T(8,128)} %bitcast.16, s32[192,128]{1,0:T(8,128)} %bitcast.19, s32[1,64]{1,0:T(1,128)} %bitcast.22), custom_call_target="tpu_custom_call" | custom-call | flops 100000000 | bytes 1000000 | tf_op jit(solution)/shard_map/gather/pallas_call | solution.py:417
  1.8 3.3 %collective-permute-start = (f32[8,8,128]{2,1,0:T(8,128)S(1)}, f32[8,8,128]{2,1,0:T(8,128)S(1)}, u32[]{:S(2)}, u32[]{:S(2)}) collective-permute-start(f32[8,8,128]{2,1,0:T(8,128)S(1)} %gather.1.picked_ref), channel_id=1, source_target_pairs={{0,4},{4,0},{8,12},{12,8},{16,20},{20,16},{24,28},{28,24},{32,36},... | collective-permute-start | bytes 98312 | tf_op jit(solution)/shard_map/ppermute | solution.py:434
  5.2 0.9 %collective-permute-done.twin_ref = f32[8,8,128]{2,1,0:T(8,128)S(1)} collective-permute-done((f32[8,8,128]{2,1,0:T(8,128)S(1)}, f32[8,8,128]{2,1,0:T(8,128)S(1)}, u32[]{:S(2)}, u32[]{:S(2)}) %collective-permute-start) | collective-permute-done | bytes 32800 | tf_op jit(solution)/shard_map/ppermute | solution.py:434
  6.0 0.9 %place.1 = (bf16[576,128]{1,0:T(8,128)(2,1)}, s32[16,128]{1,0:T(8,128)S(1)}) custom-call(f32[8,8,128]{2,1,0:T(8,128)S(1)} %gather.1.picked_ref, f32[8,8,128]{2,1,0:T(8,128)S(1)} %collective-permute-done.twin_ref), custom_call_target="tpu_custom_call" | custom-call | flops 100000000 | bytes 1000000 | tf_op jit(solution)/shard_map/place/pallas_call | solution.py:429
  6.9 9.5 %all-to-all-start = ((bf16[32,9,2,128]{3,2,1,0:T(2,128)(2,1)}), bf16[32,9,2,128]{3,2,1,0:T(2,128)(2,1)S(1)}, u32[]{:S(2)}, u32[]{:S(2)}) async-start(bf16[32,9,2,128]{3,2,1,0:T(2,128)(2,1)} %bitcast.4), calls=%async_computation | async-start | bytes 294912 | tf_op jit(solution)/shard_map/all_to_all | solution.py:415
  16.4 2.9 %ahead.1 = (f32[8,48,256]{2,1,0:T(8,128)}, f32[8,48,256]{2,1,0:T(8,128)}, bf16[1152,1152]{1,0:T(8,128)(2,1)S(1)}, bf16[256,1152]{1,0:T(8,128)(2,1)S(1)}, s32[8,128]{1,0:T(8,128)S(1)}) custom-call(bf16[576,128]{1,0:T(8,128)(2,1)} %get-tuple-element.17.order_ref, f32[6,2,48,256]{3,2,1,0:T(8,128)} %bitcast.17, f32[2,48,256]{2,1,0:T(8,128)} %scale_hbm.3, ...), custom_call_target="tpu_custom_call" | custom-call | flops 100000000 | bytes 1000000 | tf_op jit(solution)/shard_map/ahead/pallas_call | solution.py:441
  19.2 0.7 %collective-permute-start.1 = (f32[8,48,256]{2,1,0:T(8,128)}, f32[8,48,256]{2,1,0:T(8,128)}, u32[]{:S(2)}, u32[]{:S(2)}) collective-permute-start(f32[8,48,256]{2,1,0:T(8,128)} %get-tuple-element.22), channel_id=1, source_target_pairs={{0,4},{4,0},{8,12},{12,8},{16,20},{20,16},{24,28},{28,24},{32,36},... | collective-permute-start | bytes 1179656 | tf_op jit(solution)/shard_map/ppermute | solution.py:458
  20.0 1.5 %collective-permute-start.2 = (f32[8,48,256]{2,1,0:T(8,128)}, f32[8,48,256]{2,1,0:T(8,128)}, u32[]{:S(2)}, u32[]{:S(2)}) collective-permute-start(f32[8,48,256]{2,1,0:T(8,128)} %get-tuple-element.21.order_ref), channel_id=1, source_target_pairs={{4,8},{12,16},{20,24},{28,32},{36,40},{44,48},{52,56},{60,64},{68,... | collective-permute-start | bytes 1179656 | tf_op jit(solution)/shard_map/ppermute | solution.py:460
  21.5 0.0 copy-start
  21.5 0.0 copy-start.1
  21.5 4.5 %all-to-all-done.arrived_ref = bf16[32,9,2,128]{3,2,1,0:T(2,128)(2,1)S(1)} async-done(((bf16[32,9,2,128]{3,2,1,0:T(2,128)(2,1)}), bf16[32,9,2,128]{3,2,1,0:T(2,128)(2,1)S(1)}, u32[]{:S(2)}, u32[]{:S(2)}) %all-to-all-start) | async-done | bytes 147488 | tf_op jit(solution)/shard_map/all_to_all | solution.py:415
  26.0 3.1 %pile.1.order_ref = bf16[576,128]{1,0:T(8,128)(2,1)} custom-call(bf16[32,9,2,128]{3,2,1,0:T(2,128)(2,1)S(1)} %all-to-all-done.arrived_ref, bf16[1152,1152]{1,0:T(8,128)(2,1)S(1)} %get-tuple-element.18.imag_ref, bf16[256,1152]{1,0:T(8,128)(2,1)S(1)} %get-tuple-element.19.more_ref, bf16[2,1152,1152]{2,1,0:T(8,128)(2,1)} %bitcast.15, ...), custom_call_target="tpu_custom_call" | custom-call | flops 100000000 | bytes 1000000 | tf_op jit(solution)/shard_map/pile/pallas_call | solution.py:462
  29.1 4.4 %all-to-all-start.1 = ((bf16[32,9,2,128]{3,2,1,0:T(2,128)(2,1)}), bf16[32,9,2,128]{3,2,1,0:T(2,128)(2,1)S(1)}, u32[]{:S(2)}, u32[]{:S(2)}) async-start(bf16[32,9,2,128]{3,2,1,0:T(2,128)(2,1)} %bitcast.9), calls=%async_computation.1 | async-start | bytes 294912 | tf_op jit(solution)/shard_map/all_to_all | solution.py:415
  33.5 0.0 collective-permute-done.1.near_hbm
  33.5 0.0 collective-permute-done.2.far_hbm
  33.5 0.0 copy-done
  33.5 0.0 copy-done.1
  33.6 3.4 %soil.1 = (f32[6,2,48,256]{3,2,1,0:T(8,128)S(1)}, bf16[96,1024]{1,0:T(8,128)(2,1)S(1)}, bf16[256,1024]{1,0:T(8,128)(2,1)S(1)}) custom-call(bf16[576,128]{1,0:T(8,128)(2,1)} %pile.1.order_ref, f32[6,2,48,256]{3,2,1,0:T(8,128)} %bitcast.18, f32[2,48,256]{2,1,0:T(8,128)} %scale_hbm.3, s32[2,48,256]{2,1,0:T(8,128)} %kind_hbm.3, ...), custom_call_target="tpu_custom_call" | custom-call | flops 99999997952 | bytes 10000000 | tf_op jit(solution)/shard_map/soil/pallas_call | solution.py:470
  37.0 6.0 %all-to-all-done.1 = bf16[32,9,2,128]{3,2,1,0:T(2,128)(2,1)S(1)} async-done(((bf16[32,9,2,128]{3,2,1,0:T(2,128)(2,1)}), bf16[32,9,2,128]{3,2,1,0:T(2,128)(2,1)S(1)}, u32[]{:S(2)}, u32[]{:S(2)}) %all-to-all-start.1) | async-done | bytes 147488 | tf_op jit(solution)/shard_map/all_to_all | solution.py:415
  43.0 0.3 choose.1
  43.2 2.8 %collective-permute-start.3 = (f32[8,8,128]{2,1,0:T(8,128)S(1)}, f32[8,8,128]{2,1,0:T(8,128)S(1)}, u32[]{:S(2)}, u32[]{:S(2)}) collective-permute-start(f32[8,8,128]{2,1,0:T(8,128)S(1)} %get-tuple-element.26), channel_id=1, source_target_pairs={{0,4},{4,0},{8,12},{12,8},{16,20},{20,16},{24,28},{28,24},{32,36},... | collective-permute-start | bytes 98312 | tf_op jit(solution)/shard_map/ppermute | solution.py:491
  46.1 0.9 %collective-permute-done.3.twin_ref = f32[8,8,128]{2,1,0:T(8,128)S(1)} collective-permute-done((f32[8,8,128]{2,1,0:T(8,128)S(1)}, f32[8,8,128]{2,1,0:T(8,128)S(1)}, u32[]{:S(2)}, u32[]{:S(2)}) %collective-permute-start.3) | collective-permute-done | bytes 32800 | tf_op jit(solution)/shard_map/ppermute | solution.py:491
  46.9 1.3 %scatter.1 = f32[6,96,256]{2,1,0:T(8,128)} custom-call(f32[6,96,256]{2,1,0:T(8,128)S(1)} %bitcast.12, f32[8,8,128]{2,1,0:T(8,128)S(1)} %get-tuple-element.25.own_ref, f32[8,8,128]{2,1,0:T(8,128)S(1)} %collective-permute-done.3.twin_ref, bf16[96,1024]{1,0:T(8,128)(2,1)S(1)} %get-tuple-element.27.at_row_ref, bf16[256,1024]{1,0:T(8,128)(2,1)S(1)} %get-tuple-element.28.at_column_ref), custom_call_target="tpu_custom_call" | custom-call | flops 100000000 | bytes 1000000 | tf_op jit(solution)/shard_map/scatter/pallas_call | solution.py:493
  (1 shorter events, 0.0 us)
Async XLA Ops:
  1.8 4.2 %collective-permute-start = (f32[8,8,128]{2,1,0:T(8,128)S(1)}, f32[8,8,128]{2,1,0:T(8,128)S(1)}, u32[]{:S(2)}, u32[]{:S(2)}) collective-permute-start(f32[8,8,128]{2,1,0:T(8,128)S(1)} %gather.1.picked_ref), channel_id=1, source_target_pairs={{0,4},{4,0},{8,12},{12,8},{16,20},{20,16},{24,28},{28,24},{32,36},... | collective-permute-start | bytes 98312 | tf_op jit(solution)/shard_map/ppermute | solution.py:434
  6.9 19.1 %all-to-all-start = ((bf16[32,9,2,128]{3,2,1,0:T(2,128)(2,1)}), bf16[32,9,2,128]{3,2,1,0:T(2,128)(2,1)S(1)}, u32[]{:S(2)}, u32[]{:S(2)}) async-start(bf16[32,9,2,128]{3,2,1,0:T(2,128)(2,1)} %bitcast.4), calls=%async_computation | async-start | bytes 294912 | tf_op jit(solution)/shard_map/all_to_all | solution.py:415
  19.2 14.3 %collective-permute-start.1 = (f32[8,48,256]{2,1,0:T(8,128)}, f32[8,48,256]{2,1,0:T(8,128)}, u32[]{:S(2)}, u32[]{:S(2)}) collective-permute-start(f32[8,48,256]{2,1,0:T(8,128)} %get-tuple-element.22), channel_id=1, source_target_pairs={{0,4},{4,0},{8,12},{12,8},{16,20},{20,16},{24,28},{28,24},{32,36},... | collective-permute-start | bytes 1179656 | tf_op jit(solution)/shard_map/ppermute | solution.py:458
  20.0 13.6 %collective-permute-start.2 = (f32[8,48,256]{2,1,0:T(8,128)}, f32[8,48,256]{2,1,0:T(8,128)}, u32[]{:S(2)}, u32[]{:S(2)}) collective-permute-start(f32[8,48,256]{2,1,0:T(8,128)} %get-tuple-element.21.order_ref), channel_id=1, source_target_pairs={{4,8},{12,16},{20,24},{28,32},{36,40},{44,48},{52,56},{60,64},{68,... | collective-permute-start | bytes 1179656 | tf_op jit(solution)/shard_map/ppermute | solution.py:460
  21.5 12.1 %copy-start = (f32[2,16]{1,0:T(2,128)S(1)}, f32[2,16]{1,0:T(2,128)}, u32[]{:S(2)}) copy-start(f32[2,16]{1,0:T(2,128)} %stiff_ref.1) | copy-start | bytes 388
  21.5 12.1 %copy-start.1 = (f32[2,16]{1,0:T(2,128)S(1)}, f32[2,16]{1,0:T(2,128)}, u32[]{:S(2)}) copy-start(f32[2,16]{1,0:T(2,128)} %mass_ref.1) | copy-start | bytes 388
  29.1 13.9 %all-to-all-start.1 = ((bf16[32,9,2,128]{3,2,1,0:T(2,128)(2,1)}), bf16[32,9,2,128]{3,2,1,0:T(2,128)(2,1)S(1)}, u32[]{:S(2)}, u32[]{:S(2)}) async-start(bf16[32,9,2,128]{3,2,1,0:T(2,128)(2,1)} %bitcast.9), calls=%async_computation.1 | async-start | bytes 294912 | tf_op jit(solution)/shard_map/all_to_all | solution.py:415
  43.2 3.7 %collective-permute-start.3 = (f32[8,8,128]{2,1,0:T(8,128)S(1)}, f32[8,8,128]{2,1,0:T(8,128)S(1)}, u32[]{:S(2)}, u32[]{:S(2)}) collective-permute-start(f32[8,8,128]{2,1,0:T(8,128)S(1)} %get-tuple-element.26), channel_id=1, source_target_pairs={{0,4},{4,0},{8,12},{12,8},{16,20},{20,16},{24,28},{28,24},{32,36},... | collective-permute-start | bytes 98312 | tf_op jit(solution)/shard_map/ppermute | solution.py:491

commit v6 on v5

--- a/solution.py
+++ b/solution.py
@@ -158,23 +158,14 @@
     payload_ref[...] = dot(place, traction).astype(BF16)
 
 
-def choose_kernel(tiles, landed_ref, target_ref, order_ref, own_ref, twin_ref):
-    core = lax.axis_index("tile") & 1
-    slab, width = landed_ref.shape
-    count = 2 * MOST
-    shape = (count, 8, slab)
-    targets = target_ref[:, 0:1].reshape(count, 1, 1)
-    code = payload_rows(targets, iota((count, 8, 1), 1), tiles, core)
-    take = onehot(iota(shape, 2) == code).reshape(count * 8, slab)
-    chosen = dot(take, landed_ref[...]).reshape(2, MOST, 8, width)
-    own_ref[...] = chosen[0]
-    twin_ref[...] = chosen[1]
-
-
-def scatter_kernel(soil_ref, own_ref, twin_ref, at_row_ref, at_column_ref, result_hbm, result, semaphores):
+def choose_kernel(landed_ref, take_ref, own_ref):
+    own_ref[...] = dot(take_ref[0], landed_ref[...])
+
+
+def scatter_kernel(soil_ref, own_ref, twin_ref, take_ref, at_row_ref, at_column_ref, result_hbm, result, semaphores):
     components, rows, columns = soil_ref.shape
-    pieces = [own_ref[s] + twin_ref[s] for s in range(MOST)]
-    pieces = jnp.concatenate(pieces, axis=1)
+    pieces = own_ref[...] + dot(take_ref[1], twin_ref[...])
+    pieces = jnp.concatenate([pieces[s * 8 : (s + 1) * 8] for s in range(MOST)], axis=1)
     at_row = at_row_ref[...]
     half = components // 2
     copies = []
@@ -282,9 +273,11 @@
     nodes_hbm,
     stiff_ref,
     mass_ref,
+    target_ref,
     soil_ref,
     at_row_ref,
     at_column_ref,
+    take_ref,
     displacement_ref,
     scale_ref,
     kind_ref,
@@ -310,6 +303,10 @@
         lanes = slice(s * width, (s + 1) * width)
         at_row_ref[:, lanes] = onehot(iota((planes * ny, width), 0) == slot_row[s : s + 1, :])
         at_column_ref[:, lanes] = onehot(iota((nz, width), 0) == slot_column[s : s + 1, :])
+    shape3 = (MOST, 8, take_ref.shape[2])
+    for i, core in enumerate((odd, 1 - odd)):
+        code = payload_rows(target_ref[0:MOST, 0:1].reshape(MOST, 1, 1), iota((MOST, 8, 1), 1), tiles, core)
+        take_ref[i] = onehot(iota(shape3, 2) == code).reshape(take_ref.shape[1:])
     for copy in copies[1:]:
         copy.wait()
 
@@ -467,11 +464,11 @@
         [pltpu.VMEM(square, BF16), dma((2,))],
     )(arrived, imag, more, block, chip, token)
     landed = exchange(returning)
-    soil, at_row, at_column = call(
+    soil, at_row, at_column, take = call(
         functools.partial(soil_kernel, tiles),
         "soil",
-        (shape(field.shape, F32), shape((rows, MOST * width), BF16), shape((nz, MOST * width), BF16)),
-        [anywhere] + [hbm] * 6 + [smem] * 2,
+        (shape(field.shape, F32), shape((rows, MOST * width), BF16), shape((nz, MOST * width), BF16), shape((2, MOST * 8, chips * 18), BF16)),
+        [anywhere] + [hbm] * 6 + [smem] * 2 + [vmem],
         [
             pltpu.VMEM(field.shape, F32),
             pltpu.VMEM(cell_scale.shape, F32),
@@ -483,23 +480,21 @@
         ],
         flops=10**11,
         moved=10**7,
-    )(returning, *map(in_hbm, (field, cell_scale, material_id, near, far, nodes)), stiff_table, mass_table)
-    slots = shape((MOST, 8, width), F32)
-    own, twin = call(functools.partial(choose_kernel, tiles), "choose", (slots, slots), [vmem] * 2 + [anywhere])(
-        landed.reshape(slab), targets, soil
-    )
-    twin = lax.ppermute(twin, "tile", pair)
+    )(returning, *map(in_hbm, (field, cell_scale, material_id, near, far, nodes)), stiff_table, mass_table, targets)
+    landed, soil = lax.optimization_barrier((landed.reshape(slab), soil))
+    twin = lax.ppermute(landed, "tile", pair)
+    own = call(choose_kernel, "choose", shape((MOST * 8, width), F32), [vmem] * 2, flops=10**11)(landed, take)
     sums = (6, rows, nz)
     result = pl.pallas_call(
         scatter_kernel,
         out_shape=shape(sums, F32),
-        in_specs=[vmem] * 5,
+        in_specs=[vmem] * 6,
         out_specs=hbm,
         scratch_shapes=[pltpu.VMEM(sums, F32), dma((2,))],
         compiler_params=pltpu.CompilerParams(vmem_limit_bytes=16 * 1024 * 1024),
         cost_estimate=pl.CostEstimate(flops=10**8, bytes_accessed=10**6, transcendentals=0),
         name="scatter",
-    )(soil.reshape(sums), own, twin, at_row, at_column)
+    )(soil.reshape(sums), own, twin, take, at_row, at_column)
     return result.reshape(displacement.shape)
 
 

time: 48.6 us -> 48.5 us (level)
  transfers between devices with their start and end apart: 6 -> 6, of which waited for: 4 -> 4; matrix products, arithmetic and copies ran while one was open for 0% -> 0% of each run, Pallas kernels for 19% -> 20%
where the time goes in v6:
time: 48.5 us; the launch traced here: 48.2 us
  starting transfers between devices  22.2 us (46%)
  Pallas kernels  13.7 us (28%)
  waiting for transfers between devices  12.2 us (25%)
    all_to_all x2, starting transfers between devices, exchange(): lax.all_to_all(payload.reshape(cut), 'tile', 0, 0, axis_index_groups=grou...  13.9 us
    all_to_all x2, waiting for transfers between devices, exchange(): lax.all_to_all(payload.reshape(cut), 'tile', 0, 0, axis_index_groups=grou...  10.5 us
    pallas_call x1, Pallas kernels, per_device(): call(functools.partial(soil_kernel, tiles), 'soil', (shape(field.shape, F...  3.42 us
    ppermute x1, starting transfers between devices, per_device(): lax.ppermute(picked, 'tile', pair)  3.33 us
    pallas_call x1, Pallas kernels, per_device(): call(pile_kernel, 'pile', shape(slab, BF16), [vmem, vmem, vmem, hbm, vmem...  3.14 us
    pallas_call x1, Pallas kernels, per_device(): pl.pallas_call(ahead_kernel, out_shape=(shape(size, F32), shape(size, F32...  2.85 us
    ppermute x1, starting transfers between devices, per_device(): twin = lax.ppermute(landed, 'tile', pair)  2.74 us
    pallas_call x1, Pallas kernels, per_device(): call(functools.partial(gather_kernel, tiles), 'gather', shape((MOST, 8, w...  1.84 us
  transfers between devices with their start and end apart: 6, of which 4 were waited for; matrix products, arithmetic and copies ran while one was open for 0% of the time, Pallas kernels for 20%

profile of v6, /device:TPU:1, one launch (start us, length us, event | category | flops | bytes accessed | tf_op | source)
XLA Modules:
  0.0 48.2 jit_solution(16648113155684146700)
XLA Ops:
  0.0 1.8 %gather.1.picked_ref = f32[8,8,128]{2,1,0:T(8,128)S(1)} custom-call(f32[6,96,256]{2,1,0:T(8,128)} %bitcast.17, s32[192,128]{1,0:T(8,128)} %bitcast.20, s32[1,64]{1,0:T(1,128)} %bitcast.23), custom_call_target="tpu_custom_call" | custom-call | flops 100000000 | bytes 1000000 | tf_op jit(solution)/shard_map/gather/pallas_call | solution.py:414
  1.8 3.3 %collective-permute-start = (f32[8,8,128]{2,1,0:T(8,128)S(1)}, f32[8,8,128]{2,1,0:T(8,128)S(1)}, u32[]{:S(2)}, u32[]{:S(2)}) collective-permute-start(f32[8,8,128]{2,1,0:T(8,128)S(1)} %gather.1.picked_ref), channel_id=1, source_target_pairs={{0,4},{4,0},{8,12},{12,8},{16,20},{20,16},{24,28},{28,24},{32,36},... | collective-permute-start | bytes 98312 | tf_op jit(solution)/shard_map/ppermute | solution.py:431
  5.2 0.9 %collective-permute-done.twin_ref = f32[8,8,128]{2,1,0:T(8,128)S(1)} collective-permute-done((f32[8,8,128]{2,1,0:T(8,128)S(1)}, f32[8,8,128]{2,1,0:T(8,128)S(1)}, u32[]{:S(2)}, u32[]{:S(2)}) %collective-permute-start) | collective-permute-done | bytes 32800 | tf_op jit(solution)/shard_map/ppermute | solution.py:431
  6.0 0.9 %place.1 = (bf16[576,128]{1,0:T(8,128)(2,1)}, s32[16,128]{1,0:T(8,128)S(1)}) custom-call(f32[8,8,128]{2,1,0:T(8,128)S(1)} %gather.1.picked_ref, f32[8,8,128]{2,1,0:T(8,128)S(1)} %collective-permute-done.twin_ref), custom_call_target="tpu_custom_call" | custom-call | flops 100000000 | bytes 1000000 | tf_op jit(solution)/shard_map/place/pallas_call | solution.py:426
  6.9 9.5 %all-to-all-start = ((bf16[32,9,2,128]{3,2,1,0:T(2,128)(2,1)}), bf16[32,9,2,128]{3,2,1,0:T(2,128)(2,1)S(1)}, u32[]{:S(2)}, u32[]{:S(2)}) async-start(bf16[32,9,2,128]{3,2,1,0:T(2,128)(2,1)} %bitcast.4), calls=%async_computation | async-start | bytes 294912 | tf_op jit(solution)/shard_map/all_to_all | solution.py:412
  16.4 2.9 %ahead.1 = (f32[8,48,256]{2,1,0:T(8,128)}, f32[8,48,256]{2,1,0:T(8,128)}, bf16[1152,1152]{1,0:T(8,128)(2,1)S(1)}, bf16[256,1152]{1,0:T(8,128)(2,1)S(1)}, s32[8,128]{1,0:T(8,128)S(1)}) custom-call(bf16[576,128]{1,0:T(8,128)(2,1)} %get-tuple-element.18.order_ref, f32[6,2,48,256]{3,2,1,0:T(8,128)} %bitcast.18, f32[2,48,256]{2,1,0:T(8,128)} %scale_hbm.3, ...), custom_call_target="tpu_custom_call" | custom-call | flops 100000000 | bytes 1000000 | tf_op jit(solution)/shard_map/ahead/pallas_call | solution.py:438
  19.2 0.7 %collective-permute-start.1 = (f32[8,48,256]{2,1,0:T(8,128)}, f32[8,48,256]{2,1,0:T(8,128)}, u32[]{:S(2)}, u32[]{:S(2)}) collective-permute-start(f32[8,48,256]{2,1,0:T(8,128)} %get-tuple-element.23), channel_id=1, source_target_pairs={{0,4},{4,0},{8,12},{12,8},{16,20},{20,16},{24,28},{28,24},{32,36},... | collective-permute-start | bytes 1179656 | tf_op jit(solution)/shard_map/ppermute | solution.py:455
  20.0 1.5 %collective-permute-start.2 = (f32[8,48,256]{2,1,0:T(8,128)}, f32[8,48,256]{2,1,0:T(8,128)}, u32[]{:S(2)}, u32[]{:S(2)}) collective-permute-start(f32[8,48,256]{2,1,0:T(8,128)} %get-tuple-element.22.order_ref), channel_id=1, source_target_pairs={{4,8},{12,16},{20,24},{28,32},{36,40},{44,48},{52,56},{60,64},{68,... | collective-permute-start | bytes 1179656 | tf_op jit(solution)/shard_map/ppermute | solution.py:457
  21.5 0.0 copy-start
  21.5 0.0 copy-start.1
  21.5 4.5 %all-to-all-done.arrived_ref = bf16[32,9,2,128]{3,2,1,0:T(2,128)(2,1)S(1)} async-done(((bf16[32,9,2,128]{3,2,1,0:T(2,128)(2,1)}), bf16[32,9,2,128]{3,2,1,0:T(2,128)(2,1)S(1)}, u32[]{:S(2)}, u32[]{:S(2)}) %all-to-all-start) | async-done | bytes 147488 | tf_op jit(solution)/shard_map/all_to_all | solution.py:412
  26.0 3.1 %pile.1.order_ref = bf16[576,128]{1,0:T(8,128)(2,1)} custom-call(bf16[32,9,2,128]{3,2,1,0:T(2,128)(2,1)S(1)} %all-to-all-done.arrived_ref, bf16[1152,1152]{1,0:T(8,128)(2,1)S(1)} %get-tuple-element.19.imag_ref, bf16[256,1152]{1,0:T(8,128)(2,1)S(1)} %get-tuple-element.20.more_ref, bf16[2,1152,1152]{2,1,0:T(8,128)(2,1)} %bitcast.16, ...), custom_call_target="tpu_custom_call" | custom-call | flops 100000000 | bytes 1000000 | tf_op jit(solution)/shard_map/pile/pallas_call | solution.py:459
  29.1 4.4 %all-to-all-start.1 = ((bf16[32,9,2,128]{3,2,1,0:T(2,128)(2,1)}), bf16[32,9,2,128]{3,2,1,0:T(2,128)(2,1)S(1)}, u32[]{:S(2)}, u32[]{:S(2)}) async-start(bf16[32,9,2,128]{3,2,1,0:T(2,128)(2,1)} %bitcast.8), calls=%async_computation.1 | async-start | bytes 294912 | tf_op jit(solution)/shard_map/all_to_all | solution.py:412
  33.5 0.0 collective-permute-done.1.near_hbm
  33.5 0.0 collective-permute-done.2.far_hbm
  33.5 0.0 copy-done
  33.5 0.0 copy-done.1
  33.6 3.4 %soil.1 = (f32[6,2,48,256]{3,2,1,0:T(8,128)S(1)}, bf16[96,1024]{1,0:T(8,128)(2,1)S(1)}, bf16[256,1024]{1,0:T(8,128)(2,1)S(1)}, bf16[2,64,576]{2,1,0:T(8,128)(2,1)S(1)}) custom-call(bf16[576,128]{1,0:T(8,128)(2,1)} %pile.1.order_ref, f32[6,2,48,256]{3,2,1,0:T(8,128)} %bitcast.19, f32[2,48,256]{2,1,0:T(8,128)} %scale_hbm.3, s32[2,48,256]{2,1,0:T(8,128)} %kind_hbm.3, ...), custom_call_target="tpu_custom_call" | custom-call | flops 99999997952 | bytes 10000000 | tf_op jit(solution)/shard_map/soil/pallas_call | solution.py:467
  37.0 6.0 %all-to-all-done.1 = bf16[32,9,2,128]{3,2,1,0:T(2,128)(2,1)S(1)} async-done(((bf16[32,9,2,128]{3,2,1,0:T(2,128)(2,1)}), bf16[32,9,2,128]{3,2,1,0:T(2,128)(2,1)S(1)}, u32[]{:S(2)}, u32[]{:S(2)}) %all-to-all-start.1) | async-done | bytes 147488 | tf_op jit(solution)/shard_map/all_to_all | solution.py:412
  43.0 2.7 %collective-permute-start.3 = (bf16[576,128]{1,0:T(8,128)(2,1)S(1)}, bf16[576,128]{1,0:T(8,128)(2,1)S(1)}, u32[]{:S(2)}, u32[]{:S(2)}) collective-permute-start(bf16[576,128]{1,0:T(8,128)(2,1)S(1)} %bitcast.13), channel_id=1, source_target_pairs={{0,4},{4,0},{8,12},{12,8},{16,20},{20,16},{24,28},{28,24},{32,36},... | collective-permute-start | bytes 442376 | tf_op jit(solution)/shard_map/ppermute | solution.py:485
  45.7 0.2 choose.1.own_ref
  45.9 0.9 %collective-permute-done.3.twin_ref = bf16[576,128]{1,0:T(8,128)(2,1)S(1)} collective-permute-done((bf16[576,128]{1,0:T(8,128)(2,1)S(1)}, bf16[576,128]{1,0:T(8,128)(2,1)S(1)}, u32[]{:S(2)}, u32[]{:S(2)}) %collective-permute-start.3) | collective-permute-done | bytes 147488 | tf_op jit(solution)/shard_map/ppermute | solution.py:485
  46.7 1.4 %scatter.1 = f32[6,96,256]{2,1,0:T(8,128)} custom-call(f32[6,96,256]{2,1,0:T(8,128)S(1)} %bitcast.12, f32[64,128]{1,0:T(8,128)S(1)} %choose.1.own_ref, bf16[576,128]{1,0:T(8,128)(2,1)S(1)} %collective-permute-done.3.twin_ref, bf16[2,64,576]{2,1,0:T(8,128)(2,1)S(1)} %get-tuple-element.28.take_ref, bf16[96,1024]{1,0:T(8,128)(2,1)S(1)} %get-tuple-element.29.at_row_ref, ...), custom_call_target="tpu_custom_call" | custom-call | flops 100000000 | bytes 1000000 | tf_op jit(solution)/shard_map/scatter/pallas_call | solution.py:488
  (1 shorter events, 0.0 us)
Async XLA Ops:
  1.8 4.2 %collective-permute-start = (f32[8,8,128]{2,1,0:T(8,128)S(1)}, f32[8,8,128]{2,1,0:T(8,128)S(1)}, u32[]{:S(2)}, u32[]{:S(2)}) collective-permute-start(f32[8,8,128]{2,1,0:T(8,128)S(1)} %gather.1.picked_ref), channel_id=1, source_target_pairs={{0,4},{4,0},{8,12},{12,8},{16,20},{20,16},{24,28},{28,24},{32,36},... | collective-permute-start | bytes 98312 | tf_op jit(solution)/shard_map/ppermute | solution.py:431
  6.9 19.1 %all-to-all-start = ((bf16[32,9,2,128]{3,2,1,0:T(2,128)(2,1)}), bf16[32,9,2,128]{3,2,1,0:T(2,128)(2,1)S(1)}, u32[]{:S(2)}, u32[]{:S(2)}) async-start(bf16[32,9,2,128]{3,2,1,0:T(2,128)(2,1)} %bitcast.4), calls=%async_computation | async-start | bytes 294912 | tf_op jit(solution)/shard_map/all_to_all | solution.py:412
  19.2 14.3 %collective-permute-start.1 = (f32[8,48,256]{2,1,0:T(8,128)}, f32[8,48,256]{2,1,0:T(8,128)}, u32[]{:S(2)}, u32[]{:S(2)}) collective-permute-start(f32[8,48,256]{2,1,0:T(8,128)} %get-tuple-element.23), channel_id=1, source_target_pairs={{0,4},{4,0},{8,12},{12,8},{16,20},{20,16},{24,28},{28,24},{32,36},... | collective-permute-start | bytes 1179656 | tf_op jit(solution)/shard_map/ppermute | solution.py:455
  20.0 13.6 %collective-permute-start.2 = (f32[8,48,256]{2,1,0:T(8,128)}, f32[8,48,256]{2,1,0:T(8,128)}, u32[]{:S(2)}, u32[]{:S(2)}) collective-permute-start(f32[8,48,256]{2,1,0:T(8,128)} %get-tuple-element.22.order_ref), channel_id=1, source_target_pairs={{4,8},{12,16},{20,24},{28,32},{36,40},{44,48},{52,56},{60,64},{68,... | collective-permute-start | bytes 1179656 | tf_op jit(solution)/shard_map/ppermute | solution.py:457
  21.5 12.1 %copy-start = (f32[2,16]{1,0:T(2,128)S(1)}, f32[2,16]{1,0:T(2,128)}, u32[]{:S(2)}) copy-start(f32[2,16]{1,0:T(2,128)} %stiff_ref.1) | copy-start | bytes 388
  21.5 12.1 %copy-start.1 = (f32[2,16]{1,0:T(2,128)S(1)}, f32[2,16]{1,0:T(2,128)}, u32[]{:S(2)}) copy-start(f32[2,16]{1,0:T(2,128)} %mass_ref.1) | copy-start | bytes 388
  29.1 13.9 %all-to-all-start.1 = ((bf16[32,9,2,128]{3,2,1,0:T(2,128)(2,1)}), bf16[32,9,2,128]{3,2,1,0:T(2,128)(2,1)S(1)}, u32[]{:S(2)}, u32[]{:S(2)}) async-start(bf16[32,9,2,128]{3,2,1,0:T(2,128)(2,1)} %bitcast.8), calls=%async_computation.1 | async-start | bytes 294912 | tf_op jit(solution)/shard_map/all_to_all | solution.py:412
  43.0 3.7 %collective-permute-start.3 = (bf16[576,128]{1,0:T(8,128)(2,1)S(1)}, bf16[576,128]{1,0:T(8,128)(2,1)S(1)}, u32[]{:S(2)}, u32[]{:S(2)}) collective-permute-start(bf16[576,128]{1,0:T(8,128)(2,1)S(1)} %bitcast.13), channel_id=1, source_target_pairs={{0,4},{4,0},{8,12},{12,8},{16,20},{20,16},{24,28},{28,24},{32,36},... | collective-permute-start | bytes 442376 | tf_op jit(solution)/shard_map/ppermute | solution.py:485

commit v7 on v6

--- a/solution.py
+++ b/solution.py
@@ -136,7 +136,14 @@
     for i, (start, stop) in enumerate(zip(ends, ends[1:])):
         copies.append(pltpu.make_async_copy(block_hbm.at[0, start:stop], real_ref.at[start:stop], semaphores.at[i]))
         copies[i].start()
-    vector = jnp.sum(arrived_ref[...].astype(F32), axis=0)
+    lane = iota((1, width), 1)
+    block = (lane >> 1) % 3
+    chip = chip_ref[0:1, :]
+    for b in (1, 2):
+        chip = jnp.where(block == b, chip_ref[b : b + 1, :], chip)
+    code = jnp.where(lane < 2 * pieces, chip * (2 * pieces) + lane, -1)
+    place = onehot(iota((rows, width), 0) == code)
+    vector = jnp.sum(arrived_ref[...], axis=0)
     vector = jnp.concatenate([vector[k] for k in range(pieces)], axis=1).astype(BF16)
     by_imag = dot_nt(vector, imag_ref[...])
     by_real = [dot_nt(vector, more_ref[...])]
@@ -148,13 +155,6 @@
     imag = by_real[1:2] + by_imag[0:1]
     traction = [part[:, k * width : (k + 1) * width] for k in range(pieces) for part in (real, imag)]
     traction = jnp.concatenate(traction + [jnp.zeros((width - 2 * pieces, width), F32)], axis=0).astype(BF16)
-    lane = iota((1, width), 1)
-    block = (lane >> 1) % 3
-    chip = chip_ref[0:1, :]
-    for b in (1, 2):
-        chip = jnp.where(block == b, chip_ref[b : b + 1, :], chip)
-    code = jnp.where(lane < 2 * pieces, chip * (2 * pieces) + lane, -1)
-    place = onehot(iota((rows, width), 0) == code)
     payload_ref[...] = dot(place, traction).astype(BF16)
 
 
@@ -169,15 +169,14 @@
     at_row = at_row_ref[...]
     half = components // 2
     copies = []
-    for i in range(2):
+    for i, (start, stop) in enumerate(((0, 4), (4, components))):
         spread = []
-        for k in range(i * half, (i + 1) * half):
-            row = (k % half) * 2 + i
+        for k in range(start, stop):
+            row = (k % half) * 2 + k // half
             spread.append(jnp.broadcast_to(pieces[row : row + 1, :], at_row.shape).astype(BF16) * at_row)
         added = dot_nt(jnp.concatenate(spread, axis=0), at_column_ref[...])
-        part = slice(i * half, (i + 1) * half)
-        result[part] = soil_ref[part] + added.reshape(half, rows, columns)
-        copies.append(pltpu.make_async_copy(result.at[part], result_hbm.at[part], semaphores.at[i]))
+        result[start:stop] = soil_ref[start:stop] + added.reshape(stop - start, rows, columns)
+        copies.append(pltpu.make_async_copy(result.at[start:stop], result_hbm.at[start:stop], semaphores.at[i]))
         copies[i].start()
     for copy in copies:
         copy.wait()

time: 48.5 us -> 48.5 us (level)
  no operation moved by 1% of the time
where the time goes in v7:
time: 48.5 us; the launch traced here: 48.2 us
  starting transfers between devices  22.2 us (46%)
  Pallas kernels  13.7 us (28%)
  waiting for transfers between devices  12.2 us (25%)
    all_to_all x2, starting transfers between devices, exchange(): lax.all_to_all(payload.reshape(cut), 'tile', 0, 0, axis_index_groups=grou...  13.9 us
    all_to_all x2, waiting for transfers between devices, exchange(): lax.all_to_all(payload.reshape(cut), 'tile', 0, 0, axis_index_groups=grou...  10.5 us
    pallas_call x1, Pallas kernels, per_device(): call(functools.partial(soil_kernel, tiles), 'soil', (shape(field.shape, F...  3.42 us
    ppermute x1, starting transfers between devices, per_device(): lax.ppermute(picked, 'tile', pair)  3.33 us
    pallas_call x1, Pallas kernels, per_device(): call(pile_kernel, 'pile', shape(slab, BF16), [vmem, vmem, vmem, hbm, vmem...  3.15 us
    pallas_call x1, Pallas kernels, per_device(): pl.pallas_call(ahead_kernel, out_shape=(shape(size, F32), shape(size, F32...  2.85 us
    ppermute x1, starting transfers between devices, per_device(): twin = lax.ppermute(landed, 'tile', pair)  2.74 us
    pallas_call x1, Pallas kernels, per_device(): call(functools.partial(gather_kernel, tiles), 'gather', shape((MOST, 8, w...  1.84 us
  transfers between devices with their start and end apart: 6, of which 4 were waited for; matrix products, arithmetic and copies ran while one was open for 0% of the time, Pallas kernels for 20%

profile of v7, /device:TPU:1, one launch (start us, length us, event | category | flops | bytes accessed | tf_op | source)
XLA Modules:
  0.0 48.2 jit_solution(14791252359013718926)
XLA Ops:
  0.0 1.8 %gather.1.picked_ref = f32[8,8,128]{2,1,0:T(8,128)S(1)} custom-call(f32[6,96,256]{2,1,0:T(8,128)} %bitcast.17, s32[192,128]{1,0:T(8,128)} %bitcast.20, s32[1,64]{1,0:T(1,128)} %bitcast.23), custom_call_target="tpu_custom_call" | custom-call | flops 100000000 | bytes 1000000 | tf_op jit(solution)/shard_map/gather/pallas_call | solution.py:413
  1.8 3.3 %collective-permute-start = (f32[8,8,128]{2,1,0:T(8,128)S(1)}, f32[8,8,128]{2,1,0:T(8,128)S(1)}, u32[]{:S(2)}, u32[]{:S(2)}) collective-permute-start(f32[8,8,128]{2,1,0:T(8,128)S(1)} %gather.1.picked_ref), channel_id=1, source_target_pairs={{0,4},{4,0},{8,12},{12,8},{16,20},{20,16},{24,28},{28,24},{32,36},... | collective-permute-start | bytes 98312 | tf_op jit(solution)/shard_map/ppermute | solution.py:430
  5.2 0.9 %collective-permute-done.twin_ref = f32[8,8,128]{2,1,0:T(8,128)S(1)} collective-permute-done((f32[8,8,128]{2,1,0:T(8,128)S(1)}, f32[8,8,128]{2,1,0:T(8,128)S(1)}, u32[]{:S(2)}, u32[]{:S(2)}) %collective-permute-start) | collective-permute-done | bytes 32800 | tf_op jit(solution)/shard_map/ppermute | solution.py:430
  6.0 0.9 %place.1 = (bf16[576,128]{1,0:T(8,128)(2,1)}, s32[16,128]{1,0:T(8,128)S(1)}) custom-call(f32[8,8,128]{2,1,0:T(8,128)S(1)} %gather.1.picked_ref, f32[8,8,128]{2,1,0:T(8,128)S(1)} %collective-permute-done.twin_ref), custom_call_target="tpu_custom_call" | custom-call | flops 100000000 | bytes 1000000 | tf_op jit(solution)/shard_map/place/pallas_call | solution.py:425
  6.9 9.5 %all-to-all-start = ((bf16[32,9,2,128]{3,2,1,0:T(2,128)(2,1)}), bf16[32,9,2,128]{3,2,1,0:T(2,128)(2,1)S(1)}, u32[]{:S(2)}, u32[]{:S(2)}) async-start(bf16[32,9,2,128]{3,2,1,0:T(2,128)(2,1)} %bitcast.4), calls=%async_computation | async-start | bytes 294912 | tf_op jit(solution)/shard_map/all_to_all | solution.py:411
  16.4 2.9 %ahead.1 = (f32[8,48,256]{2,1,0:T(8,128)}, f32[8,48,256]{2,1,0:T(8,128)}, bf16[1152,1152]{1,0:T(8,128)(2,1)S(1)}, bf16[256,1152]{1,0:T(8,128)(2,1)S(1)}, s32[8,128]{1,0:T(8,128)S(1)}) custom-call(bf16[576,128]{1,0:T(8,128)(2,1)} %get-tuple-element.18.order_ref, f32[6,2,48,256]{3,2,1,0:T(8,128)} %bitcast.18, f32[2,48,256]{2,1,0:T(8,128)} %scale_hbm.3, ...), custom_call_target="tpu_custom_call" | custom-call | flops 100000000 | bytes 1000000 | tf_op jit(solution)/shard_map/ahead/pallas_call | solution.py:437
  19.2 0.7 %collective-permute-start.1 = (f32[8,48,256]{2,1,0:T(8,128)}, f32[8,48,256]{2,1,0:T(8,128)}, u32[]{:S(2)}, u32[]{:S(2)}) collective-permute-start(f32[8,48,256]{2,1,0:T(8,128)} %get-tuple-element.23), channel_id=1, source_target_pairs={{0,4},{4,0},{8,12},{12,8},{16,20},{20,16},{24,28},{28,24},{32,36},... | collective-permute-start | bytes 1179656 | tf_op jit(solution)/shard_map/ppermute | solution.py:454
  20.0 1.5 %collective-permute-start.2 = (f32[8,48,256]{2,1,0:T(8,128)}, f32[8,48,256]{2,1,0:T(8,128)}, u32[]{:S(2)}, u32[]{:S(2)}) collective-permute-start(f32[8,48,256]{2,1,0:T(8,128)} %get-tuple-element.22.order_ref), channel_id=1, source_target_pairs={{4,8},{12,16},{20,24},{28,32},{36,40},{44,48},{52,56},{60,64},{68,... | collective-permute-start | bytes 1179656 | tf_op jit(solution)/shard_map/ppermute | solution.py:456
  21.5 0.0 copy-start
  21.5 0.0 copy-start.1
  21.5 4.5 %all-to-all-done.arrived_ref = bf16[32,9,2,128]{3,2,1,0:T(2,128)(2,1)S(1)} async-done(((bf16[32,9,2,128]{3,2,1,0:T(2,128)(2,1)}), bf16[32,9,2,128]{3,2,1,0:T(2,128)(2,1)S(1)}, u32[]{:S(2)}, u32[]{:S(2)}) %all-to-all-start) | async-done | bytes 147488 | tf_op jit(solution)/shard_map/all_to_all | solution.py:411
  26.0 3.2 %pile.1.order_ref = bf16[576,128]{1,0:T(8,128)(2,1)} custom-call(bf16[32,9,2,128]{3,2,1,0:T(2,128)(2,1)S(1)} %all-to-all-done.arrived_ref, bf16[1152,1152]{1,0:T(8,128)(2,1)S(1)} %get-tuple-element.19.imag_ref, bf16[256,1152]{1,0:T(8,128)(2,1)S(1)} %get-tuple-element.20.more_ref, bf16[2,1152,1152]{2,1,0:T(8,128)(2,1)} %bitcast.16, ...), custom_call_target="tpu_custom_call" | custom-call | flops 100000000 | bytes 1000000 | tf_op jit(solution)/shard_map/pile/pallas_call | solution.py:458
  29.1 4.4 %all-to-all-start.1 = ((bf16[32,9,2,128]{3,2,1,0:T(2,128)(2,1)}), bf16[32,9,2,128]{3,2,1,0:T(2,128)(2,1)S(1)}, u32[]{:S(2)}, u32[]{:S(2)}) async-start(bf16[32,9,2,128]{3,2,1,0:T(2,128)(2,1)} %bitcast.8), calls=%async_computation.1 | async-start | bytes 294912 | tf_op jit(solution)/shard_map/all_to_all | solution.py:411
  33.5 0.0 collective-permute-done.1.near_hbm
  33.5 0.0 collective-permute-done.2.far_hbm
  33.6 0.0 copy-done
  33.6 0.0 copy-done.1
  33.6 3.4 %soil.1 = (f32[6,2,48,256]{3,2,1,0:T(8,128)S(1)}, bf16[96,1024]{1,0:T(8,128)(2,1)S(1)}, bf16[256,1024]{1,0:T(8,128)(2,1)S(1)}, bf16[2,64,576]{2,1,0:T(8,128)(2,1)S(1)}) custom-call(bf16[576,128]{1,0:T(8,128)(2,1)} %pile.1.order_ref, f32[6,2,48,256]{3,2,1,0:T(8,128)} %bitcast.19, f32[2,48,256]{2,1,0:T(8,128)} %scale_hbm.3, s32[2,48,256]{2,1,0:T(8,128)} %kind_hbm.3, ...), custom_call_target="tpu_custom_call" | custom-call | flops 99999997952 | bytes 10000000 | tf_op jit(solution)/shard_map/soil/pallas_call | solution.py:466
  37.0 6.0 %all-to-all-done.1 = bf16[32,9,2,128]{3,2,1,0:T(2,128)(2,1)S(1)} async-done(((bf16[32,9,2,128]{3,2,1,0:T(2,128)(2,1)}), bf16[32,9,2,128]{3,2,1,0:T(2,128)(2,1)S(1)}, u32[]{:S(2)}, u32[]{:S(2)}) %all-to-all-start.1) | async-done | bytes 147488 | tf_op jit(solution)/shard_map/all_to_all | solution.py:411
  43.0 2.7 %collective-permute-start.3 = (bf16[576,128]{1,0:T(8,128)(2,1)S(1)}, bf16[576,128]{1,0:T(8,128)(2,1)S(1)}, u32[]{:S(2)}, u32[]{:S(2)}) collective-permute-start(bf16[576,128]{1,0:T(8,128)(2,1)S(1)} %bitcast.13), channel_id=1, source_target_pairs={{0,4},{4,0},{8,12},{12,8},{16,20},{20,16},{24,28},{28,24},{32,36},... | collective-permute-start | bytes 442376 | tf_op jit(solution)/shard_map/ppermute | solution.py:484
  45.8 0.2 choose.1.own_ref
  45.9 0.9 %collective-permute-done.3.twin_ref = bf16[576,128]{1,0:T(8,128)(2,1)S(1)} collective-permute-done((bf16[576,128]{1,0:T(8,128)(2,1)S(1)}, bf16[576,128]{1,0:T(8,128)(2,1)S(1)}, u32[]{:S(2)}, u32[]{:S(2)}) %collective-permute-start.3) | collective-permute-done | bytes 147488 | tf_op jit(solution)/shard_map/ppermute | solution.py:484
  46.8 1.5 %scatter.1 = f32[6,96,256]{2,1,0:T(8,128)} custom-call(f32[6,96,256]{2,1,0:T(8,128)S(1)} %bitcast.12, f32[64,128]{1,0:T(8,128)S(1)} %choose.1.own_ref, bf16[576,128]{1,0:T(8,128)(2,1)S(1)} %collective-permute-done.3.twin_ref, bf16[2,64,576]{2,1,0:T(8,128)(2,1)S(1)} %get-tuple-element.28.take_ref, bf16[96,1024]{1,0:T(8,128)(2,1)S(1)} %get-tuple-element.29.at_row_ref, ...), custom_call_target="tpu_custom_call" | custom-call | flops 100000000 | bytes 1000000 | tf_op jit(solution)/shard_map/scatter/pallas_call | solution.py:487
  (1 shorter events, 0.0 us)
Async XLA Ops:
  1.8 4.2 %collective-permute-start = (f32[8,8,128]{2,1,0:T(8,128)S(1)}, f32[8,8,128]{2,1,0:T(8,128)S(1)}, u32[]{:S(2)}, u32[]{:S(2)}) collective-permute-start(f32[8,8,128]{2,1,0:T(8,128)S(1)} %gather.1.picked_ref), channel_id=1, source_target_pairs={{0,4},{4,0},{8,12},{12,8},{16,20},{20,16},{24,28},{28,24},{32,36},... | collective-permute-start | bytes 98312 | tf_op jit(solution)/shard_map/ppermute | solution.py:430
  6.9 19.1 %all-to-all-start = ((bf16[32,9,2,128]{3,2,1,0:T(2,128)(2,1)}), bf16[32,9,2,128]{3,2,1,0:T(2,128)(2,1)S(1)}, u32[]{:S(2)}, u32[]{:S(2)}) async-start(bf16[32,9,2,128]{3,2,1,0:T(2,128)(2,1)} %bitcast.4), calls=%async_computation | async-start | bytes 294912 | tf_op jit(solution)/shard_map/all_to_all | solution.py:411
  19.2 14.3 %collective-permute-start.1 = (f32[8,48,256]{2,1,0:T(8,128)}, f32[8,48,256]{2,1,0:T(8,128)}, u32[]{:S(2)}, u32[]{:S(2)}) collective-permute-start(f32[8,48,256]{2,1,0:T(8,128)} %get-tuple-element.23), channel_id=1, source_target_pairs={{0,4},{4,0},{8,12},{12,8},{16,20},{20,16},{24,28},{28,24},{32,36},... | collective-permute-start | bytes 1179656 | tf_op jit(solution)/shard_map/ppermute | solution.py:454
  20.0 13.6 %collective-permute-start.2 = (f32[8,48,256]{2,1,0:T(8,128)}, f32[8,48,256]{2,1,0:T(8,128)}, u32[]{:S(2)}, u32[]{:S(2)}) collective-permute-start(f32[8,48,256]{2,1,0:T(8,128)} %get-tuple-element.22.order_ref), channel_id=1, source_target_pairs={{4,8},{12,16},{20,24},{28,32},{36,40},{44,48},{52,56},{60,64},{68,... | collective-permute-start | bytes 1179656 | tf_op jit(solution)/shard_map/ppermute | solution.py:456
  21.5 12.1 %copy-start = (f32[2,16]{1,0:T(2,128)S(1)}, f32[2,16]{1,0:T(2,128)}, u32[]{:S(2)}) copy-start(f32[2,16]{1,0:T(2,128)} %stiff_ref.1) | copy-start | bytes 388
  21.5 12.1 %copy-start.1 = (f32[2,16]{1,0:T(2,128)S(1)}, f32[2,16]{1,0:T(2,128)}, u32[]{:S(2)}) copy-start(f32[2,16]{1,0:T(2,128)} %mass_ref.1) | copy-start | bytes 388
  29.1 13.9 %all-to-all-start.1 = ((bf16[32,9,2,128]{3,2,1,0:T(2,128)(2,1)}), bf16[32,9,2,128]{3,2,1,0:T(2,128)(2,1)S(1)}, u32[]{:S(2)}, u32[]{:S(2)}) async-start(bf16[32,9,2,128]{3,2,1,0:T(2,128)(2,1)} %bitcast.8), calls=%async_computation.1 | async-start | bytes 294912 | tf_op jit(solution)/shard_map/all_to_all | solution.py:411
  43.0 3.7 %collective-permute-start.3 = (bf16[576,128]{1,0:T(8,128)(2,1)S(1)}, bf16[576,128]{1,0:T(8,128)(2,1)S(1)}, u32[]{:S(2)}, u32[]{:S(2)}) collective-permute-start(bf16[576,128]{1,0:T(8,128)(2,1)S(1)} %bitcast.13), channel_id=1, source_target_pairs={{0,4},{4,0},{8,12},{12,8},{16,20},{20,16},{24,28},{28,24},{32,36},... | collective-permute-start | bytes 442376 | tf_op jit(solution)/shard_map/ppermute | solution.py:484
